TPU v7x, 128 devices: a whole 4x4x4 slice. The times are simulated.
128 devices in a mesh: dp: 2 (over y_lo), ctx: 32 (over z, x, core), branch: 2 (over y_hi).
Axes of the slice: x: 4, y: 4 (y_hi: 2, y_lo: 2; y = y_hi * 2 + y_lo), z: 4, core: 2. Of those that a mesh axis runs over, the one named last changes fastest.
Arguments:
- prompt_query_projection: bfloat16 [2, 4096, 2560], P('dp', ('ctx', 'branch')), may hold values from -16 to 16
- prompt_key_projection: bfloat16 [2, 4096, 512], P('dp', ('ctx', 'branch')), may hold values from -16 to 16
- prompt_value_projection: bfloat16 [2, 4096, 512], P('dp', ('ctx', 'branch')), may hold values from -6 to 6
- prompt_output_gradient: bfloat16 [2, 4096, 2560], P('dp', ('ctx', 'branch')), may hold values from -6 to 6
- response_query: bfloat16 [2, 2, 2048, 2560], P('dp', 'branch', 'ctx'), may hold values from -16 to 16
- response_key_projection: bfloat16 [2, 2, 2048, 512], P('dp', 'branch', 'ctx'), may hold values from -16 to 16
- response_value_projection: bfloat16 [2, 2, 2048, 512], P('dp', 'branch', 'ctx'), may hold values from -6 to 6
- response_output_gradient: bfloat16 [2, 2, 2048, 2560], P('dp', 'branch', 'ctx'), may hold values from -6 to 6
- query_projection_bias: bfloat16 [2560], replicated, may hold values from -3 to 3
- key_projection_bias: bfloat16 [512], replicated, may hold values from -3 to 3
- value_projection_bias: bfloat16 [512], replicated, may hold values from -3 to 3
- segments: int32 [2, 4096], P('dp', ('ctx', 'branch')), may hold values from 0 to 3, never falling along the last dimension, each value on 1 to 2048 neighbouring positions
- lengths: int32 [2, 2], P('dp', 'branch'), may hold values from 512 to 2048, as said below
Outputs:
- prompt_output: bfloat16 [2, 4096, 2560], P('dp', ('ctx', 'branch'))
- response_output: bfloat16 [2, 2, 2048, 2560], P('dp', 'branch', 'ctx')
- prompt_query_grad: bfloat16 [2, 4096, 2560], P('dp', ('ctx', 'branch'))
- prompt_key_grad: bfloat16 [2, 4096, 512], P('dp', ('ctx', 'branch'))
- prompt_value_grad: bfloat16 [2, 4096, 512], P('dp', ('ctx', 'branch'))
- response_query_grad: bfloat16 [2, 2, 2048, 2560], P('dp', 'branch', 'ctx')
- response_key_grad: bfloat16 [2, 2, 2048, 512], P('dp', 'branch', 'ctx')
- response_value_grad: bfloat16 [2, 2, 2048, 512], P('dp', 'branch', 'ctx')
- query_bias_grad: float32 [2560], replicated
- key_bias_grad: float32 [512], replicated
- value_bias_grad: float32 [512], replicated
Inputs may be any that keep to these rules, and one draw needn't show every extreme that they name: `segments`: segment ids never fall along the prompt; each segment has at most 2048 positions, and one has exactly that many. In each example one of the two responses has exactly 2048 tokens; a response's tokens are its first lengths positions.
All inputs are finite; a program needn't handle non-finite values.
Results may differ from a plain program's by a relative error of at most 0.025.
The roundings to bfloat16 on the way count: a program that leaves them out, or rounds other values in their place, can miss the bound.
Values may be sent and summed in bfloat16 or wider, within the bound.
No kernel may reach another device: no remote copies, remote signals or barrier semaphores. Data moves between devices by JAX's collectives and lax.ppermute only.
A program may use at most 128 MiB of HBM per device.

v0:
```python
import jax
import jax.numpy as jnp
from jax import lax
from jax.sharding import PartitionSpec as P

QUERY_HEADS = 20
KEY_VALUE_HEADS = 4
HEAD_SIZE = 128
SEGS = 4


rope_base = 1000000.0
score_masked = -1e30


def rope_tables(positions, head_dim):
    half_dim = head_dim // 2
    frequency = rope_base ** (-(jnp.arange(half_dim, dtype=jnp.float32) * 2.0 / head_dim))
    angles = positions.astype(jnp.float32)[:, None] * frequency[None, :]
    angles = jnp.concatenate([angles, angles], axis=1)
    return (jnp.cos(angles), jnp.sin(angles))


def rotate(values, positions):
    cosine_table, sine_table = rope_tables(positions, values.shape[-1])
    half_dim = values.shape[-1] // 2
    turned = jnp.concatenate([-values[..., half_dim:], values[..., :half_dim]], axis=-1)
    return values * cosine_table[:, None, :] + turned * sine_table[:, None, :]


def inverse_rotation(gradients, positions):
    cosine_table, sine_table = rope_tables(positions, gradients.shape[-1])
    half_dim = gradients.shape[-1] // 2
    scaled = gradients * sine_table[:, None, :]
    turned = jnp.concatenate([scaled[..., half_dim:], -scaled[..., :half_dim]], axis=-1)
    return gradients * cosine_table[:, None, :] + turned


def prepare_inputs(row_values, bias_row, head_count, positions):
    biased = row_values.astype(jnp.float32) + bias_row.astype(jnp.float32)[None, :]
    biased = biased.reshape(row_values.shape[0], head_count, -1)
    return rotate(biased, positions).astype(jnp.bfloat16)


def score_block(query_rows_all, key_block, score_scale):
    return (
        jnp.einsum("ngmd,kgd->gmnk", query_rows_all, key_block, preferred_element_type=jnp.float32)
        * score_scale
    )


def stat_pass(query_rows_all, keys, visible_fn, block_rows, state, score_scale):
    blocks = keys.shape[0] // block_rows

    def stat_advance(block_index, carried):
        highest, running_total = carried
        key_start = block_index * block_rows
        key_block = lax.dynamic_slice_in_dim(keys, key_start, block_rows, 0)
        visible = visible_fn(key_start, block_rows)[None, None]
        scores = jnp.where(
            visible, score_block(query_rows_all, key_block, score_scale), score_masked
        )
        raised = jnp.maximum(highest, jnp.max(scores, axis=-1))
        block_total = jnp.sum(jnp.where(visible, jnp.exp(scores - raised[..., None]), 0.0), axis=-1)
        return (raised, running_total * jnp.exp(highest - raised) + block_total)

    return lax.fori_loop(0, blocks, stat_advance, state)


def output_pass(
    query_rows_all, keys, values, log_total, visible_fn, block_rows, output_total, score_scale
):
    blocks = keys.shape[0] // block_rows

    def output_advance(block_index, running_sum):
        key_start = block_index * block_rows
        key_block = lax.dynamic_slice_in_dim(keys, key_start, block_rows, 0)
        value_block = lax.dynamic_slice_in_dim(values, key_start, block_rows, 0)
        visible = visible_fn(key_start, block_rows)[None, None]
        scores = score_block(query_rows_all, key_block, score_scale)
        weights = jnp.where(visible, jnp.exp(scores - log_total[..., None]), 0.0).astype(
            jnp.bfloat16
        )
        return running_sum + jnp.einsum(
            "gmnk,kgd->ngmd", weights, value_block, preferred_element_type=jnp.float32
        )

    return lax.fori_loop(0, blocks, output_advance, output_total)


def block_grads(
    query_rows_all,
    incoming_gradient,
    log_total,
    row_dot,
    key_block,
    value_block,
    visible,
    score_scale,
):
    scores = score_block(query_rows_all, key_block, score_scale)
    weights = jnp.where(visible, jnp.exp(scores - log_total[..., None]), 0.0)
    weights_low = weights.astype(jnp.bfloat16)
    weight_grad = jnp.einsum(
        "ngmd,kgd->gmnk", incoming_gradient, value_block, preferred_element_type=jnp.float32
    )
    score_grad = (weights * (weight_grad - row_dot[..., None])).astype(jnp.bfloat16)
    query_add = jnp.einsum(
        "gmnk,kgd->ngmd", score_grad, key_block, preferred_element_type=jnp.float32
    )
    key_add = (
        jnp.einsum("gmnk,ngmd->kgd", score_grad, query_rows_all, preferred_element_type=jnp.float32)
        * score_scale
    )
    value_add = jnp.einsum(
        "gmnk,ngmd->kgd", weights_low, incoming_gradient, preferred_element_type=jnp.float32
    )
    return (query_add, key_add, value_add)


def grads_collect(
    query_rows_all,
    incoming_gradient,
    log_total,
    row_dot,
    keys,
    values,
    visible_fn,
    block_rows,
    query_total,
    score_scale,
):
    blocks = keys.shape[0] // block_rows

    def grads_advance(block_index, carried):
        running_query, key_buffer, value_buffer = carried
        key_start = block_index * block_rows
        key_block = lax.dynamic_slice_in_dim(keys, key_start, block_rows, 0)
        value_block = lax.dynamic_slice_in_dim(values, key_start, block_rows, 0)
        visible = visible_fn(key_start, block_rows)[None, None]
        query_add, key_add, value_add = block_grads(
            query_rows_all,
            incoming_gradient,
            log_total,
            row_dot,
            key_block,
            value_block,
            visible,
            score_scale,
        )
        key_buffer = lax.dynamic_update_slice_in_dim(key_buffer, key_add, key_start, 0)
        value_buffer = lax.dynamic_update_slice_in_dim(value_buffer, value_add, key_start, 0)
        return (running_query + query_add, key_buffer, value_buffer)

    empty_buffer = jnp.zeros(keys.shape, jnp.float32)
    return lax.fori_loop(0, blocks, grads_advance, (query_total, empty_buffer, empty_buffer))


def on_device(
    prompt_query_projection,
    prompt_key_projection,
    prompt_value_projection,
    prompt_output_gradient,
    response_query,
    response_key_projection,
    response_value_projection,
    response_output_gradient,
    query_projection_bias,
    key_projection_bias,
    value_projection_bias,
    segments,
    lengths,
):
    query_groups = QUERY_HEADS // KEY_VALUE_HEADS
    score_scale = HEAD_SIZE ** (-0.5)
    prompt_row_block = prompt_query_projection.shape[1]
    reply_rows = response_query.shape[2]
    query_number = prompt_row_block + reply_rows
    context_parts = lax.axis_size("ctx")
    prompt_parts = lax.axis_size(("ctx", "branch"))
    prompt_index = lax.axis_index(("ctx", "branch"))
    context_index = lax.axis_index("ctx")
    prompt_gradient_total = prompt_row_block * prompt_parts
    answer_total = reply_rows * context_parts
    prompt_slots = prompt_index * prompt_row_block + jnp.arange(prompt_row_block, dtype=jnp.int32)
    reply_slots = context_index * reply_rows + jnp.arange(reply_rows, dtype=jnp.int32)
    length = lengths[0, 0]
    prompt_queries = prepare_inputs(
        prompt_query_projection[0], query_projection_bias, QUERY_HEADS, prompt_slots
    )
    answer_queries = prepare_inputs(
        response_query[0, 0],
        query_projection_bias,
        QUERY_HEADS,
        prompt_gradient_total + reply_slots,
    )
    query_rows_all = jnp.concatenate([prompt_queries, answer_queries], axis=0).reshape(
        query_number, KEY_VALUE_HEADS, query_groups, HEAD_SIZE
    )
    prompt_key_rows = prepare_inputs(
        prompt_key_projection[0], key_projection_bias, KEY_VALUE_HEADS, prompt_slots
    )
    prompt_values = (
        (
            prompt_value_projection[0].astype(jnp.float32)
            + value_projection_bias.astype(jnp.float32)[None, :]
        )
        .astype(jnp.bfloat16)
        .reshape(prompt_row_block, KEY_VALUE_HEADS, HEAD_SIZE)
    )
    reply_keys = prepare_inputs(
        response_key_projection[0, 0],
        key_projection_bias,
        KEY_VALUE_HEADS,
        prompt_gradient_total + reply_slots,
    )
    answer_values = (
        (
            response_value_projection[0, 0].astype(jnp.float32)
            + value_projection_bias.astype(jnp.float32)[None, :]
        )
        .astype(jnp.bfloat16)
        .reshape(reply_rows, KEY_VALUE_HEADS, HEAD_SIZE)
    )
    validity = jnp.concatenate([jnp.ones((prompt_row_block,), bool), reply_slots < length], axis=0)
    incoming_gradient = jnp.concatenate(
        [prompt_output_gradient[0], response_output_gradient[0, 0]], axis=0
    )
    incoming_gradient = jnp.where(
        validity[:, None], incoming_gradient, jnp.zeros_like(incoming_gradient)
    )
    incoming_gradient = incoming_gradient.reshape(
        query_number, KEY_VALUE_HEADS, query_groups, HEAD_SIZE
    )
    segment_ids = segments[0]
    segment_range = jnp.arange(SEGS, dtype=jnp.int32)
    below_counts = jnp.sum(
        (segment_ids[:, None] < segment_range[None, :]).astype(jnp.int32), axis=0
    )
    segment_starts = lax.psum(below_counts, ("ctx", "branch"))
    own_starts = jnp.sum(
        jnp.where(segment_ids[:, None] == segment_range[None, :], segment_starts[None, :], 0),
        axis=1,
    )
    gathered_keys, gathered_values = (
        lax.all_gather(prompt_key_rows, ("ctx", "branch"), axis=0, tiled=True),
        lax.all_gather(prompt_values, ("ctx", "branch"), axis=0, tiled=True),
    )
    answer_keys_all, answer_values_all = (
        lax.all_gather(reply_keys, "ctx", axis=0, tiled=True),
        lax.all_gather(answer_values, "ctx", axis=0, tiled=True),
    )

    def prompt_visible(key_start, block_rows):
        key_places = key_start + jnp.arange(block_rows, dtype=jnp.int32)
        earlier = (key_places[None, :] <= prompt_slots[:, None]) & (
            key_places[None, :] >= own_starts[:, None]
        )
        return jnp.concatenate([earlier, jnp.ones((reply_rows, block_rows), bool)], axis=0)

    def answer_visible(key_start, block_rows):
        key_places = key_start + jnp.arange(block_rows, dtype=jnp.int32)
        return (key_places[None, :] <= reply_slots[:, None]) & (key_places[None, :] < length)

    prompt_block = min(512, prompt_gradient_total)
    answer_block = min(512, answer_total)
    answer_part = query_rows_all[prompt_row_block:]
    start_state = (
        jnp.full((KEY_VALUE_HEADS, query_groups, query_number), score_masked, jnp.float32),
        jnp.zeros((KEY_VALUE_HEADS, query_groups, query_number), jnp.float32),
    )
    highest, running_total = stat_pass(
        query_rows_all, gathered_keys, prompt_visible, prompt_block, start_state, score_scale
    )
    answer_high, answer_total_sum = stat_pass(
        answer_part,
        answer_keys_all,
        answer_visible,
        answer_block,
        (highest[..., prompt_row_block:], running_total[..., prompt_row_block:]),
        score_scale,
    )
    highest = jnp.concatenate([highest[..., :prompt_row_block], answer_high], axis=-1)
    running_total = jnp.concatenate(
        [running_total[..., :prompt_row_block], answer_total_sum], axis=-1
    )
    log_total = highest + jnp.log(running_total)
    output_total = jnp.zeros((query_number, KEY_VALUE_HEADS, query_groups, HEAD_SIZE), jnp.float32)
    output_total = output_pass(
        query_rows_all,
        gathered_keys,
        gathered_values,
        log_total,
        prompt_visible,
        prompt_block,
        output_total,
        score_scale,
    )
    answer_sum = output_pass(
        answer_part,
        answer_keys_all,
        answer_values_all,
        log_total[..., prompt_row_block:],
        answer_visible,
        answer_block,
        output_total[prompt_row_block:],
        score_scale,
    )
    output_total = jnp.concatenate([output_total[:prompt_row_block], answer_sum], axis=0)
    output_low = jnp.where(validity[:, None, None, None], output_total, 0.0).astype(jnp.bfloat16)
    row_dot = jnp.sum(
        incoming_gradient.astype(jnp.float32) * output_low.astype(jnp.float32), axis=-1
    )
    row_dot = jnp.transpose(row_dot, (1, 2, 0))
    query_total = jnp.zeros((query_number, KEY_VALUE_HEADS, query_groups, HEAD_SIZE), jnp.float32)
    query_total, key_buffer, value_buffer = grads_collect(
        query_rows_all,
        incoming_gradient,
        log_total,
        row_dot,
        gathered_keys,
        gathered_values,
        prompt_visible,
        prompt_block,
        query_total,
        score_scale,
    )
    prompt_key_total, prompt_value_total = (
        lax.psum_scatter(key_buffer, ("ctx", "branch"), scatter_dimension=0, tiled=True),
        lax.psum_scatter(value_buffer, ("ctx", "branch"), scatter_dimension=0, tiled=True),
    )
    answer_query_sum, answer_buffer, answer_value_buffer = grads_collect(
        answer_part,
        incoming_gradient[prompt_row_block:],
        log_total[..., prompt_row_block:],
        row_dot[..., prompt_row_block:],
        answer_keys_all,
        answer_values_all,
        answer_visible,
        answer_block,
        query_total[prompt_row_block:],
        score_scale,
    )
    answer_key_sum, reply_value_total = (
        lax.psum_scatter(
            answer_buffer.astype(jnp.bfloat16), "ctx", scatter_dimension=0, tiled=True
        ).astype(jnp.float32),
        lax.psum_scatter(
            answer_value_buffer.astype(jnp.bfloat16), "ctx", scatter_dimension=0, tiled=True
        ).astype(jnp.float32),
    )
    query_total = (
        jnp.concatenate([query_total[:prompt_row_block], answer_query_sum], axis=0) * score_scale
    )
    query_places = jnp.concatenate([prompt_slots, prompt_gradient_total + reply_slots], axis=0)
    query_pre = inverse_rotation(
        query_total.reshape(query_number, QUERY_HEADS, HEAD_SIZE), query_places
    ).reshape(query_number, QUERY_HEADS * HEAD_SIZE)
    prompt_key_unbiased = inverse_rotation(prompt_key_total, prompt_slots).reshape(
        prompt_row_block, KEY_VALUE_HEADS * HEAD_SIZE
    )
    prompt_value_unbiased = prompt_value_total.reshape(
        prompt_row_block, KEY_VALUE_HEADS * HEAD_SIZE
    )
    answer_key_pre = inverse_rotation(answer_key_sum, prompt_gradient_total + reply_slots).reshape(
        reply_rows, KEY_VALUE_HEADS * HEAD_SIZE
    )
    reply_value_unbiased = reply_value_total.reshape(reply_rows, KEY_VALUE_HEADS * HEAD_SIZE)
    query_bias_grad, key_bias_grad, value_bias_grad = lax.psum(
        (
            jnp.sum(query_pre, axis=0),
            jnp.sum(prompt_key_unbiased, axis=0) + jnp.sum(answer_key_pre, axis=0),
            jnp.sum(prompt_value_unbiased, axis=0) + jnp.sum(reply_value_unbiased, axis=0),
        ),
        ("dp", "ctx", "branch"),
    )
    flat_output = output_low.reshape(query_number, QUERY_HEADS * HEAD_SIZE)
    query_low = query_pre.astype(jnp.bfloat16)
    return (
        flat_output[:prompt_row_block][None],
        flat_output[prompt_row_block:][None, None],
        query_low[:prompt_row_block][None],
        prompt_key_unbiased.astype(jnp.bfloat16)[None],
        prompt_value_unbiased.astype(jnp.bfloat16)[None],
        query_low[prompt_row_block:][None, None],
        answer_key_pre.astype(jnp.bfloat16)[None, None],
        reply_value_unbiased.astype(jnp.bfloat16)[None, None],
        query_bias_grad,
        key_bias_grad,
        value_bias_grad,
    )


def solution(mesh):
    return jax.shard_map(
        on_device,
        mesh=mesh,
        in_specs=(
            P("dp", ("ctx", "branch"), None),
            P("dp", ("ctx", "branch"), None),
            P("dp", ("ctx", "branch"), None),
            P("dp", ("ctx", "branch"), None),
            P("dp", "branch", "ctx", None),
            P("dp", "branch", "ctx", None),
            P("dp", "branch", "ctx", None),
            P("dp", "branch", "ctx", None),
            P(),
            P(),
            P(),
            P("dp", ("ctx", "branch")),
            P("dp", "branch"),
        ),
        out_specs=(
            P("dp", ("ctx", "branch"), None),
            P("dp", "branch", "ctx", None),
            P("dp", ("ctx", "branch"), None),
            P("dp", ("ctx", "branch"), None),
            P("dp", ("ctx", "branch"), None),
            P("dp", "branch", "ctx", None),
            P("dp", "branch", "ctx", None),
            P("dp", "branch", "ctx", None),
            P(),
            P(),
            P(),
        ),
        check_vma=False,
    )
```

profile of v0, /device:TPU:0, one launch (start us, length us, event | category | flops | bytes accessed | tf_op | source)
XLA Modules:
  0.0 1787.4 jit_solution(10917703910852265222)
XLA Ops:
  23.9 22.0 %psum.28 = s32[4]{0:T(128)S(1)} all-reduce(s32[4]{0:T(128)S(1)} %convert_reduce_fusion.1), channel_id=1, replica_groups=mesh['dp'=2,'ctx'=32,'branch'=2] {'ctx','branch'}, use_global_device_ids=true, to_apply=%region_1.2 | all-reduce | flops 4 | bytes 32 | tf_op jit(solution)/shard_map/psum | solution.py:240
  52.8 6.0 all-gather.9.cloned.1.call-done
  60.6 44.2 %all-gather.11.cloned.1.call-done = bf16[2048,4,128]{2,1,0:T(4,128)(2,1)} async-done(((bf16[64,4,128]{2,1,0:T(4,128)(2,1)}), bf16[2048,4,128]{2,1,0:T(4,128)(2,1)}) %all-gather.11.cloned.1.call-update) | async-done | bytes 2097168 | tf_op jit(solution)/shard_map/all_gather | solution.py:251
  108.0 71.9 %all-gather.7.cloned.1.call-done = bf16[4096,4,128]{2,1,0:T(4,128)(2,1)} async-done(((bf16[64,4,128]{2,1,0:T(4,128)(2,1)}), bf16[4096,4,128]{2,1,0:T(4,128)(2,1)}) %all-gather.7.cloned.1.call-update) | async-done | bytes 4194320 | tf_op jit(solution)/shard_map/all_gather | solution.py:246
  179.9 4.8 copy.219
  184.7 66.9 %while.99 = (s32[]{:T(128)}, f32[4,5,128]{2,1,0:T(8,128)S(1)}, f32[4,5,128]{2,1,0:T(8,128)S(1)}, s32[64]{0:T(128)S(1)}, bf16[4096,4,128]{2,0,1:T(8,128)(2,1)}, /...) while((s32[]{:T(128)}, f32[4,5,128]{2,1,0:T(8,128)S(1)}, ...), condition=%wide.region_6.7_spmd.clone, body=%wide.region_3.6_spmd.clone.sunk | while | flops 346141760 | bytes 12065731 | solution.py:67
  185.3 4.3 fusion.242
  193.6 4.3 fusion.242
  201.9 4.3 fusion.242
  210.2 4.3 fusion.242
  218.4 4.3 fusion.242
  226.7 4.3 fusion.242
  235.1 4.3 fusion.242
  243.4 4.3 fusion.242
  251.7 9.2 while.96
  261.7 54.3 %while.100 = (s32[]{:T(128)}, f32[128,4,5,128]{0,3,2,1:T(8,128)}, bf16[4096,4,128]{2,1,0:T(4,128)(2,1)}, s32[64]{0:T(128)S(1)}, bf16[4096,4,128]{2,0,1:T(8,128)(...) while((s32[]{:T(128)}, f32[128,4,5,128]{0,3,2,1:T(8,128)}, ...), condition=%wide.region_12.13_spmd.clone, body=%wide.region_11.12_spmd.clone.sunk | while | flops 677085760 | bytes 6634446 | solution.py:88
  270.7 4.2 fusion.248
  277.5 4.2 fusion.248
  284.4 4.2 fusion.248
  291.2 4.2 fusion.248
  298.0 4.2 fusion.248
  304.9 4.2 fusion.248
  311.7 4.2 fusion.248
  324.3 15.3 while.97
  352.6 3.9 broadcast_in_dim.357
  356.6 109.3 %while.101 = (s32[]{:T(128)}, f32[128,4,5,128]{0,3,2,1:T(8,128)}, f32[4096,4,128]{2,1,0:T(4,128)}, f32[4096,4,128]{2,0,1:T(8,128)}, bf16[4096,4,128]{2,0,1:T(8,1...) while((s32[]{:T(128)}, f32[128,4,5,128]{0,3,2,1:T(8,128)}, ...), condition=%wide.region_17.18_spmd.clone, body=%wide.region_16.17_spmd.clone.sunk | while | flops 1691845120 | bytes 83135600 | solution.py:156
  472.9 33.6 %while.98 = (s32[]{:T(128)}, f32[64,4,5,128]{3,0,2,1:T(8,128)S(1)}, bf16[2048,4,128]{2,1,0:T(4,128)(2,1)}, bf16[2048,4,128]{2,0,1:T(8,128)(2,1)}, bf16[2048,4,12...) while((s32[]{:T(128)}, f32[64,4,5,128]{3,0,2,1:T(8,128)S(1)}, ...), condition=%wide.region_19.20_spmd.clone, body=%wide.region_18.19_spmd.clone.sunk | while | flops 846169664 | bytes 35520296 | solution.py:156
  530.8 80.2 %all-reduce.12.cloned.1.call-done = bf16[2048,4,128]{2,1,0:T(4,128)(2,1)} async-done(((bf16[2048,4,128]{2,1,0:T(4,128)(2,1)}), bf16[2048,4,128]{2,1,0:T(4,128)(2,1)}) %all-reduce.12.cloned.1.call-update) | async-done | bytes 2097168
  613.7 79.3 %reduce-scatter.5.cloned.1.call-done = bf16[64,4,128]{2,0,1:T(8,128)(2,1)} async-done(((bf16[2048,4,128]{2,0,1:T(8,128)(2,1)}), bf16[64,4,128]{2,0,1:T(8,128)(2,1)}) %reduce-scatter.5.cloned.1.call-update) | async-done | bytes 65552 | tf_op jit(solution)/shard_map/reduce_scatter | solution.py:348
  695.4 672.9 %all-reduce.10.cloned.1.call-done = f32[4096,4,128]{2,1,0:T(4,128)} async-done(((f32[4096,4,128]{2,1,0:T(4,128)}), f32[4096,4,128]{2,1,0:T(4,128)}) %all-reduce.10.cloned.1.call-update) | async-done | bytes 8388624
  1371.1 344.8 %reduce-scatter.3.cloned.1.call-done = f32[64,4,128]{2,0,1:T(8,128)} async-done(((f32[4096,4,128]{2,0,1:T(8,128)}), f32[64,4,128]{2,0,1:T(8,128)}) %reduce-scatter.3.cloned.1.call-update) | async-done | bytes 131088 | tf_op jit(solution)/shard_map/reduce_scatter | solution.py:330
  1717.7 62.7 %all-reduce.6 = (f32[2560]{0:T(1024)}, f32[512]{0:T(512)}, f32[512]{0:T(512)}) all-reduce(f32[2560]{0:T(1024)S(1)} %bitcast.374, f32[512]{0:T(512)S(1)} %add_bitcast_fusion.1, f32[512]{0:T(512)S(1)} %add_bitcast_fusion), channel_id=1, replica_groups=mesh['dp'=2,'ctx'=32,'branch'=2] {'dp','ctx','branch'}, use_global_device_ids=true, to_apply=%region_25.26 | all-reduce | flops 3584 | bytes 28672 | tf_op jit(solution)/shard_map/psum | solution.py:369
  (558 shorter events, 311.1 us)
Async XLA Ops:
  7.2 6.8 copy-start.29
  7.2 9.4 copy-start.13
  7.2 51.6 %all-gather.9.cloned.1.call-start = ((), (), s32[]{:S(2)}) async-start(), calls=%async_computation.4 | async-start | bytes 2162688 | tf_op jit(solution)/shard_map/all_gather | solution.py:250
  7.3 3.9 copy-start.27
  11.1 38.4 %copy-start.17 = (f32[64,128]{1,0:T(8,128)}, f32[64,128]{1,0:T(8,128)S(1)}, u32[]{:S(2)}) copy-start(f32[64,128]{1,0:T(8,128)S(1)} %get-tuple-element.1563) | copy-start | bytes 98308
  11.1 38.4 %copy-start.23 = (f32[64,128]{1,0:T(8,128)}, f32[64,128]{1,0:T(8,128)S(1)}, u32[]{:S(2)}) copy-start(f32[64,128]{1,0:T(8,128)S(1)} %get-tuple-element.1562) | copy-start | bytes 98308
  11.3 5.8 copy-start.26
  11.3 5.9 copy-start.14
  12.1 92.7 %all-gather.11.cloned.1.call-start = ((), (), s32[]{:S(2)}) async-start(), calls=%async_computation.5 | async-start | bytes 2162688 | tf_op jit(solution)/shard_map/all_gather | solution.py:251
  14.7 165.2 %all-gather.7.cloned.1.call-start = ((), (), s32[]{:S(2)}) async-start(), calls=%async_computation.3 | async-start | bytes 4259840 | tf_op jit(solution)/shard_map/all_gather | solution.py:246
  15.0 34.6 %copy-start.19 = (f32[64,128]{1,0:T(8,128)}, f32[64,128]{1,0:T(8,128)S(1)}, u32[]{:S(2)}) copy-start(f32[64,128]{1,0:T(8,128)S(1)} %get-tuple-element.1564) | copy-start | bytes 98308
  15.0 34.6 %copy-start.21 = (f32[64,128]{1,0:T(8,128)}, f32[64,128]{1,0:T(8,128)S(1)}, u32[]{:S(2)}) copy-start(f32[64,128]{1,0:T(8,128)S(1)} %get-tuple-element.1565) | copy-start | bytes 98308
  15.9 245.2 %all-gather.5.cloned.1.call-start = ((), (), s32[]{:S(2)}) async-start(), calls=%async_computation.2 | async-start | bytes 4259840 | tf_op jit(solution)/shard_map/all_gather | solution.py:247
  16.5 594.5 %all-reduce.12.cloned.1.call-start = ((), (), s32[]{:S(2)}) async-start(), calls=%async_computation.9 | async-start | bytes 4194304
  16.8 6.9 copy-start.30
  318.8 5.5 copy-start.5
  339.5 6.6 copy-start.2
  356.7 3.8 copy-start.15
  370.0 3.8 copy-start.15
  397.3 3.8 copy-start.15
  411.0 3.8 copy-start.15
  424.7 3.8 copy-start.15
  438.4 3.8 copy-start.15
  506.5 186.5 %reduce-scatter.5.cloned.1.call-start = ((), (), s32[]{:S(2)}) async-start(), calls=%async_computation.7 | async-start | bytes 2162688 | tf_op jit(solution)/shard_map/reduce_scatter | solution.py:348
  507.1 861.2 %all-reduce.10.cloned.1.call-start = ((), (), s32[]{:S(2)}) async-start(), calls=%async_computation.8 | async-start | bytes 16777216
  507.8 1208.1 %reduce-scatter.3.cloned.1.call-start = ((), (), s32[]{:S(2)}) async-start(), calls=%async_computation.6 | async-start | bytes 8519680 | tf_op jit(solution)/shard_map/reduce_scatter | solution.py:330
  513.7 6.8 copy-start.7
  522.5 5.6 copy-start.10
  528.1 82.9 %copy-start.18 = (f32[64,128]{1,0:T(8,128)S(1)}, f32[64,128]{1,0:T(8,128)}, u32[]{:S(2)}) copy-start(f32[64,128]{1,0:T(8,128)} %copy-done.17) | copy-start | bytes 98308
  528.1 83.9 %copy-start.24 = (f32[64,128]{1,0:T(8,128)S(1)}, f32[64,128]{1,0:T(8,128)}, u32[]{:S(2)}) copy-start(f32[64,128]{1,0:T(8,128)} %copy-done.23) | copy-start | bytes 98308
  529.9 838.4 %copy-start.22 = (f32[64,128]{1,0:T(8,128)S(1)}, f32[64,128]{1,0:T(8,128)}, u32[]{:S(2)}) copy-start(f32[64,128]{1,0:T(8,128)} %copy-done.21) | copy-start | bytes 98308
  529.9 839.5 %copy-start.20 = (f32[64,128]{1,0:T(8,128)S(1)}, f32[64,128]{1,0:T(8,128)}, u32[]{:S(2)}) copy-start(f32[64,128]{1,0:T(8,128)} %copy-done.19) | copy-start | bytes 98308
  (45 other events, 118.1 us)
Sparse Core Ops, SparseCore 0:
  12.3 46.4 all-gather.8
  61.6 43.1 all-gather.10
  108.6 71.2 all-gather.6
  183.5 68.8 all-gather.4
  506.6 104.2 all-reduce.11
  614.4 78.5 reduce-scatter.4
  695.5 672.7 all-reduce.9
  1370.7 345.2 reduce-scatter.2
where the time goes:
time: 1800 us; the launch traced here: 1790 us
  waiting for transfers between devices  1300 us (72%)
  matrix products  179 us (10%)
  local copies, waits for them, and re-layouts  134 us (7%)
  blocking collectives  84.7 us (5%)
  other arithmetic  68.1 us (4%)
    unnamed x10, waiting for transfers between devices  755 us
    reduce_scatter x1, waiting for transfers between devices, on_device(): lax.psum_scatter(value_buffer, ('ctx', 'branch'), scatter_dimension=0, ti...  345 us
    reduce_scatter x1, waiting for transfers between devices, on_device(): lax.psum_scatter(answer_value_buffer.astype(jnp.bfloat16), 'ctx', scatter...  79.3 us
    all_gather x1, waiting for transfers between devices, on_device(): lax.all_gather(prompt_key_rows, ('ctx', 'branch'), axis=0, tiled=True)  71.9 us
    psum x1, blocking collectives, on_device(): lax.psum((jnp.sum(query_pre, axis=0), jnp.sum(prompt_key_unbiased, axis=0...  62.7 us
    dot_general x24, matrix products, score_block(): jnp.einsum('ngmd,kgd->gmnk', query_rows_all, key_block, preferred_element...  54 us
    dot_general x12, matrix products, output_advance(): jnp.einsum('gmnk,kgd->ngmd', weights, value_block, preferred_element_type...  45.7 us
    all_gather x1, waiting for transfers between devices, on_device(): lax.all_gather(answer_values, 'ctx', axis=0, tiled=True)  44.2 us
  transfers between devices with their start and end apart: 8, of which 7 were waited for; matrix products, arithmetic and copies ran while one was open for 7% of the time, Pallas kernels for 0%

commit v1 on v0

v1 whole, which is shorter than its diff:
```python
import functools

import jax
import jax.numpy as jnp
import numpy as np
from jax import lax
from jax.experimental import pallas as pl
from jax.experimental.pallas import tpu as pltpu
from jax.sharding import Mesh
from jax.sharding import PartitionSpec as P

HEADS = 4
GROUP = 5
HD = 128
ROWS = 64
STRIPE = GROUP * ROWS
PROMPT = 4096
REPLY = 2048
BLOCK = 512
SCALE = HD**-0.5
LOG2 = float(SCALE * np.log2(np.e))
LOW = -1e30
MASKED = -3e38
KV = 2 * ROWS
PKV = KV + 16
OWN = PKV + KV
PIECE = 4 * OWN + 4 * PKV

bf16 = jnp.bfloat16
f32 = jnp.float32
NT = (((1,), (1,)), ((), ()))
NN = (((1,), (0,)), ((), ()))
TN = (((0,), (0,)), ((), ()))


def dot(a, b, dims):
    return lax.dot_general(a, b, dims, preferred_element_type=f32)


def angle_tables():
    frequency = 1000000.0 ** (-(np.arange(HD // 2) * 2.0 / HD))
    frequency = np.concatenate([frequency, frequency])
    sign = np.where(np.arange(HD) < HD // 2, -1.0, 1.0)
    coarse = np.arange((PROMPT + REPLY) // ROWS)[:, None] * ROWS * frequency
    fine = np.arange(ROWS)[:, None] * frequency
    return [
        jnp.asarray(t.astype(np.float32))
        for t in (np.cos(coarse), np.sin(coarse) * sign, np.cos(fine), np.sin(fine) * sign)
    ]


def turn(tables, block):
    coarse_cos, coarse_sin, fine_cos, fine_sin = tables
    ca, sa = coarse_cos[pl.ds(block, 1), :], coarse_sin[pl.ds(block, 1), :]
    cb, sb = fine_cos[...], fine_sin[...]
    return ca * cb - sa * sb, sa * cb + ca * sb


def rotate(x, cosine, sine):
    return x * cosine + pltpu.roll(x, HD // 2, 1) * sine


def unrotate(x, cosine, sine):
    return x * cosine - pltpu.roll(x, HD // 2, 1) * sine


def prompt_block(sc, z):
    return z * 16 + sc[1] * 4 + sc[2] * 2 + sc[3]


def reply_block(sc, z):
    return z * 8 + sc[1] * 2 + sc[2]


def part(i):
    return pl.ds(pl.multiple_of(i, ROWS), ROWS)


def lanes(i):
    return pl.ds(pl.multiple_of(i * HD, HD), HD)


def prepare_kv_body(sc, pk, pv, rk, rv, kbias, vbias, seg, t0, t1, t2, t3, *outs):
    tables = (t0, t1, t2, t3)
    z = sc[0]
    prompt_turn = turn(tables, prompt_block(sc, z))
    reply_turn = turn(tables, PROMPT // ROWS + reply_block(sc, z))
    ids = seg[...]
    row = lax.broadcasted_iota(jnp.int32, (16, HD), 0)
    lane = lax.broadcasted_iota(jnp.int32, (16, HD), 1)
    note = jnp.zeros((16, HD), f32)
    for s in range(1, HEADS):
        below = jnp.sum((ids < s).astype(f32), axis=1, keepdims=True) * 0.5
        note = jnp.where((row == 0) & (lane == s), below, note)
    note = jnp.where(row == 1, ids.astype(f32), note).astype(bf16)
    for s, out in enumerate(outs):
        at = lanes(lax.rem(z + s, HEADS))
        kb, vb = kbias[:, at].astype(f32), vbias[:, at].astype(f32)
        out[0:64, :] = rotate(pk[:, at].astype(f32) + kb, *prompt_turn).astype(bf16)
        out[64:128, :] = (pv[:, at].astype(f32) + vb).astype(bf16)
        out[128:144, :] = note
        out[144:208, :] = rotate(rk[:, at].astype(f32) + kb, *reply_turn).astype(bf16)
        out[208:272, :] = (rv[:, at].astype(f32) + vb).astype(bf16)


def prepare_q_body(sc, pq, pg, rq, rg, qbias, t0, t1, t2, t3, *outs):
    tables = (t0, t1, t2, t3)
    z = sc[0]
    prompt_turn = turn(tables, prompt_block(sc, z))
    reply_turn = turn(tables, PROMPT // ROWS + reply_block(sc, z))
    place = reply_block(sc, z) * ROWS + lax.broadcasted_iota(jnp.int32, (ROWS, HD), 0)
    valid = place < sc[4]
    for s, out in enumerate(outs):
        h = lax.rem(z + s, HEADS) * GROUP
        for m in range(GROUP):
            at = lanes(h + m)
            qb = qbias[:, at].astype(f32)
            o = m * ROWS
            out[o : o + 64, :] = rotate(pq[:, at].astype(f32) + qb, *prompt_turn).astype(bf16)
            o += STRIPE
            out[o : o + 64, :] = pg[:, at]
            o += STRIPE
            out[o : o + 64, :] = rotate(rq[:, at].astype(f32) + qb, *reply_turn).astype(bf16)
            o += STRIPE
            out[o : o + 64, :] = jnp.where(valid, rg[:, at].astype(f32), 0.0).astype(bf16)


def attend_body(
    sc, *refs
):
    q_in, kv_in, tables = refs[0:4], refs[4:12], refs[12:16]
    o_out, dq_out, send, keep, bias_out = refs[16:20], refs[20:24], refs[24:28], refs[28:32], refs[32]
    (pq, pg, rq, rg, pk, pv, rk, rv, pdq, rdq, pdk, pdv, rdk, rdv, p_lse, p_rd, stat_m, stat_l,
     acc_r, note) = refs[33:]
    z, x, core, b, length = sc[0], sc[1], sc[2], sc[3], sc[4]

    for s in range(4):
        at = pl.ds(pl.multiple_of(lax.rem(z + 4 - s, 4) * STRIPE, STRIPE), STRIPE)
        for i, ref in enumerate((pq, pg, rq, rg)):
            ref[at, :] = q_in[s][i * STRIPE : (i + 1) * STRIPE, :]
    counts = jnp.zeros((16, HD), f32)
    for s in range(4):
        xx = lax.rem(x + 4 - s, 4)
        for other in range(2):
            piece = kv_in[s * 2 + other]
            cc = core if other == 0 else 1 - core
            for t in range(4):
                zz = lax.rem(z + 4 - t, 4)
                to = part((zz * 8 + xx * 2 + cc) * ROWS)
                o = t * OWN + PKV
                rk[to, :] = piece[o : o + 64, :]
                rv[to, :] = piece[o + 64 : o + 128, :]
                for far in range(2):
                    bb = b if far == 0 else 1 - b
                    to = part((zz * 16 + xx * 4 + cc * 2 + bb) * ROWS)
                    o = t * OWN if far == 0 else 4 * OWN + t * PKV
                    pk[to, :] = piece[o : o + 64, :]
                    pv[to, :] = piece[o + 64 : o + 128, :]
                    told = piece[o + 128 : o + 144, :].astype(f32)
                    counts = counts + told
                    if s == 0 and other == 0 and far == 0:
                        note[pl.ds(zz, 1)] = told[None]

    lane = lax.broadcasted_iota(jnp.int32, (1, HD), 1)
    starts = [
        jnp.sum(jnp.where(lane == s, counts[0:1, :], 0.0)).astype(jnp.int32) for s in range(HEADS)
    ]

    def prompt_limits(j):
        ids = note[j, 1:2, :].astype(jnp.int32)
        start = jnp.zeros((1, HD), jnp.int32)
        for s in range(1, HEADS):
            start = jnp.where(ids == s, starts[s], start)
        first = jnp.sum(jnp.where(lane == 0, start, 0))
        place = prompt_block(sc, j) * ROWS + jnp.bitwise_and(lane, ROWS - 1)
        start = jnp.concatenate([start, start, start[:, :64]], axis=1)
        place = jnp.concatenate([place, place, place[:, :64]], axis=1)
        lowest = first // BLOCK
        highest = (prompt_block(sc, j) * ROWS + ROWS - 1) // BLOCK + 1
        return start, place, lowest, highest

    def prompt_seen(key_at, start, place):
        key = key_at + lax.broadcasted_iota(jnp.int32, (BLOCK, STRIPE), 0)
        return (key >= start) & (key <= place)

    column = lax.broadcasted_iota(jnp.int32, (1, 4 * STRIPE), 1)
    stripe = sum((column >= j * STRIPE).astype(jnp.int32) for j in range(1, 4))
    reply_place = reply_block(sc, stripe) * ROWS + jnp.bitwise_and(column, ROWS - 1)

    def reply_seen(key_at, place):
        key = key_at + lax.broadcasted_iota(jnp.int32, (BLOCK, place.shape[1]), 0)
        return (key < length) & (key <= place)

    def online(state, q, k, v, seen):
        top, total, acc = state
        scores = dot(k, q, NT) * LOG2
        if seen is not None:
            scores = jnp.where(seen, scores, MASKED)
        raised = jnp.maximum(top, jnp.max(scores, axis=0, keepdims=True))
        shrink = jnp.exp2(top - raised)
        p = jnp.exp2(scores - raised)
        total = total * shrink + jnp.sum(p, axis=0, keepdims=True)
        return raised, total, acc * shrink + dot(v, p.astype(bf16), TN)

    def empty(n):
        return jnp.full((1, n), LOW, f32), jnp.zeros((1, n), f32), jnp.zeros((HD, n), f32)

    q_all = rq[...]

    def forward_reply(i, state):
        at = pl.ds(pl.multiple_of(i * BLOCK, BLOCK), BLOCK)
        return online(state, q_all, pk[at, :], pv[at, :], None)

    top, total, acc = lax.fori_loop(0, PROMPT // BLOCK, forward_reply, empty(4 * STRIPE))
    half = 2 * STRIPE
    for i in range(4):
        at = slice(i * BLOCK, (i + 1) * BLOCK)
        if i < 2:
            top, total, acc = online(
                (top, total, acc), q_all, rk[at, :], rv[at, :], reply_seen(i * BLOCK, reply_place)
            )
            if i == 1:
                stat_m[0:1, :] = top
                stat_l[0:1, :] = total
                acc_r[...] = acc
                state = (top[:, half:], total[:, half:], acc[:, half:])
        else:
            state = online(
                state, rq[half:, :], rk[at, :], rv[at, :], reply_seen(i * BLOCK, reply_place[:, half:])
            )
    stat_m[0:1, half:] = state[0]
    stat_l[0:1, half:] = state[1]
    acc_r[:, half:] = state[2]
    total = stat_l[0:1, :]
    r_lse = stat_m[0:1, :] + jnp.log2(total)
    out = jnp.where(reply_place < length, acc_r[...] / total, 0.0).astype(bf16).astype(f32)
    r_rd = jnp.sum(out * rg[...].astype(f32).T, axis=0, keepdims=True)
    stat_m[0:1, :] = r_lse
    stat_l[0:1, :] = r_rd
    acc_r[...] = out
    out = acc_r[...].T.astype(bf16)
    rk_out = out

    p_out = []
    limits = [prompt_limits(j) for j in range(4)]
    for j in range(4):
        start, place, lowest, highest = limits[j]
        rows = slice(j * STRIPE, (j + 1) * STRIPE)

        def forward_prompt(i, state, rows=rows, start=start, place=place):
            key_at = pl.multiple_of(i * BLOCK, BLOCK)
            at = pl.ds(key_at, BLOCK)
            return online(
                state, pq[rows, :], pk[at, :], pv[at, :], prompt_seen(key_at, start, place)
            )

        top, total, acc = lax.fori_loop(lowest, highest, forward_prompt, empty(STRIPE))
        out = (acc / total).astype(bf16).astype(f32)
        p_lse[j, 0:1, :] = top + jnp.log2(total)
        p_rd[j, 0:1, :] = jnp.sum(out * pg[rows, :].astype(f32).T, axis=0, keepdims=True)
        p_out.append(out.T.astype(bf16))
    pdq[...] = jnp.concatenate(p_out, axis=0).astype(f32)
    rdq[...] = rk_out.astype(f32)
    for s in range(4):
        at = pl.ds(pl.multiple_of(lax.rem(z + 4 - s, 4) * STRIPE, STRIPE), STRIPE)
        o_out[s][0:STRIPE, :] = pdq[at, :].astype(bf16)
        o_out[s][STRIPE:, :] = rdq[at, :].astype(bf16)

    pdq[...] = jnp.zeros_like(pdq)
    rdq[...] = jnp.zeros_like(rdq)

    def grads(q, g, lse, rd, k, v, seen):
        w = jnp.exp2(dot(k, q, NT) * LOG2 - lse)
        if seen is not None:
            w = jnp.where(seen, w, 0.0)
        ds = (w * (dot(v, g, NT) - rd)).astype(bf16)
        return dot(ds, q, NN), dot(w.astype(bf16), g, NN), dot(ds, k, TN)

    def backward_reply(i, carry):
        at = pl.ds(pl.multiple_of(i * BLOCK, BLOCK), BLOCK)
        dk, dv, dq = grads(
            rq[...], rg[...], stat_m[0:1, :], stat_l[0:1, :], pk[at, :], pv[at, :], None
        )
        pdk[at, :] = dk
        pdv[at, :] = dv
        rdq[...] += dq
        return carry

    lax.fori_loop(0, PROMPT // BLOCK, backward_reply, 0)
    for j in range(4):
        start, place, lowest, highest = limits[j]
        rows = slice(j * STRIPE, (j + 1) * STRIPE)

        def backward_prompt(i, carry, j=j, rows=rows, start=start, place=place):
            key_at = pl.multiple_of(i * BLOCK, BLOCK)
            at = pl.ds(key_at, BLOCK)
            dk, dv, dq = grads(
                pq[rows, :], pg[rows, :], p_lse[j, 0:1, :], p_rd[j, 0:1, :],
                pk[at, :], pv[at, :], prompt_seen(key_at, start, place),
            )
            pdk[at, :] += dk
            pdv[at, :] += dv
            pdq[rows, :] += dq
            return carry

        lax.fori_loop(lowest, highest, backward_prompt, 0)
    for i in range(4):
        at = slice(i * BLOCK, (i + 1) * BLOCK)
        cols = slice(0 if i < 2 else half, 4 * STRIPE)
        dk, dv, dq = grads(
            rq[cols, :], rg[cols, :], stat_m[0:1, cols], stat_l[0:1, cols], rk[at, :], rv[at, :],
            reply_seen(i * BLOCK, reply_place[:, cols]),
        )
        rdk[at, :] = dk
        rdv[at, :] = dv
        rdq[cols, :] += dq

    head_sums = [jnp.zeros((1, HD), f32) for _ in range(GROUP)]
    for s in range(4):
        zz = lax.rem(z + 4 - s, 4)
        for i, (ref, base) in enumerate(
            ((pdq, prompt_block(sc, zz)), (rdq, PROMPT // ROWS + reply_block(sc, zz)))
        ):
            cosine, sine = turn(tables, base)
            for m in range(GROUP):
                at = part(zz * STRIPE + m * ROWS)
                pre = unrotate(ref[at, :] * SCALE, cosine, sine)
                head_sums[m] = head_sums[m] + jnp.sum(pre, axis=0, keepdims=True)
                o = i * STRIPE + m * ROWS
                dq_out[s][o : o + ROWS, :] = pre.astype(bf16)

    def sum_rows(i, carry):
        key_sum, value_sum = carry
        at = part(i * ROWS)
        cosine, sine = turn(tables, i)
        return key_sum + unrotate(pdk[at, :], cosine, sine), value_sum + pdv[at, :]

    def sum_reply_rows(i, carry):
        key_sum, value_sum = carry
        at = part(i * ROWS)
        cosine, sine = turn(tables, PROMPT // ROWS + i)
        return key_sum + unrotate(rdk[at, :], cosine, sine), value_sum + rdv[at, :]

    zero = jnp.zeros((ROWS, HD), f32)
    sums = lax.fori_loop(0, PROMPT // ROWS, sum_rows, (zero, zero))
    key_sum, value_sum = lax.fori_loop(0, REPLY // ROWS, sum_reply_rows, sums)
    for m in range(GROUP):
        bias_out[m : m + 1, :] = head_sums[m]
    bias_out[5:6, :] = jnp.sum(key_sum, axis=0, keepdims=True) * SCALE
    bias_out[6:7, :] = jnp.sum(value_sum, axis=0, keepdims=True)
    bias_out[7:8, :] = jnp.zeros((1, HD), f32)
    for s in range(4):
        xx = lax.rem(x + s, 4)
        for t in range(4):
            zz = lax.rem(z + t, 4)
            for far in range(2):
                bb = b if far == 0 else 1 - b
                own = part((zz * 16 + xx * 4 + core * 2 + bb) * ROWS)
                theirs = part((zz * 16 + xx * 4 + (1 - core) * 2 + bb) * ROWS)
                o = far * 512 + t * ROWS
                keep[s][o : o + 64, :] = pdk[own, :] * SCALE
                keep[s][o + 256 : o + 320, :] = pdv[own, :]
                send[s][o : o + 64, :] = (pdk[theirs, :] * SCALE).astype(bf16)
                send[s][o + 256 : o + 320, :] = pdv[theirs, :].astype(bf16)
            own = part((zz * 8 + xx * 2 + core) * ROWS)
            theirs = part((zz * 8 + xx * 2 + 1 - core) * ROWS)
            o = 1024 + t * ROWS
            keep[s][o : o + 64, :] = rdk[own, :] * SCALE
            keep[s][o + 256 : o + 320, :] = rdv[own, :]
            send[s][o : o + 64, :] = (rdk[theirs, :] * SCALE).astype(bf16)
            send[s][o + 256 : o + 320, :] = rdv[theirs, :].astype(bf16)


def settle_body(sc, total, far, t0, t1, t2, t3, *outs):
    tables = (t0, t1, t2, t3)
    z = sc[0]
    for t, out in enumerate(outs):
        zz = lax.rem(z + t, 4)
        o = t * ROWS
        key = total[o : o + 64, :] + far[o : o + 64, :].astype(f32)
        out[0:64, :] = unrotate(key, *turn(tables, prompt_block(sc, zz))).astype(bf16)
        value = total[o + 256 : o + 320, :] + far[o + 256 : o + 320, :].astype(f32)
        out[64:128, :] = value.astype(bf16)
        o += 1024
        base = PROMPT // ROWS + reply_block(sc, zz)
        out[128:192, :] = unrotate(total[o : o + 64, :], *turn(tables, base)).astype(bf16)
        out[192:256, :] = total[o + 256 : o + 320, :].astype(bf16)


def gather_heads_body(step, sc, *refs):
    pieces, outs = refs[:4], refs[4:]
    z = sc[0]
    for s, piece in enumerate(pieces):
        h = lax.rem(z + (s * step) % 4, 4)
        width = piece.shape[0] // ROWS // len(outs)
        for i, out in enumerate(outs):
            for m in range(width):
                o = (i * width + m) * ROWS
                out[:, lanes(h * width + m)] = piece[o : o + ROWS, :]


def call(body, n_in, outs, scratch=()):
    spec = pl.BlockSpec(memory_space=pltpu.VMEM)
    return pl.pallas_call(
        body,
        in_specs=[pl.BlockSpec(memory_space=pltpu.SMEM)] + [spec] * n_in,
        out_specs=[spec] * len(outs),
        out_shape=[jax.ShapeDtypeStruct(s, t) for s, t in outs],
        scratch_shapes=list(scratch),
        compiler_params=pltpu.CompilerParams(vmem_limit_bytes=56 * 1024 * 1024),
    )


def shift(v, axis, s):
    n = lax.axis_size(axis)
    return lax.ppermute(v, axis, [(i, (i + s) % n) for i in range(n)])


def swap(v, axis, bit):
    return lax.ppermute(v, axis, [(i, i ^ bit) for i in range(lax.axis_size(axis))])


def on_device(pq, pk, pv, pg, rq, rk, rv, rg, qbias, kbias, vbias, segments, lengths):
    sc = jnp.stack(
        [lax.axis_index(a) for a in ("z", "x", "core", "branch")] + [lengths[0, 0]]
    ).astype(jnp.int32)
    tables = angle_tables()
    kbias, vbias, qbias = kbias[None], vbias[None], qbias[None]
    seg = jnp.concatenate([segments, segments], axis=1)
    kv = call(prepare_kv_body, 11, [((OWN, HD), bf16)] * 4)(
        sc, pk[0], pv[0], rk[0, 0], rv[0, 0], kbias, vbias, seg, *tables
    )
    kv = jnp.stack([kv[0]] + [shift(kv[s], "z", s) for s in (1, 2, 3)])
    q = call(prepare_q_body, 9, [((4 * STRIPE, HD), bf16)] * 4)(
        sc, pq[0], pg[0], rq[0, 0], rg[0, 0], qbias, *tables
    )
    q = [q[0]] + [shift(q[s], "z", s) for s in (1, 2, 3)]
    far = shift(kv[:, :PKV].reshape(4 * PKV, HD), "branch", 1)
    kv = jnp.concatenate([kv.reshape(4 * OWN, HD), far])
    pieces = []
    for s in range(4):
        piece = kv if s == 0 else shift(kv, "x", s)
        pieces += [piece, shift(piece, "core", 1)]

    rows = 4 * STRIPE
    outs = call(
        attend_body,
        16,
        [((2 * STRIPE, HD), bf16)] * 8 + [((1536, HD), bf16)] * 4 + [((1536, HD), f32)] * 4
        + [((8, HD), f32)],
        [pltpu.VMEM((rows, HD), bf16)] * 4
        + [pltpu.VMEM((PROMPT, HD), bf16)] * 2
        + [pltpu.VMEM((REPLY, HD), bf16)] * 2
        + [pltpu.VMEM((rows, HD), f32)] * 2
        + [pltpu.VMEM((PROMPT, HD), f32)] * 2
        + [pltpu.VMEM((REPLY, HD), f32)] * 2
        + [pltpu.VMEM((4, 8, STRIPE), f32)] * 2
        + [pltpu.VMEM((8, rows), f32)] * 2
        + [pltpu.VMEM((HD, rows), f32), pltpu.VMEM((4, 16, HD), f32)],
    )(sc, *q, *pieces, *tables)
    o, dq, send, keep, bias = outs[0:4], outs[4:8], outs[8:12], outs[12:16], outs[16]

    o = [o[0]] + [shift(o[s], "z", -s) for s in (1, 2, 3)]
    dq = [dq[0]] + [shift(dq[s], "z", -s) for s in (1, 2, 3)]
    summed = [keep[s] + shift(send[s], "core", 1).astype(f32) for s in range(4)]
    total = summed[0]
    for s in (1, 2, 3):
        total = total + shift(summed[s].astype(bf16), "x", s).astype(f32)
    near = shift(total[512:1024].astype(bf16), "branch", 1)
    dkv = call(settle_body, 6, [((4 * ROWS, HD), bf16)] * 4)(sc, total, near, *tables)
    dkv = [dkv[0]] + [shift(dkv[s], "z", s) for s in (1, 2, 3)]

    wide = ((ROWS, HEADS * GROUP * HD), bf16)
    narrow = ((ROWS, HEADS * HD), bf16)
    p_out, r_out = call(functools.partial(gather_heads_body, 1), 4, [wide] * 2)(sc, *o)
    p_dq, r_dq = call(functools.partial(gather_heads_body, 1), 4, [wide] * 2)(sc, *dq)
    p_dk, p_dv, r_dk, r_dv = call(functools.partial(gather_heads_body, 3), 4, [narrow] * 4)(
        sc, *dkv
    )

    bias = bias + swap(bias, "core", 1)
    bias = bias + swap(bias, "x", 1)
    bias = bias + swap(bias, "x", 2)
    bias = bias + swap(bias, "branch", 1)
    bias = bias + swap(bias, "dp", 1)
    z = lax.axis_index("z")
    bias = jnp.where(jnp.arange(4)[:, None, None] == z, bias[None], 0.0)
    bias = bias + swap(bias, "z", 1)
    bias = bias + swap(bias, "z", 2)
    return (
        p_out[None],
        r_out[None, None],
        p_dq[None],
        p_dk[None],
        p_dv[None],
        r_dq[None, None],
        r_dk[None, None],
        r_dv[None, None],
        bias[:, :5].reshape(-1),
        bias[:, 5].reshape(-1),
        bias[:, 6].reshape(-1),
    )


def solution(mesh):
    fine = Mesh(mesh.devices.reshape(2, 4, 4, 2, 2), ("dp", "z", "x", "core", "branch"))
    prompt = P("dp", ("z", "x", "core", "branch"), None)
    reply = P("dp", "branch", ("z", "x", "core"), None)
    return jax.shard_map(
        on_device,
        mesh=fine,
        in_specs=(prompt,) * 4
        + (reply,) * 4
        + (P(),) * 3
        + (P("dp", ("z", "x", "core", "branch")), P("dp", "branch")),
        out_specs=(prompt, reply, prompt, prompt, prompt, reply, reply, reply, P(), P(), P()),
        check_vma=False,
    )
```

time: 1800 us -> 198 us (0.11)
  waiting for transfers between devices: 1300 us -> 52.9 us
  matrix products: 179 us -> 0 us
  local copies, waits for them, and re-layouts: 134 us -> 7.1 us
  blocking collectives: 84.7 us -> 0 us
  Pallas kernels: 0 us -> 75.8 us
  other arithmetic: 68.1 us -> 4.13 us
  starting transfers between devices: 0.53 us -> 56 us
    unnamed x10 -> x0, waiting for transfers between devices: 755 us -> none
    reduce_scatter x2 -> x0, waiting for transfers between devices: 424 us -> none  [the longest x1 345 us: on_device(): lax.psum_scatter(value_buffer, ('ctx', 'branch'), scatter_dimension=0, ti...]
    dot_general x84 -> x0, matrix products: 179 us -> none  [the longest x24 54 us: score_block(): jnp.einsum('ngmd,kgd->gmnk', query_rows_all, key_block, preferred_element...]
    all_gather x4 -> x0, waiting for transfers between devices: 122 us -> none  [the longest x1 71.9 us: on_device(): lax.all_gather(prompt_key_rows, ('ctx', 'branch'), axis=0, tiled=True)]
    psum x2 -> x0, blocking collectives: 84.7 us -> none  [the longest x1 62.7 us: on_device(): lax.psum((jnp.sum(query_pre, axis=0), jnp.sum(prompt_key_unbiased, axis=0...]
    pallas_call x0 -> x7, Pallas kernels: none -> 75.8 us  [the longest x1 63.3 us: on_device(): call(attend_body, 16, [((2 * STRIPE, HD), bf16)] * 8 + [((1536, HD), bf16...]
    ppermute x0 -> x38, starting transfers between devices: none -> 56 us  [the longest x31 43.8 us: shift(): return lax.ppermute(v, axis, [(i, (i + s) % n) for i in range(n)])]
    ppermute x0 -> x38, waiting for transfers between devices: none -> 52.9 us  [the longest x31 34.5 us: shift(): return lax.ppermute(v, axis, [(i, (i + s) % n) for i in range(n)])]
  transfers between devices with their start and end apart: 8 -> 38, of which waited for: 7 -> 16; matrix products, arithmetic and copies ran while one was open for 7% -> 2% of each run, Pallas kernels for 0% -> 5%
where the time goes in v1:
time: 198 us
  Pallas kernels  75.8 us (38%)
  starting transfers between devices  56 us (28%)
  waiting for transfers between devices  52.9 us (27%)
  local copies, waits for them, and re-layouts  7.1 us (4%)
  other arithmetic  4.13 us (2%)
    pallas_call x1, Pallas kernels, on_device(): call(attend_body, 16, [((2 * STRIPE, HD), bf16)] * 8 + [((1536, HD), bf16...  63.3 us
    ppermute x31, starting transfers between devices, shift(): return lax.ppermute(v, axis, [(i, (i + s) % n) for i in range(n)])  43.8 us
    ppermute x31, waiting for transfers between devices, shift(): return lax.ppermute(v, axis, [(i, (i + s) % n) for i in range(n)])  34.5 us
    ppermute x7, waiting for transfers between devices, swap(): lax.ppermute(v, axis, [(i, i ^ bit) for i in range(lax.axis_size(axis))])  18.4 us
    ppermute x7, starting transfers between devices, swap(): lax.ppermute(v, axis, [(i, i ^ bit) for i in range(lax.axis_size(axis))])  12.2 us
  transfers between devices with their start and end apart: 38, of which 16 were waited for; matrix products, arithmetic and copies ran while one was open for 2% of the time, Pallas kernels for 5%

profile of v1, /device:TPU:0, one launch (start us, length us, event | category | flops | bytes accessed | tf_op | source)
XLA Modules:
  0.0 197.6 jit_solution(4461948391234907629)
XLA Ops:
  3.9 1.8 shard_map.249
  5.8 2.0 %collective-permute-start.3 = (bf16[272,128]{1,0:T(8,128)(2,1)}, bf16[272,128]{1,0:T(8,128)(2,1)S(1)}, u32[]{:S(2)}, u32[]{:S(2)}) collective-permute-start(bf16[272,128]{1,0:T(8,128)(2,1)} %get-tuple-element.53), channel_id=1, source_target_pairs={{0,16},{16,32},{32,48},{48,0},{1,17},{17,33},{33,49},{49,1},{2,18}... | collective-permute-start | bytes 208904 | tf_op jit(solution)/shard_map/ppermute | solution.py:416
  7.8 3.6 %collective-permute-start.4 = (bf16[272,128]{1,0:T(8,128)(2,1)}, bf16[272,128]{1,0:T(8,128)(2,1)S(1)}, u32[]{:S(2)}, u32[]{:S(2)}) collective-permute-start(bf16[272,128]{1,0:T(8,128)(2,1)} %get-tuple-element.54), channel_id=1, source_target_pairs={{0,32},{16,48},{32,0},{48,16},{1,33},{17,49},{33,1},{49,17},{2,34}... | collective-permute-start | bytes 208904 | tf_op jit(solution)/shard_map/ppermute | solution.py:416
  12.4 2.6 %collective-permute-done.4 = bf16[272,128]{1,0:T(8,128)(2,1)S(1)} collective-permute-done((bf16[272,128]{1,0:T(8,128)(2,1)}, bf16[272,128]{1,0:T(8,128)(2,1)S(1)}, u32[]{:S(2)}, u32[]{:S(2)}) %collective-permute-start.4) | collective-permute-done | bytes 69664 | tf_op jit(solution)/shard_map/ppermute | solution.py:416
  16.8 3.3 %collective-permute-start.6 = (bf16[576,128]{1,0:T(8,128)(2,1)S(1)}, bf16[576,128]{1,0:T(8,128)(2,1)S(1)}, u32[]{:S(2)}, u32[]{:S(2)}) collective-permute-start(bf16[576,128]{1,0:T(8,128)(2,1)S(1)} %bitcast.36), channel_id=1, source_target_pairs={{0,1},{1,0},{2,3},{3,2},{4,5},{5,4},{6,7},{7,6},{8,9},{9,8},{10,11... | collective-permute-start | bytes 442376 | tf_op jit(solution)/shard_map/ppermute | solution.py:416
  20.1 3.5 %collective-permute-done.6 = bf16[576,128]{1,0:T(8,128)(2,1)S(1)} collective-permute-done((bf16[576,128]{1,0:T(8,128)(2,1)S(1)}, bf16[576,128]{1,0:T(8,128)(2,1)S(1)}, u32[]{:S(2)}, u32[]{:S(2)}) %collective-permute-start.6) | collective-permute-done | bytes 147488 | tf_op jit(solution)/shard_map/ppermute | solution.py:416
  23.6 2.8 %collective-permute-start.12 = (bf16[1664,128]{1,0:T(8,128)(2,1)S(1)}, bf16[1664,128]{1,0:T(8,128)(2,1)S(1)}, u32[]{:S(2)}, u32[]{:S(2)}) collective-permute-start(bf16[1664,128]{1,0:T(8,128)(2,1)S(1)} %pad_maximum_fusion.refs_4_), channel_id=1, source_target_pairs={{0,12},{4,0},{8,4},{12,8},{1,13},{5,1},{9,5},{13,9},{2,14},{6,2},{... | collective-permute-start | bytes 1277960 | tf_op jit(solution)/shard_map/ppermute | solution.py:416
  28.7 2.7 %shard_map.248 = (bf16[1280,128]{1,0:T(8,128)(2,1)}, bf16[1280,128]{1,0:T(8,128)(2,1)}, bf16[1280,128]{1,0:T(8,128)(2,1)}, bf16[1280,128]{1,0:T(8,128)(2,1)}) custom-call(s32[5]{0:T(128)} %stack.34.sc, bf16[64,2560]{1,0:T(8,128)(2,1)} %bitcast.32, bf16[64,2560]{1,0:T(8,128)(2,1)} %bitcast.33, bf16[64,2560]{1,0:T(8,128)(2,1)} %bitcast.34, ...), custom_call_target="tpu_custom_call" | custom-call | tf_op jit(solution)/shard_map/pallas_call | solution.py:434
  31.6 3.4 %collective-permute-start.1 = (bf16[1280,128]{1,0:T(8,128)(2,1)}, bf16[1280,128]{1,0:T(8,128)(2,1)S(1)}, u32[]{:S(2)}, u32[]{:S(2)}) collective-permute-start(bf16[1280,128]{1,0:T(8,128)(2,1)} %get-tuple-element.50), channel_id=1, source_target_pairs={{0,32},{16,48},{32,0},{48,16},{1,33},{17,49},{33,1},{49,17},{2,34}... | collective-permute-start | bytes 983048 | tf_op jit(solution)/shard_map/ppermute | solution.py:416
  35.0 7.8 %collective-permute-done.refs_1_ = bf16[1280,128]{1,0:T(8,128)(2,1)S(1)} collective-permute-done((bf16[1280,128]{1,0:T(8,128)(2,1)}, bf16[1280,128]{1,0:T(8,128)(2,1)S(1)}, u32[]{:S(2)}, u32[]{:S(2)}) %collective-permute-start) | collective-permute-done | bytes 327712 | tf_op jit(solution)/shard_map/ppermute | solution.py:416
  43.5 2.3 %collective-permute-done.8.refs_6_ = bf16[1664,128]{1,0:T(8,128)(2,1)S(1)} collective-permute-done((bf16[1664,128]{1,0:T(8,128)(2,1)S(1)}, bf16[1664,128]{1,0:T(8,128)(2,1)S(1)}, u32[]{:S(2)}, u32[]{:S(2)}) %collective-permute-start.8) | collective-permute-done | bytes 426016 | tf_op jit(solution)/shard_map/ppermute | solution.py:416
  46.3 1.8 collective-permute-start.2
  48.1 8.0 %collective-permute-done.2.refs_3_ = bf16[1280,128]{1,0:T(8,128)(2,1)S(1)} collective-permute-done((bf16[1280,128]{1,0:T(8,128)(2,1)}, bf16[1280,128]{1,0:T(8,128)(2,1)S(1)}, u32[]{:S(2)}, u32[]{:S(2)}) %collective-permute-start.2) | collective-permute-done | bytes 327712 | tf_op jit(solution)/shard_map/ppermute | solution.py:416
  57.4 63.3 %shard_map.250 = (bf16[640,128]{1,0:T(8,128)(2,1)}, bf16[640,128]{1,0:T(8,128)(2,1)}, bf16[640,128]{1,0:T(8,128)(2,1)}, bf16[640,128]{1,0:T(8,128)(2,1)}, bf16[6...) custom-call(s32[5]{0:T(128)} %stack.34.sc, ...), custom_call_target="tpu_custom_call" | custom-call | tf_op jit(solution)/shard_map/pallas_call | solution.py:446
  123.4 3.6 %collective-permute-done.32 = f32[8,128]{1,0:T(8,128)S(1)} collective-permute-done((f32[8,128]{1,0:T(8,128)S(1)}, f32[8,128]{1,0:T(8,128)S(1)}, u32[]{:S(2)}, u32[]{:S(2)}) %collective-permute-start.32) | collective-permute-done | bytes 4128 | tf_op jit(solution)/shard_map/ppermute | solution.py:420
  127.0 6.5 %collective-permute-start.33 = (f32[8,128]{1,0:T(8,128)S(1)}, f32[8,128]{1,0:T(8,128)S(1)}, u32[]{:S(2)}, u32[]{:S(2)}) collective-permute-start(f32[8,128]{1,0:T(8,128)S(1)} %add.50), channel_id=1, source_target_pairs={{0,8},{4,12},{8,0},{12,4},{1,9},{5,13},{9,1},{13,5},{2,10},{6,14},... | collective-permute-start | bytes 12296 | tf_op jit(solution)/shard_map/ppermute | solution.py:420
  135.1 3.1 %collective-permute-start.34 = (f32[8,128]{1,0:T(8,128)S(1)}, f32[8,128]{1,0:T(8,128)S(1)}, u32[]{:S(2)}, u32[]{:S(2)}) collective-permute-start(f32[8,128]{1,0:T(8,128)S(1)} %add.51), channel_id=1, source_target_pairs={{0,1},{1,0},{2,3},{3,2},{4,5},{5,4},{6,7},{7,6},{8,9},{9,8},{10,11... | collective-permute-start | bytes 12296 | tf_op jit(solution)/shard_map/ppermute | solution.py:420
  138.3 2.0 collective-permute-done.34
  145.9 4.2 %collective-permute-start.24 = (bf16[1536,128]{1,0:T(8,128)(2,1)S(1)}, bf16[1536,128]{1,0:T(8,128)(2,1)S(1)}, u32[]{:S(2)}, u32[]{:S(2)}) collective-permute-start(bf16[1536,128]{1,0:T(8,128)(2,1)S(1)} %add_convert_fusion.1), channel_id=1, source_target_pairs={{0,8},{4,12},{8,0},{12,4},{1,9},{5,13},{9,1},{13,5},{2,10},{6,14},... | collective-permute-start | bytes 1179656 | tf_op jit(solution)/shard_map/ppermute | solution.py:416
  152.3 3.4 %collective-permute-done.36 = f32[4,8,128]{2,1,0:T(8,128)S(1)} collective-permute-done((f32[4,8,128]{2,1,0:T(8,128)S(1)}, f32[4,8,128]{2,1,0:T(8,128)S(1)}, u32[]{:S(2)}, u32[]{:S(2)}) %collective-permute-start.36) | collective-permute-done | bytes 16416 | tf_op jit(solution)/shard_map/ppermute | solution.py:420
  155.7 3.3 %collective-permute-start.14 = (bf16[640,128]{1,0:T(8,128)(2,1)S(1)}, bf16[640,128]{1,0:T(8,128)(2,1)S(1)}, u32[]{:S(2)}, u32[]{:S(2)}) collective-permute-start(bf16[640,128]{1,0:T(8,128)(2,1)S(1)} %copy-done.33), channel_id=1, source_target_pairs={{0,48},{16,0},{32,16},{48,32},{1,49},{17,1},{33,17},{49,33},{2,50}... | collective-permute-start | bytes 491528 | tf_op jit(solution)/shard_map/ppermute | solution.py:416
  160.1 5.4 %collective-permute-done.24 = bf16[1536,128]{1,0:T(8,128)(2,1)S(1)} collective-permute-done((bf16[1536,128]{1,0:T(8,128)(2,1)S(1)}, bf16[1536,128]{1,0:T(8,128)(2,1)S(1)}, u32[]{:S(2)}, u32[]{:S(2)}) %collective-permute-start.24) | collective-permute-done | bytes 393248 | tf_op jit(solution)/shard_map/ppermute | solution.py:416
  165.4 3.5 %collective-permute-start.17 = (bf16[640,128]{1,0:T(8,128)(2,1)S(1)}, bf16[640,128]{1,0:T(8,128)(2,1)S(1)}, u32[]{:S(2)}, u32[]{:S(2)}) collective-permute-start(bf16[640,128]{1,0:T(8,128)(2,1)S(1)} %copy-done.30), channel_id=1, source_target_pairs={{0,48},{16,0},{32,16},{48,32},{1,49},{17,1},{33,17},{49,33},{2,50}... | collective-permute-start | bytes 491528 | tf_op jit(solution)/shard_map/ppermute | solution.py:416
  169.2 5.0 %collective-permute-done.37 = f32[4,8,128]{2,1,0:T(8,128)S(1)} collective-permute-done((f32[4,8,128]{2,1,0:T(8,128)S(1)}, f32[4,8,128]{2,1,0:T(8,128)S(1)}, u32[]{:S(2)}, u32[]{:S(2)}) %collective-permute-start.37) | collective-permute-done | bytes 16416 | tf_op jit(solution)/shard_map/ppermute | solution.py:420
  174.2 2.9 %collective-permute-start.27 = (bf16[512,128]{1,0:T(8,128)(2,1)S(1)}, bf16[512,128]{1,0:T(8,128)(2,1)S(1)}, u32[]{:S(2)}, u32[]{:S(2)}) collective-permute-start(bf16[512,128]{1,0:T(8,128)(2,1)S(1)} %slice.27), channel_id=1, source_target_pairs={{0,1},{1,0},{2,3},{3,2},{4,5},{5,4},{6,7},{7,6},{8,9},{9,8},{10,11... | collective-permute-start | bytes 393224 | tf_op jit(solution)/shard_map/ppermute | solution.py:416
  177.2 3.5 %collective-permute-done.27.far = bf16[512,128]{1,0:T(8,128)(2,1)S(1)} collective-permute-done((bf16[512,128]{1,0:T(8,128)(2,1)S(1)}, bf16[512,128]{1,0:T(8,128)(2,1)S(1)}, u32[]{:S(2)}, u32[]{:S(2)}) %collective-permute-start.27) | collective-permute-done | bytes 131104 | tf_op jit(solution)/shard_map/ppermute | solution.py:416
  181.3 2.0 %shard_map.253 = (bf16[256,128]{1,0:T(8,128)(2,1)}, bf16[256,128]{1,0:T(8,128)(2,1)}, bf16[256,128]{1,0:T(8,128)(2,1)}, bf16[256,128]{1,0:T(8,128)(2,1)}) custom-call(s32[5]{0:T(128)} %stack.34.sc, f32[1536,128]{1,0:T(8,128)} %copy-done, bf16[512,128]{1,0:T(8,128)(2,1)} %copy-done.21, f32[96,128]{1,0:T(8,128)} %constant.25.clone.t0.refs_12_, ...), custom_call_target="tpu_custom_call" | custom-call | tf_op jit(solution)/shard_map/pallas_call | solution.py:470
  184.0 2.3 %collective-permute-start.28 = (bf16[256,128]{1,0:T(8,128)(2,1)}, bf16[256,128]{1,0:T(8,128)(2,1)S(1)}, u32[]{:S(2)}, u32[]{:S(2)}) collective-permute-start(bf16[256,128]{1,0:T(8,128)(2,1)} %get-tuple-element.76), channel_id=1, source_target_pairs={{0,16},{16,32},{32,48},{48,0},{1,17},{17,33},{33,49},{49,1},{2,18}... | collective-permute-start | bytes 196616 | tf_op jit(solution)/shard_map/ppermute | solution.py:416
  186.3 1.9 collective-permute-start.29
  190.3 2.1 %shard_map.251 = (bf16[64,2560]{1,0:T(8,128)(2,1)}, bf16[64,2560]{1,0:T(8,128)(2,1)}) custom-call(s32[5]{0:T(128)} %stack.34.sc, bf16[640,128]{1,0:T(8,128)(2,1)} %get-tuple-element.56.refs_0_, bf16[640,128]{1,0:T(8,128)(2,1)} %copy-done.15, bf16[640,128]{1,0:T(8,128)(2,1)} %copy-done.16, bf16[640,128]{1,0:T(8,128)(2,1)} %copy-done.18), custom_call_target="tpu_custom_call" | custom-call | tf_op jit(solution)/shard_map/pallas_call | solution.py:475
  193.1 2.1 %shard_map.252 = (bf16[64,2560]{1,0:T(8,128)(2,1)}, bf16[64,2560]{1,0:T(8,128)(2,1)}) custom-call(s32[5]{0:T(128)} %stack.34.sc, bf16[640,128]{1,0:T(8,128)(2,1)} %get-tuple-element.62.refs_0_, bf16[640,128]{1,0:T(8,128)(2,1)} %copy-done.17, bf16[640,128]{1,0:T(8,128)(2,1)} %copy-done.19, bf16[640,128]{1,0:T(8,128)(2,1)} %copy-done.20), custom_call_target="tpu_custom_call" | custom-call | tf_op jit(solution)/shard_map/pallas_call | solution.py:476
  196.0 1.7 shard_map.254
  (145 shorter events, 28.7 us)
Async XLA Ops:
  5.8 6.6 %collective-permute-start.3 = (bf16[272,128]{1,0:T(8,128)(2,1)}, bf16[272,128]{1,0:T(8,128)(2,1)S(1)}, u32[]{:S(2)}, u32[]{:S(2)}) collective-permute-start(bf16[272,128]{1,0:T(8,128)(2,1)} %get-tuple-element.53), channel_id=1, source_target_pairs={{0,16},{16,32},{32,48},{48,0},{1,17},{17,33},{33,49},{49,1},{2,18}... | collective-permute-start | bytes 208904 | tf_op jit(solution)/shard_map/ppermute | solution.py:416
  7.8 7.2 %collective-permute-start.4 = (bf16[272,128]{1,0:T(8,128)(2,1)}, bf16[272,128]{1,0:T(8,128)(2,1)S(1)}, u32[]{:S(2)}, u32[]{:S(2)}) collective-permute-start(bf16[272,128]{1,0:T(8,128)(2,1)} %get-tuple-element.54), channel_id=1, source_target_pairs={{0,32},{16,48},{32,0},{48,16},{1,33},{17,49},{33,1},{49,17},{2,34}... | collective-permute-start | bytes 208904 | tf_op jit(solution)/shard_map/ppermute | solution.py:416
  16.8 6.7 %collective-permute-start.6 = (bf16[576,128]{1,0:T(8,128)(2,1)S(1)}, bf16[576,128]{1,0:T(8,128)(2,1)S(1)}, u32[]{:S(2)}, u32[]{:S(2)}) collective-permute-start(bf16[576,128]{1,0:T(8,128)(2,1)S(1)} %bitcast.36), channel_id=1, source_target_pairs={{0,1},{1,0},{2,3},{3,2},{4,5},{5,4},{6,7},{7,6},{8,9},{9,8},{10,11... | collective-permute-start | bytes 442376 | tf_op jit(solution)/shard_map/ppermute | solution.py:416
  23.6 19.3 %collective-permute-start.12 = (bf16[1664,128]{1,0:T(8,128)(2,1)S(1)}, bf16[1664,128]{1,0:T(8,128)(2,1)S(1)}, u32[]{:S(2)}, u32[]{:S(2)}) collective-permute-start(bf16[1664,128]{1,0:T(8,128)(2,1)S(1)} %pad_maximum_fusion.refs_4_), channel_id=1, source_target_pairs={{0,12},{4,0},{8,4},{12,8},{1,13},{5,1},{9,5},{13,9},{2,14},{6,2},{... | collective-permute-start | bytes 1277960 | tf_op jit(solution)/shard_map/ppermute | solution.py:416
  26.4 17.0 %collective-permute-start.10 = (bf16[1664,128]{1,0:T(8,128)(2,1)S(1)}, bf16[1664,128]{1,0:T(8,128)(2,1)S(1)}, u32[]{:S(2)}, u32[]{:S(2)}) collective-permute-start(bf16[1664,128]{1,0:T(8,128)(2,1)S(1)} %pad_maximum_fusion.refs_4_), channel_id=1, source_target_pairs={{0,8},{4,12},{8,0},{12,4},{1,9},{5,13},{9,1},{13,5},{2,10},{6,14},... | collective-permute-start | bytes 1277960 | tf_op jit(solution)/shard_map/ppermute | solution.py:416
  27.2 18.5 %collective-permute-start.8 = (bf16[1664,128]{1,0:T(8,128)(2,1)S(1)}, bf16[1664,128]{1,0:T(8,128)(2,1)S(1)}, u32[]{:S(2)}, u32[]{:S(2)}) collective-permute-start(bf16[1664,128]{1,0:T(8,128)(2,1)S(1)} %pad_maximum_fusion.refs_4_), channel_id=1, source_target_pairs={{0,4},{4,8},{8,12},{12,0},{1,5},{5,9},{9,13},{13,1},{2,6},{6,10},{... | collective-permute-start | bytes 1277960 | tf_op jit(solution)/shard_map/ppermute | solution.py:416
  31.4 11.5 %collective-permute-start = (bf16[1280,128]{1,0:T(8,128)(2,1)}, bf16[1280,128]{1,0:T(8,128)(2,1)S(1)}, u32[]{:S(2)}, u32[]{:S(2)}) collective-permute-start(bf16[1280,128]{1,0:T(8,128)(2,1)} %get-tuple-element.49), channel_id=1, source_target_pairs={{0,16},{16,32},{32,48},{48,0},{1,17},{17,33},{33,49},{49,1},{2,18}... | collective-permute-start | bytes 983048 | tf_op jit(solution)/shard_map/ppermute | solution.py:416
  31.6 14.7 %collective-permute-start.1 = (bf16[1280,128]{1,0:T(8,128)(2,1)}, bf16[1280,128]{1,0:T(8,128)(2,1)S(1)}, u32[]{:S(2)}, u32[]{:S(2)}) collective-permute-start(bf16[1280,128]{1,0:T(8,128)(2,1)} %get-tuple-element.50), channel_id=1, source_target_pairs={{0,32},{16,48},{32,0},{48,16},{1,33},{17,49},{33,1},{49,17},{2,34}... | collective-permute-start | bytes 983048 | tf_op jit(solution)/shard_map/ppermute | solution.py:416
  42.8 13.3 %collective-permute-start.7 = (bf16[1664,128]{1,0:T(8,128)(2,1)S(1)}, bf16[1664,128]{1,0:T(8,128)(2,1)S(1)}, u32[]{:S(2)}, u32[]{:S(2)}) collective-permute-start(bf16[1664,128]{1,0:T(8,128)(2,1)S(1)} %pad_maximum_fusion.refs_4_), channel_id=1, source_target_pairs={{0,2},{2,0},{1,3},{3,1},{4,6},{6,4},{5,7},{7,5},{8,10},{10,8},{9,1... | collective-permute-start | bytes 1277960 | tf_op jit(solution)/shard_map/ppermute | solution.py:416
  42.9 13.2 %collective-permute-start.13 = (bf16[1664,128]{1,0:T(8,128)(2,1)S(1)}, bf16[1664,128]{1,0:T(8,128)(2,1)S(1)}, u32[]{:S(2)}, u32[]{:S(2)}) collective-permute-start(bf16[1664,128]{1,0:T(8,128)(2,1)S(1)} %collective-permute-done.12.refs_10_), channel_id=1, source_target_pairs={{0,2},{2,0},{1,3},{3,1},{4,6},{6,4},{5,7},{7,5},{8,10},{10,8},{9,1... | collective-permute-start | bytes 1277960 | tf_op jit(solution)/shard_map/ppermute | solution.py:416
  43.4 12.8 %collective-permute-start.11 = (bf16[1664,128]{1,0:T(8,128)(2,1)S(1)}, bf16[1664,128]{1,0:T(8,128)(2,1)S(1)}, u32[]{:S(2)}, u32[]{:S(2)}) collective-permute-start(bf16[1664,128]{1,0:T(8,128)(2,1)S(1)} %collective-permute-done.10.refs_8_), channel_id=1, source_target_pairs={{0,2},{2,0},{1,3},{3,1},{4,6},{6,4},{5,7},{7,5},{8,10},{10,8},{9,1... | collective-permute-start | bytes 1277960 | tf_op jit(solution)/shard_map/ppermute | solution.py:416
  45.7 10.4 %collective-permute-start.9 = (bf16[1664,128]{1,0:T(8,128)(2,1)S(1)}, bf16[1664,128]{1,0:T(8,128)(2,1)S(1)}, u32[]{:S(2)}, u32[]{:S(2)}) collective-permute-start(bf16[1664,128]{1,0:T(8,128)(2,1)S(1)} %collective-permute-done.8.refs_6_), channel_id=1, source_target_pairs={{0,2},{2,0},{1,3},{3,1},{4,6},{6,4},{5,7},{7,5},{8,10},{10,8},{9,1... | collective-permute-start | bytes 1277960 | tf_op jit(solution)/shard_map/ppermute | solution.py:416
  46.3 9.7 %collective-permute-start.2 = (bf16[1280,128]{1,0:T(8,128)(2,1)}, bf16[1280,128]{1,0:T(8,128)(2,1)S(1)}, u32[]{:S(2)}, u32[]{:S(2)}) collective-permute-start(bf16[1280,128]{1,0:T(8,128)(2,1)} %get-tuple-element.51), channel_id=1, source_target_pairs={{0,48},{16,0},{32,16},{48,32},{1,49},{17,1},{33,17},{49,33},{2,50}... | collective-permute-start | bytes 983048 | tf_op jit(solution)/shard_map/ppermute | solution.py:416
  120.7 23.2 %collective-permute-start.21 = (bf16[1536,128]{1,0:T(8,128)(2,1)}, bf16[1536,128]{1,0:T(8,128)(2,1)S(1)}, u32[]{:S(2)}, u32[]{:S(2)}) collective-permute-start(bf16[1536,128]{1,0:T(8,128)(2,1)} %get-tuple-element.70), channel_id=1, source_target_pairs={{0,2},{2,0},{1,3},{3,1},{4,6},{6,4},{5,7},{7,5},{8,10},{10,8},{9,1... | collective-permute-start | bytes 1179656 | tf_op jit(solution)/shard_map/ppermute | solution.py:416
  127.0 8.1 %collective-permute-start.33 = (f32[8,128]{1,0:T(8,128)S(1)}, f32[8,128]{1,0:T(8,128)S(1)}, u32[]{:S(2)}, u32[]{:S(2)}) collective-permute-start(f32[8,128]{1,0:T(8,128)S(1)} %add.50), channel_id=1, source_target_pairs={{0,8},{4,12},{8,0},{12,4},{1,9},{5,13},{9,1},{13,5},{2,10},{6,14},... | collective-permute-start | bytes 12296 | tf_op jit(solution)/shard_map/ppermute | solution.py:420
  135.1 5.1 %collective-permute-start.34 = (f32[8,128]{1,0:T(8,128)S(1)}, f32[8,128]{1,0:T(8,128)S(1)}, u32[]{:S(2)}, u32[]{:S(2)}) collective-permute-start(f32[8,128]{1,0:T(8,128)S(1)} %add.51), channel_id=1, source_target_pairs={{0,1},{1,0},{2,3},{3,2},{4,5},{5,4},{6,7},{7,6},{8,9},{9,8},{10,11... | collective-permute-start | bytes 12296 | tf_op jit(solution)/shard_map/ppermute | solution.py:420
  141.8 17.3 %collective-permute-start.20 = (bf16[1536,128]{1,0:T(8,128)(2,1)}, bf16[1536,128]{1,0:T(8,128)(2,1)S(1)}, u32[]{:S(2)}, u32[]{:S(2)}) collective-permute-start(bf16[1536,128]{1,0:T(8,128)(2,1)} %get-tuple-element.68), channel_id=1, source_target_pairs={{0,2},{2,0},{1,3},{3,1},{4,6},{6,4},{5,7},{7,5},{8,10},{10,8},{9,1... | collective-permute-start | bytes 1179656 | tf_op jit(solution)/shard_map/ppermute | solution.py:416
  142.3 7.9 %collective-permute-start.25 = (bf16[1536,128]{1,0:T(8,128)(2,1)}, bf16[1536,128]{1,0:T(8,128)(2,1)S(1)}, u32[]{:S(2)}, u32[]{:S(2)}) collective-permute-start(bf16[1536,128]{1,0:T(8,128)(2,1)} %get-tuple-element.74), channel_id=1, source_target_pairs={{0,2},{2,0},{1,3},{3,1},{4,6},{6,4},{5,7},{7,5},{8,10},{10,8},{9,1... | collective-permute-start | bytes 1179656 | tf_op jit(solution)/shard_map/ppermute | solution.py:416
  145.2 14.0 %collective-permute-start.22 = (bf16[1536,128]{1,0:T(8,128)(2,1)S(1)}, bf16[1536,128]{1,0:T(8,128)(2,1)S(1)}, u32[]{:S(2)}, u32[]{:S(2)}) collective-permute-start(bf16[1536,128]{1,0:T(8,128)(2,1)S(1)} %add_convert_fusion.2), channel_id=1, source_target_pairs={{0,4},{4,8},{8,12},{12,0},{1,5},{5,9},{9,13},{13,1},{2,6},{6,10},{... | collective-permute-start | bytes 1179656 | tf_op jit(solution)/shard_map/ppermute | solution.py:416
  145.9 19.5 %collective-permute-start.24 = (bf16[1536,128]{1,0:T(8,128)(2,1)S(1)}, bf16[1536,128]{1,0:T(8,128)(2,1)S(1)}, u32[]{:S(2)}, u32[]{:S(2)}) collective-permute-start(bf16[1536,128]{1,0:T(8,128)(2,1)S(1)} %add_convert_fusion.1), channel_id=1, source_target_pairs={{0,8},{4,12},{8,0},{12,4},{1,9},{5,13},{9,1},{13,5},{2,10},{6,14},... | collective-permute-start | bytes 1179656 | tf_op jit(solution)/shard_map/ppermute | solution.py:416
  150.3 18.6 %collective-permute-start.26 = (bf16[1536,128]{1,0:T(8,128)(2,1)S(1)}, bf16[1536,128]{1,0:T(8,128)(2,1)S(1)}, u32[]{:S(2)}, u32[]{:S(2)}) collective-permute-start(bf16[1536,128]{1,0:T(8,128)(2,1)S(1)} %add_convert_fusion), channel_id=1, source_target_pairs={{0,12},{4,0},{8,4},{12,8},{1,13},{5,1},{9,5},{13,9},{2,14},{6,2},{... | collective-permute-start | bytes 1179656 | tf_op jit(solution)/shard_map/ppermute | solution.py:416
  155.7 27.6 %collective-permute-start.14 = (bf16[640,128]{1,0:T(8,128)(2,1)S(1)}, bf16[640,128]{1,0:T(8,128)(2,1)S(1)}, u32[]{:S(2)}, u32[]{:S(2)}) collective-permute-start(bf16[640,128]{1,0:T(8,128)(2,1)S(1)} %copy-done.33), channel_id=1, source_target_pairs={{0,48},{16,0},{32,16},{48,32},{1,49},{17,1},{33,17},{49,33},{2,50}... | collective-permute-start | bytes 491528 | tf_op jit(solution)/shard_map/ppermute | solution.py:416
  159.1 24.9 %collective-permute-start.15 = (bf16[640,128]{1,0:T(8,128)(2,1)S(1)}, bf16[640,128]{1,0:T(8,128)(2,1)S(1)}, u32[]{:S(2)}, u32[]{:S(2)}) collective-permute-start(bf16[640,128]{1,0:T(8,128)(2,1)S(1)} %copy-done.32), channel_id=1, source_target_pairs={{0,32},{16,48},{32,0},{48,16},{1,33},{17,49},{33,1},{49,17},{2,34}... | collective-permute-start | bytes 491528 | tf_op jit(solution)/shard_map/ppermute | solution.py:416
  159.2 27.1 %collective-permute-start.16 = (bf16[640,128]{1,0:T(8,128)(2,1)S(1)}, bf16[640,128]{1,0:T(8,128)(2,1)S(1)}, u32[]{:S(2)}, u32[]{:S(2)}) collective-permute-start(bf16[640,128]{1,0:T(8,128)(2,1)S(1)} %copy-done.31), channel_id=1, source_target_pairs={{0,16},{16,32},{32,48},{48,0},{1,17},{17,33},{33,49},{49,1},{2,18}... | collective-permute-start | bytes 491528 | tf_op jit(solution)/shard_map/ppermute | solution.py:416
  165.4 22.7 %collective-permute-start.17 = (bf16[640,128]{1,0:T(8,128)(2,1)S(1)}, bf16[640,128]{1,0:T(8,128)(2,1)S(1)}, u32[]{:S(2)}, u32[]{:S(2)}) collective-permute-start(bf16[640,128]{1,0:T(8,128)(2,1)S(1)} %copy-done.30), channel_id=1, source_target_pairs={{0,48},{16,0},{32,16},{48,32},{1,49},{17,1},{33,17},{49,33},{2,50}... | collective-permute-start | bytes 491528 | tf_op jit(solution)/shard_map/ppermute | solution.py:416
  168.9 5.2 %collective-permute-start.37 = (f32[4,8,128]{2,1,0:T(8,128)S(1)}, f32[4,8,128]{2,1,0:T(8,128)S(1)}, u32[]{:S(2)}, u32[]{:S(2)}) collective-permute-start(f32[4,8,128]{2,1,0:T(8,128)S(1)} %fusion), channel_id=1, source_target_pairs={{0,32},{16,48},{32,0},{48,16},{1,33},{17,49},{33,1},{49,17},{2,34}... | collective-permute-start | bytes 49160 | tf_op jit(solution)/shard_map/ppermute | solution.py:420
  174.2 6.5 %collective-permute-start.27 = (bf16[512,128]{1,0:T(8,128)(2,1)S(1)}, bf16[512,128]{1,0:T(8,128)(2,1)S(1)}, u32[]{:S(2)}, u32[]{:S(2)}) collective-permute-start(bf16[512,128]{1,0:T(8,128)(2,1)S(1)} %slice.27), channel_id=1, source_target_pairs={{0,1},{1,0},{2,3},{3,2},{4,5},{5,4},{6,7},{7,6},{8,9},{9,8},{10,11... | collective-permute-start | bytes 393224 | tf_op jit(solution)/shard_map/ppermute | solution.py:416
  180.6 11.7 %collective-permute-start.18 = (bf16[640,128]{1,0:T(8,128)(2,1)S(1)}, bf16[640,128]{1,0:T(8,128)(2,1)S(1)}, u32[]{:S(2)}, u32[]{:S(2)}) collective-permute-start(bf16[640,128]{1,0:T(8,128)(2,1)S(1)} %copy-done.29), channel_id=1, source_target_pairs={{0,32},{16,48},{32,0},{48,16},{1,33},{17,49},{33,1},{49,17},{2,34}... | collective-permute-start | bytes 491528 | tf_op jit(solution)/shard_map/ppermute | solution.py:416
  183.4 9.0 %collective-permute-start.19 = (bf16[640,128]{1,0:T(8,128)(2,1)S(1)}, bf16[640,128]{1,0:T(8,128)(2,1)S(1)}, u32[]{:S(2)}, u32[]{:S(2)}) collective-permute-start(bf16[640,128]{1,0:T(8,128)(2,1)S(1)} %copy-done.28), channel_id=1, source_target_pairs={{0,16},{16,32},{32,48},{48,0},{1,17},{17,33},{33,49},{49,1},{2,18}... | collective-permute-start | bytes 491528 | tf_op jit(solution)/shard_map/ppermute | solution.py:416
  184.0 11.3 %collective-permute-start.28 = (bf16[256,128]{1,0:T(8,128)(2,1)}, bf16[256,128]{1,0:T(8,128)(2,1)S(1)}, u32[]{:S(2)}, u32[]{:S(2)}) collective-permute-start(bf16[256,128]{1,0:T(8,128)(2,1)} %get-tuple-element.76), channel_id=1, source_target_pairs={{0,16},{16,32},{32,48},{48,0},{1,17},{17,33},{33,49},{49,1},{2,18}... | collective-permute-start | bytes 196616 | tf_op jit(solution)/shard_map/ppermute | solution.py:416
  186.3 9.0 %collective-permute-start.29 = (bf16[256,128]{1,0:T(8,128)(2,1)}, bf16[256,128]{1,0:T(8,128)(2,1)S(1)}, u32[]{:S(2)}, u32[]{:S(2)}) collective-permute-start(bf16[256,128]{1,0:T(8,128)(2,1)} %get-tuple-element.77), channel_id=1, source_target_pairs={{0,32},{16,48},{32,0},{48,16},{1,33},{17,49},{33,1},{49,17},{2,34}... | collective-permute-start | bytes 196616 | tf_op jit(solution)/shard_map/ppermute | solution.py:416
  188.1 7.1 %collective-permute-start.30 = (bf16[256,128]{1,0:T(8,128)(2,1)}, bf16[256,128]{1,0:T(8,128)(2,1)S(1)}, u32[]{:S(2)}, u32[]{:S(2)}) collective-permute-start(bf16[256,128]{1,0:T(8,128)(2,1)} %get-tuple-element.78), channel_id=1, source_target_pairs={{0,48},{16,0},{32,16},{48,32},{1,49},{17,1},{33,17},{49,33},{2,50}... | collective-permute-start | bytes 196616 | tf_op jit(solution)/shard_map/ppermute | solution.py:416
  (41 other events, 227.1 us)

commit v2 on v1

v2 whole, which is shorter than its diff:
```python
import functools

import jax
import jax.numpy as jnp
import numpy as np
from jax import lax
from jax.experimental import pallas as pl
from jax.experimental.pallas import tpu as pltpu
from jax.sharding import Mesh
from jax.sharding import PartitionSpec as P

HEADS = 4
GROUP = 5
HD = 128
ROWS = 64
STRIPE = GROUP * ROWS
PROMPT = 4096
REPLY = 2048
BLOCK = 512
SCALE = HD**-0.5
LOG2 = float(SCALE * np.log2(np.e))
LOW = -1e30
MASKED = -3e38
KV = 2 * ROWS
PKV = KV + 16
OWN = PKV + KV
PIECE = 4 * OWN + 4 * PKV
TERMS = 1536

bf16 = jnp.bfloat16
f32 = jnp.float32
NT = (((1,), (1,)), ((), ()))
NN = (((1,), (0,)), ((), ()))
TN = (((0,), (0,)), ((), ()))


def dot(a, b, dims):
    return lax.dot_general(a, b, dims, preferred_element_type=f32)


def angle_tables():
    frequency = 1000000.0 ** (-(np.arange(HD // 2) * 2.0 / HD))
    frequency = np.concatenate([frequency, frequency])
    sign = np.where(np.arange(HD) < HD // 2, -1.0, 1.0)
    coarse = np.arange((PROMPT + REPLY) // ROWS)[:, None] * ROWS * frequency
    fine = np.arange(ROWS)[:, None] * frequency
    return [
        jnp.asarray(t.astype(np.float32))
        for t in (np.cos(coarse), np.sin(coarse) * sign, np.cos(fine), np.sin(fine) * sign)
    ]


def turn(tables, block):
    coarse_cos, coarse_sin, fine_cos, fine_sin = tables
    ca, sa = coarse_cos[pl.ds(block, 1), :], coarse_sin[pl.ds(block, 1), :]
    cb, sb = fine_cos[...], fine_sin[...]
    return ca * cb - sa * sb, sa * cb + ca * sb


def rotate(x, cosine, sine):
    return x * cosine + pltpu.roll(x, HD // 2, 1) * sine


def unrotate(x, cosine, sine):
    return x * cosine - pltpu.roll(x, HD // 2, 1) * sine


def prompt_block(sc, z):
    return z * 16 + sc[1] * 4 + sc[2] * 2 + sc[3]


def reply_block(sc, z):
    return z * 8 + sc[1] * 2 + sc[2]


def part(i):
    return pl.ds(pl.multiple_of(i, ROWS), ROWS)


def lanes(i):
    return pl.ds(pl.multiple_of(i * HD, HD), HD)


def prepare_kv_body(sc, pk, pv, rk, rv, bias, seg, t0, t1, t2, t3, *outs):
    tables = (t0, t1, t2, t3)
    z = sc[0]
    prompt_turn = turn(tables, prompt_block(sc, z))
    reply_turn = turn(tables, PROMPT // ROWS + reply_block(sc, z))
    ids = jnp.concatenate([seg[...], seg[...]], axis=1)
    row = lax.broadcasted_iota(jnp.int32, (16, HD), 0)
    lane = lax.broadcasted_iota(jnp.int32, (16, HD), 1)
    note = jnp.zeros((16, HD), f32)
    for s in range(1, HEADS):
        below = jnp.sum((ids < s).astype(f32), axis=1, keepdims=True) * 0.5
        note = jnp.where((row == 0) & (lane == s), below, note)
    note = jnp.where(row == 1, ids.astype(f32), note).astype(bf16)
    for s, out in enumerate(outs):
        h = lax.rem(z + s, HEADS)
        at = lanes(h)
        kb, vb = bias[:, lanes(20 + h)].astype(f32), bias[:, lanes(24 + h)].astype(f32)
        out[0:64, :] = rotate(pk[:, at].astype(f32) + kb, *prompt_turn).astype(bf16)
        out[64:128, :] = (pv[:, at].astype(f32) + vb).astype(bf16)
        out[128:144, :] = note
        out[144:208, :] = rotate(rk[:, at].astype(f32) + kb, *reply_turn).astype(bf16)
        out[208:272, :] = (rv[:, at].astype(f32) + vb).astype(bf16)


def prepare_q_body(sc, pq, pg, rq, rg, bias, t0, t1, t2, t3, *outs):
    tables = (t0, t1, t2, t3)
    z = sc[0]
    prompt_turn = turn(tables, prompt_block(sc, z))
    reply_turn = turn(tables, PROMPT // ROWS + reply_block(sc, z))
    place = reply_block(sc, z) * ROWS + lax.broadcasted_iota(jnp.int32, (ROWS, HD), 0)
    valid = place < sc[4]
    for s, out in enumerate(outs):
        h = lax.rem(z + s, HEADS) * GROUP
        for m in range(GROUP):
            at = lanes(h + m)
            qb = bias[:, at].astype(f32)
            o = m * ROWS
            out[o : o + 64, :] = rotate(pq[:, at].astype(f32) + qb, *prompt_turn).astype(bf16)
            o += STRIPE
            out[o : o + 64, :] = pg[:, at]
            o += STRIPE
            out[o : o + 64, :] = rotate(rq[:, at].astype(f32) + qb, *reply_turn).astype(bf16)
            o += STRIPE
            out[o : o + 64, :] = jnp.where(valid, rg[:, at].astype(f32), 0.0).astype(bf16)


def granule(s, zz, sub=0):
    return s * 1024 + zz * 256 + sub * ROWS


def x_of(sc, s):
    return lax.rem(sc[1] + 4 - s, 4)


def prompt_rows(sc, i):
    pair = [granule(lax.rem(sc[1] + 4 - lax.rem(i, 2) * 2 - n, 4), i // 2) for n in range(2)]
    return [pl.ds(pl.multiple_of(row, 256), 256) for row in pair]


def prompt_block_of(sc, i, count, pk, pv, start, place):
    rows = prompt_rows(sc, jnp.minimum(i, PROMPT // BLOCK - 1))
    key = i * BLOCK + lax.broadcasted_iota(jnp.int32, (BLOCK, STRIPE), 0)
    k, v = [jnp.concatenate([ref[at, :] for at in rows], axis=0) for ref in (pk, pv)]
    return k, v, (key >= start) & (key <= jnp.where(i < count, place, -1))


def prompt_limits(sc, j, start):
    lane = lax.broadcasted_iota(jnp.int32, start.shape, 1)
    first = jnp.sum(jnp.where(lane == 0, start, 0))
    return first // BLOCK, (prompt_block(sc, j) * ROWS + ROWS - 1) // BLOCK + 1


def reply_places(sc):
    column = lax.broadcasted_iota(jnp.int32, (1, 4 * STRIPE), 1)
    stripe = sum((column >= j * STRIPE).astype(jnp.int32) for j in range(1, 4))
    return reply_block(sc, stripe) * ROWS + jnp.bitwise_and(column, ROWS - 1)


def reply_seen(sc, key_at, place):
    key = key_at + lax.broadcasted_iota(jnp.int32, (BLOCK, place.shape[1]), 0)
    return (key < sc[4]) & (key <= place)


def prompt_places(sc, j):
    lane = lax.broadcasted_iota(jnp.int32, (1, STRIPE), 1)
    return prompt_block(sc, j) * ROWS + jnp.bitwise_and(lane, ROWS - 1)


def online(state, q, k, v, seen):
    top, total, acc = state
    scores = dot(k, q, NT) * LOG2
    if seen is not None:
        scores = jnp.where(seen, scores, MASKED)
    raised = jnp.maximum(top, jnp.max(scores, axis=0, keepdims=True))
    shrink = jnp.exp2(top - raised)
    p = jnp.exp2(scores - raised)
    total = total * shrink + jnp.sum(p, axis=0, keepdims=True)
    return raised, total, acc * shrink + dot(v, p.astype(bf16), TN)


def empty(n):
    return jnp.full((1, n), LOW, f32), jnp.zeros((1, n), f32), jnp.zeros((HD, n), f32)


def grads(q, g, lse, rd, k, v, seen):
    w = jnp.exp2(dot(k, q, NT) * LOG2 - lse)
    if seen is not None:
        w = jnp.where(seen, w, 0.0)
    ds = (w * (dot(v, g, NT) - rd)).astype(bf16)
    return dot(ds, q, NN), dot(w.astype(bf16), g, NN), dot(ds, k, TN)


def attend_body(sc, *refs):
    q_in, kv_in, tables = refs[0:4], refs[4:12], refs[12:16]
    back, keep, send = refs[16:20], refs[20], refs[21]
    (pq, pg, rq, rg, pk, pv, rk, rv, r_stat, p_stat, pdq, rdq, pdk, pdv, rdk, rdv,
     stat_m, stat_l, acc_r, p_out, r_out, note, bias) = refs[22:]
    z, x, core, b, length = sc[0], sc[1], sc[2], sc[3], sc[4]

    for s in range(4):
        at = pl.ds(pl.multiple_of(lax.rem(z + 4 - s, 4) * STRIPE, STRIPE), STRIPE)
        for i, ref in enumerate((pq, pg, rq, rg)):
            ref[at, :] = q_in[s][i * STRIPE : (i + 1) * STRIPE, :]
    counts = jnp.zeros((16, HD), f32)
    for s in range(4):
        xx = x_of(sc, s)
        for other in range(2):
            piece = kv_in[s * 2 + other]
            cc = core if other == 0 else 1 - core
            for t in range(4):
                zz = lax.rem(z + 4 - t, 4)
                to = part((zz * 8 + xx * 2 + cc) * ROWS)
                o = t * OWN + PKV
                rk[to, :] = piece[o : o + 64, :]
                rv[to, :] = piece[o + 64 : o + 128, :]
                for far in range(2):
                    bb = b if far == 0 else 1 - b
                    to = part(granule(s, zz, cc * 2 + bb))
                    o = t * OWN if far == 0 else 4 * OWN + t * PKV
                    pk[to, :] = piece[o : o + 64, :]
                    pv[to, :] = piece[o + 64 : o + 128, :]
                    told = piece[o + 128 : o + 144, :].astype(f32)
                    counts = counts + told
                    if s == 0 and other == 0 and far == 0:
                        note[pl.ds(zz, 1)] = told[None]

    lane = lax.broadcasted_iota(jnp.int32, (1, HD), 1)
    starts = [
        jnp.sum(jnp.where(lane == s, counts[0:1, :], 0.0)).astype(jnp.int32) for s in range(HEADS)
    ]

    reply_place = reply_places(sc)
    q_all = rq[...]

    def forward_reply(i, state):
        at = pl.ds(pl.multiple_of(i * BLOCK, BLOCK), BLOCK)
        return online(state, q_all, pk[at, :], pv[at, :], None)

    top, total, acc = lax.fori_loop(0, PROMPT // BLOCK, forward_reply, empty(4 * STRIPE))
    half = 2 * STRIPE
    for i in range(4):
        at = slice(i * BLOCK, (i + 1) * BLOCK)
        if i < 2:
            seen = reply_seen(sc, i * BLOCK, reply_place)
            top, total, acc = online((top, total, acc), q_all, rk[at, :], rv[at, :], seen)
            if i == 1:
                stat_m[0:1, :] = top
                stat_l[0:1, :] = total
                acc_r[...] = acc
                state = (top[:, half:], total[:, half:], acc[:, half:])
        else:
            seen = reply_seen(sc, i * BLOCK, reply_place[:, half:])
            state = online(state, rq[half:, :], rk[at, :], rv[at, :], seen)
    stat_m[0:1, half:] = state[0]
    stat_l[0:1, half:] = state[1]
    acc_r[:, half:] = state[2]
    total = stat_l[0:1, :]
    out = jnp.where(reply_place < length, acc_r[...] / total, 0.0).astype(bf16).astype(f32)
    r_stat[0:1, :] = stat_m[0:1, :] + jnp.log2(total)
    r_stat[1:2, :] = jnp.sum(out * rg[...].astype(f32).T, axis=0, keepdims=True)
    acc_r[...] = out
    r_out[...] = acc_r[...].T

    limits, seen_from, places = [], [], []
    for j in range(4):
        ids = note[j, 1:2, :].astype(jnp.int32)
        start = jnp.zeros((1, HD), jnp.int32)
        for s in range(1, HEADS):
            start = jnp.where(ids == s, starts[s], start)
        limits.append(prompt_limits(sc, j, start))
        seen_from.append(jnp.concatenate([start, start, start[:, :64]], axis=1))
        places.append(prompt_places(sc, j))
    stripes = [slice(j * STRIPE, (j + 1) * STRIPE) for j in range(4)]
    for pair in ((0, 1), (2, 3)):

        def forward_prompt(i, states, pair=pair):
            out = []
            for j, state in zip(pair, states):
                low, high = limits[j]
                k, v, seen = prompt_block_of(
                    sc, low + i, high, pk, pv, seen_from[j], places[j]
                )
                out.append(online(state, pq[stripes[j], :], k, v, seen))
            return tuple(out)

        steps = jnp.maximum(*[limits[j][1] - limits[j][0] for j in pair])
        states = lax.fori_loop(0, steps, forward_prompt, (empty(STRIPE),) * 2)
        for j, (top, total, acc) in zip(pair, states):
            out = (acc / total).astype(bf16).astype(f32)
            p_stat[j, 0:1, :] = top + jnp.log2(total)
            p_stat[j, 1:2, :] = jnp.sum(
                out * pg[stripes[j], :].astype(f32).T, axis=0, keepdims=True
            )
            p_out[stripes[j], :] = out.T
    for s in range(4):
        at = pl.ds(pl.multiple_of(lax.rem(z + 4 - s, 4) * STRIPE, STRIPE), STRIPE)
        back[s][0:STRIPE, :] = p_out[at, :].astype(bf16)
        back[s][STRIPE : 2 * STRIPE, :] = r_out[at, :].astype(bf16)

    pdq[...] = jnp.zeros_like(pdq)
    rdq[...] = jnp.zeros_like(rdq)
    bias[...] = jnp.zeros_like(bias)

    def backward_reply(i, carry):
        at = pl.ds(pl.multiple_of(i * BLOCK, BLOCK), BLOCK)
        dk, dv, dq = grads(
            rq[...], rg[...], r_stat[0:1, :], r_stat[1:2, :], pk[at, :], pv[at, :], None
        )
        pdk[at, :] = dk
        pdv[at, :] = dv
        rdq[...] += dq
        return carry

    lax.fori_loop(0, PROMPT // BLOCK, backward_reply, 0)
    for pair in ((0, 1), (2, 3)):

        def backward_prompt(i, carry, pair=pair):
            done = []
            for j in pair:
                low, high = limits[j]
                k, v, seen = prompt_block_of(sc, low + i, high, pk, pv, seen_from[j], places[j])
                done.append(
                    grads(pq[stripes[j], :], pg[stripes[j], :], p_stat[j, 0:1, :],
                          p_stat[j, 1:2, :], k, v, seen)
                )
            for j, (dk, dv, dq) in zip(pair, done):
                at = jnp.minimum(limits[j][0] + i, PROMPT // BLOCK - 1)
                for n, rows in enumerate(prompt_rows(sc, at)):
                    pdk[rows, :] += dk[n * 256 : (n + 1) * 256, :]
                    pdv[rows, :] += dv[n * 256 : (n + 1) * 256, :]
                pdq[stripes[j], :] += dq
            return carry

        steps = jnp.maximum(*[limits[j][1] - limits[j][0] for j in pair])
        lax.fori_loop(0, steps, backward_prompt, 0)
    for i in range(4):
        at = slice(i * BLOCK, (i + 1) * BLOCK)
        cols = slice(0 if i < 2 else half, 4 * STRIPE)
        dk, dv, dq = grads(
            rq[cols, :], rg[cols, :], r_stat[0:1, cols], r_stat[1:2, cols], rk[at, :], rv[at, :],
            reply_seen(sc, i * BLOCK, reply_place[:, cols]),
        )
        rdk[at, :] = dk
        rdv[at, :] = dv
        rdq[cols, :] += dq

    coarse_cos, coarse_sin, fine_cos, fine_sin = tables

    def add(keys, values, row, block, sums):
        key = keys[pl.ds(pl.multiple_of(row, 256), 256), :]
        value = values[pl.ds(pl.multiple_of(row, 256), 256), :]
        for i in range(4):
            cut = slice(i * ROWS, (i + 1) * ROWS)
            at = pl.ds(block + i, 1)
            sums = (
                sums[0] + key[cut] * coarse_cos[at, :],
                sums[1] + key[cut] * coarse_sin[at, :],
                sums[2] + value[cut],
            )
        return sums

    sums = (jnp.zeros((ROWS, HD), f32),) * 3
    for s in range(4):
        sums = lax.fori_loop(
            0, 4, lambda zz, c, s=s: add(pdk, pdv, granule(s, zz), zz * 16 + x_of(sc, s) * 4, c), sums
        )
    sums = lax.fori_loop(0, 8, lambda i, c: add(rdk, rdv, i * 256, PROMPT // ROWS + i * 4, c), sums)
    key_sum = unrotate(sums[0] + pltpu.roll(sums[1], HD // 2, 1), fine_cos[...], fine_sin[...])
    bias[5:6, :] = jnp.sum(key_sum, axis=0, keepdims=True) * SCALE
    bias[6:7, :] = jnp.sum(sums[2], axis=0, keepdims=True)
    for s in range(4):
        zz = lax.rem(z + 4 - s, 4)
        for i, (ref, block) in enumerate(
            ((pdq, prompt_block(sc, zz)), (rdq, PROMPT // ROWS + reply_block(sc, zz)))
        ):
            cosine, sine = turn(tables, block)
            for m in range(GROUP):
                at = part(zz * STRIPE + m * ROWS)
                pre = unrotate(ref[at, :] * SCALE, cosine, sine)
                bias[m : m + 1, :] += jnp.sum(pre, axis=0, keepdims=True)
                o = (2 + i) * STRIPE + m * ROWS
                back[s][o : o + ROWS, :] = pre.astype(bf16)

    for s in range(4):
        xx = lax.rem(x + s, 4)
        for t in range(4):
            zz = lax.rem(z + t, 4)
            for far in range(2):
                bb = b if far == 0 else 1 - b
                own = part(granule((4 - s) % 4, zz, core * 2 + bb))
                theirs = part(granule((4 - s) % 4, zz, (1 - core) * 2 + bb))
                o = s * TERMS + far * 512 + t * ROWS
                keep[o : o + 64, :] = (pdk[own, :] * SCALE).astype(bf16)
                keep[o + 256 : o + 320, :] = pdv[own, :].astype(bf16)
                send[o : o + 64, :] = (pdk[theirs, :] * SCALE).astype(bf16)
                send[o + 256 : o + 320, :] = pdv[theirs, :].astype(bf16)
            own = part((zz * 8 + xx * 2 + core) * ROWS)
            theirs = part((zz * 8 + xx * 2 + 1 - core) * ROWS)
            o = s * TERMS + 1024 + t * ROWS
            keep[o : o + 64, :] = (rdk[own, :] * SCALE).astype(bf16)
            keep[o + 256 : o + 320, :] = rdv[own, :].astype(bf16)
            send[o : o + 64, :] = (rdk[theirs, :] * SCALE).astype(bf16)
            send[o + 256 : o + 320, :] = rdv[theirs, :].astype(bf16)
    words = two_words(bias[...])
    keep[4 * TERMS :, :] = words
    send[4 * TERMS :, :] = words


def two_words(x):
    high = x.astype(bf16).astype(f32)
    return jnp.concatenate([high, x - high], axis=0).astype(bf16)


def one_word(x):
    x = x.astype(f32)
    return x[0:8] + x[8:16]


def along_core_body(keep, got, near, p1, p2, p3, bias):
    at = slice(4 * TERMS, 4 * TERMS + 16)
    bias[...] = one_word(keep[at, :]) + one_word(got[at, :])
    for i, out in enumerate((near, p1, p2, p3)):
        at = slice(i * TERMS, (i + 1) * TERMS)
        out[...] = (keep[at, :].astype(f32) + got[at, :].astype(f32)).astype(out.dtype)


def along_x_body(after, own, r1, r2, r3, b0, b1, b2, b3, p_own, r_own, p_far, bias):
    total = own[...] + (r1[...].astype(f32) + r2[...].astype(f32) + r3[...].astype(f32))
    words = two_words((b0[...] + b2[...]) + (b1[...] + b3[...]))
    p_own[...] = total[0:512]
    r_own[...] = total[1024:1536]
    p_far[0:512, :] = total[512:1024].astype(bf16)
    p_far[512:528, :] = words
    bias[...] = one_word(words)


def settle_body(sc, p_own, r_own, p_far, b0, t0, t1, t2, t3, *outs):
    tables = (t0, t1, t2, t3)
    z = sc[0]
    words = two_words(b0[...] + one_word(p_far[512:528, :]))
    for t, out in enumerate(outs):
        zz = lax.rem(z + t, 4)
        o = t * ROWS
        key = p_own[o : o + 64, :] + p_far[o : o + 64, :].astype(f32)
        out[0:64, :] = unrotate(key, *turn(tables, prompt_block(sc, zz))).astype(bf16)
        value = p_own[o + 256 : o + 320, :] + p_far[o + 256 : o + 320, :].astype(f32)
        out[64:128, :] = value.astype(bf16)
        block = PROMPT // ROWS + reply_block(sc, zz)
        out[128:192, :] = unrotate(r_own[o : o + 64, :], *turn(tables, block)).astype(bf16)
        out[192:256, :] = r_own[o + 256 : o + 320, :].astype(bf16)
        out[256:272, :] = words


def finish_body(sc, *refs):
    pieces, outs, (qsum, ksum, vsum) = refs[0:4], refs[4:8], refs[8:]
    z = sc[0]
    for t, piece in enumerate(pieces):
        h = lax.rem(z + 4 - t, 4)
        for i, out in enumerate(outs):
            out[:, lanes(h)] = piece[i * ROWS : (i + 1) * ROWS, :]
        bias = one_word(piece[256:272, :])
        for m in range(GROUP):
            qsum[:, lanes(h * GROUP + m)] = bias[m : m + 1]
        ksum[:, lanes(h)] = bias[5:6]
        vsum[:, lanes(h)] = bias[6:7]


def gather_heads_body(step, sc, *refs):
    pieces, outs = refs[:4], refs[4:]
    z = sc[0]
    for s, piece in enumerate(pieces):
        h = lax.rem(z + (s * step) % 4, 4)
        width = piece.shape[0] // ROWS // len(outs)
        for i, out in enumerate(outs):
            for m in range(width):
                o = (i * width + m) * ROWS
                out[:, lanes(h * width + m)] = piece[o : o + ROWS, :]


def call(body, n_in, outs, scratch=(), scalars=True, anywhere=(), us=1, mib=16):
    spec = pl.BlockSpec(memory_space=pltpu.VMEM)
    first = [pl.BlockSpec(memory_space=pltpu.SMEM)] if scalars else []
    ins = [pl.BlockSpec(memory_space=pl.ANY) if i in anywhere else spec for i in range(n_in)]
    return pl.pallas_call(
        body,
        in_specs=first + ins,
        out_specs=[spec] * len(outs),
        out_shape=[jax.ShapeDtypeStruct(s, t) for s, t in outs],
        scratch_shapes=list(scratch),
        cost_estimate=pl.CostEstimate(
            flops=us * 1000000, bytes_accessed=us * 3000000, transcendentals=0
        ),
        compiler_params=pltpu.CompilerParams(vmem_limit_bytes=mib * 1024 * 1024),
    )


def shift(v, axis, s):
    n = lax.axis_size(axis)
    return lax.ppermute(v, axis, [(i, (i + s) % n) for i in range(n)])


def on_device(pq, pk, pv, pg, rq, rk, rv, rg, qbias, kbias, vbias, segments, lengths):
    sc = jnp.stack(
        [lax.axis_index(a) for a in ("z", "x", "core", "branch")] + [lengths[0, 0]]
    ).astype(jnp.int32)
    tables = angle_tables()
    bias = jnp.concatenate([qbias, kbias, vbias])[None]
    kv = call(prepare_kv_body, 10, [((OWN, HD), bf16)] * 4, mib=56)(
        sc, pk[0], pv[0], rk[0, 0], rv[0, 0], bias, segments, *tables
    )
    q = call(prepare_q_body, 9, [((4 * STRIPE, HD), bf16)] * 4, mib=56)(
        sc, pq[0], pg[0], rq[0, 0], rg[0, 0], bias, *tables
    )
    kv = jnp.stack([kv[0]] + [shift(kv[s], "z", s) for s in (1, 2, 3)])
    kv, q = lax.optimization_barrier((kv, q))
    q = [q[0]] + [shift(q[s], "z", s) for s in (1, 2, 3)]
    far = shift(kv[:, :PKV].reshape(4 * PKV, HD), "branch", 1)
    kv = jnp.concatenate([kv.reshape(4 * OWN, HD), far])
    across = [kv] + [shift(kv, "x", s) for s in (1, 2, 3)]
    across[2], q = lax.optimization_barrier((across[2], q))
    pieces = [v for piece in across for v in (piece, shift(piece, "core", 1))]

    rows = 4 * STRIPE
    outs = call(
        attend_body,
        16,
        [((rows, HD), bf16)] * 4 + [((4 * TERMS + 16, HD), bf16)] * 2,
        [pltpu.VMEM((rows, HD), bf16)] * 4
        + [pltpu.VMEM((PROMPT, HD), bf16)] * 2
        + [pltpu.VMEM((REPLY, HD), bf16)] * 2
        + [pltpu.VMEM((8, rows), f32), pltpu.VMEM((4, 8, STRIPE), f32)]
        + [pltpu.VMEM((rows, HD), f32)] * 2
        + [pltpu.VMEM((PROMPT, HD), f32)] * 2
        + [pltpu.VMEM((REPLY, HD), f32)] * 2
        + [pltpu.VMEM((8, rows), f32)] * 2
        + [pltpu.VMEM((HD, rows), f32)]
        + [pltpu.VMEM((rows, HD), f32)] * 2
        + [pltpu.VMEM((4, 16, HD), f32), pltpu.VMEM((8, HD), f32)],
        us=60,
        mib=40,
    )(sc, *q, *pieces, *tables)
    back, (keep, send) = outs[:4], outs[4:]
    own, *parts, bias = call(
        along_core_body,
        2,
        [((TERMS, HD), f32)] + [((TERMS, HD), bf16)] * 3 + [((8, HD), f32)],
        scalars=False,
        us=2,
    )(keep, shift(send, "core", 1))
    back = [back[0]] + [shift(back[s], "z", -s) for s in (1, 2, 3)]
    parts = [shift(parts[s - 1], "x", s) for s in (1, 2, 3)]
    bias = bias + shift(bias, "dp", 1)
    biases = [bias] + [shift(bias, "x", s) for s in (1, 2, 3)]
    wide = ((ROWS, HEADS * GROUP * HD), bf16)
    p_out, r_out, p_dq, r_dq = call(functools.partial(gather_heads_body, 1), 4, [wide] * 4, us=2)(
        sc, *back
    )
    p_own, r_own, p_far, bias = call(
        along_x_body,
        9,
        [((512, HD), f32)] * 2 + [((528, HD), bf16), ((8, HD), f32)],
        scalars=False,
        anywhere=(0,),
        us=2,
    )(p_out, own, *parts, *biases)
    p_far = shift(p_far, "branch", 1)
    dkv = call(settle_body, 8, [((4 * ROWS + 16, HD), bf16)] * 4)(
        sc, p_own, r_own, p_far, bias, *tables
    )
    dkv = [dkv[0]] + [shift(dkv[t], "z", t) for t in (1, 2, 3)]
    narrow = ((ROWS, HEADS * HD), bf16)
    p_dk, p_dv, r_dk, r_dv, qsum, ksum, vsum = call(
        finish_body,
        4,
        [narrow] * 4 + [((1, HEADS * GROUP * HD), f32)] + [((1, HEADS * HD), f32)] * 2,
    )(sc, *dkv)
    return (
        p_out[None],
        r_out[None, None],
        p_dq[None],
        p_dk[None],
        p_dv[None],
        r_dq[None, None],
        r_dk[None, None],
        r_dv[None, None],
        qsum.reshape(-1),
        ksum.reshape(-1),
        vsum.reshape(-1),
    )


def solution(mesh):
    fine = Mesh(mesh.devices.reshape(2, 4, 4, 2, 2), ("dp", "z", "x", "core", "branch"))
    prompt = P("dp", ("z", "x", "core", "branch"), None)
    reply = P("dp", "branch", ("z", "x", "core"), None)
    return jax.shard_map(
        on_device,
        mesh=fine,
        in_specs=(prompt,) * 4
        + (reply,) * 4
        + (P(),) * 3
        + (P("dp", ("z", "x", "core", "branch")), P("dp", "branch")),
        out_specs=(prompt, reply, prompt, prompt, prompt, reply, reply, reply, P(), P(), P()),
        check_vma=False,
    )
```

time: 198 us -> 155 us (0.78)
  Pallas kernels: 75.8 us -> 60.7 us
  waiting for transfers between devices: 52.9 us -> 38.7 us
  starting transfers between devices: 56 us -> 49.8 us
  local copies, waits for them, and re-layouts: 7.1 us -> 2.22 us
    ppermute x7 -> x0, waiting for transfers between devices: 18.4 us -> none  [swap(): lax.ppermute(v, axis, [(i, i ^ bit) for i in range(lax.axis_size(axis))])]
    pallas_call x7 -> x8, Pallas kernels: 75.8 us -> 60.7 us  [the longest x1 51.7 us: on_device(): call(attend_body, 16, [((rows, HD), bf16)] * 4 + [((4 * TERMS + 16, HD),...]
    ppermute x7 -> x0, starting transfers between devices: 12.2 us -> none  [swap(): lax.ppermute(v, axis, [(i, i ^ bit) for i in range(lax.axis_size(axis))])]
    ppermute x31 -> x29, starting transfers between devices: 43.8 us -> 49.8 us  [shift(): return lax.ppermute(v, axis, [(i, (i + s) % n) for i in range(n)])]
    ppermute x31 -> x29, waiting for transfers between devices: 34.5 us -> 38.7 us  [shift(): return lax.ppermute(v, axis, [(i, (i + s) % n) for i in range(n)])]
    unnamed x70 -> x18, local copies, waits for them, and re-layouts: 3.45 us -> 1 us
  transfers between devices with their start and end apart: 38 -> 29, of which waited for: 16 -> 17; matrix products, arithmetic and copies ran while one was open for 2% -> 0% of each run, Pallas kernels for 5% -> 3%
where the time goes in v2:
time: 155 us
  Pallas kernels  60.7 us (39%)
  starting transfers between devices  49.8 us (32%)
  waiting for transfers between devices  38.7 us (25%)
  other arithmetic  2.31 us (1%)
  local copies, waits for them, and re-layouts  2.22 us (1%)
    pallas_call x1, Pallas kernels, on_device(): call(attend_body, 16, [((rows, HD), bf16)] * 4 + [((4 * TERMS + 16, HD),...  51.7 us
    ppermute x29, starting transfers between devices, shift(): return lax.ppermute(v, axis, [(i, (i + s) % n) for i in range(n)])  49.8 us
    ppermute x29, waiting for transfers between devices, shift(): return lax.ppermute(v, axis, [(i, (i + s) % n) for i in range(n)])  38.7 us
  transfers between devices with their start and end apart: 29, of which 17 were waited for; matrix products, arithmetic and copies ran while one was open for 0% of the time, Pallas kernels for 3%

profile of v2, /device:TPU:0, one launch (start us, length us, event | category | flops | bytes accessed | tf_op | source)
XLA Modules:
  0.0 155.1 jit_solution(15722162850901063647)
XLA Ops:
  3.2 1.9 %shard_map.248 = (bf16[272,128]{1,0:T(8,128)(2,1)}, bf16[272,128]{1,0:T(8,128)(2,1)}, bf16[272,128]{1,0:T(8,128)(2,1)}, bf16[272,128]{1,0:T(8,128)(2,1)}) custom-call(s32[5]{0:T(128)} %stack.34.sc, bf16[64,512]{1,0:T(8,128)(2,1)} %bitcast.41, bf16[64,512]{1,0:T(8,128)(2,1)} %bitcast.42, bf16[64,512]{1,0:T(8,128)(2,1)} %bitcast.43, bf16[64,512]{1,0:T(8,128)(2,1)} %bitcast.44, ...), custom_call_target="tpu_custom_call" | custom-call | flops 1000000 | bytes 3000000 | tf_op jit(solution)/shard_map/pallas_call | solution.py:511
  5.2 2.0 %collective-permute-start = (bf16[272,128]{1,0:T(8,128)(2,1)}, bf16[272,128]{1,0:T(8,128)(2,1)S(1)}, u32[]{:S(2)}, u32[]{:S(2)}) collective-permute-start(bf16[272,128]{1,0:T(8,128)(2,1)} %get-tuple-element.60), channel_id=1, source_target_pairs={{0,16},{16,32},{32,48},{48,0},{1,17},{17,33},{33,49},{49,1},{2,18}... | collective-permute-start | bytes 208904 | tf_op jit(solution)/shard_map/ppermute | solution.py:502
  7.2 3.6 %collective-permute-start.1 = (bf16[272,128]{1,0:T(8,128)(2,1)}, bf16[272,128]{1,0:T(8,128)(2,1)S(1)}, u32[]{:S(2)}, u32[]{:S(2)}) collective-permute-start(bf16[272,128]{1,0:T(8,128)(2,1)} %get-tuple-element.61), channel_id=1, source_target_pairs={{0,32},{16,48},{32,0},{48,16},{1,33},{17,49},{33,1},{49,17},{2,34}... | collective-permute-start | bytes 208904 | tf_op jit(solution)/shard_map/ppermute | solution.py:502
  11.8 2.7 %shard_map.249 = (bf16[1280,128]{1,0:T(8,128)(2,1)}, bf16[1280,128]{1,0:T(8,128)(2,1)}, bf16[1280,128]{1,0:T(8,128)(2,1)}, bf16[1280,128]{1,0:T(8,128)(2,1)}) custom-call(s32[5]{0:T(128)} %stack.34.sc, bf16[64,2560]{1,0:T(8,128)(2,1)} %bitcast.32, bf16[64,2560]{1,0:T(8,128)(2,1)} %bitcast.33, bf16[64,2560]{1,0:T(8,128)(2,1)} %bitcast.34, ...), custom_call_target="tpu_custom_call" | custom-call | flops 1000000 | bytes 3000000 | tf_op jit(solution)/shard_map/pallas_call | solution.py:514
  16.2 3.3 %collective-permute-start.3 = (bf16[576,128]{1,0:T(8,128)(2,1)S(1)}, bf16[576,128]{1,0:T(8,128)(2,1)S(1)}, u32[]{:S(2)}, u32[]{:S(2)}) collective-permute-start(bf16[576,128]{1,0:T(8,128)(2,1)S(1)} %bitcast.36), channel_id=1, source_target_pairs={{0,1},{1,0},{2,3},{3,2},{4,5},{5,4},{6,7},{7,6},{8,9},{9,8},{10,11... | collective-permute-start | bytes 442376 | tf_op jit(solution)/shard_map/ppermute | solution.py:502
  19.9 3.1 %collective-permute-done.3 = bf16[576,128]{1,0:T(8,128)(2,1)S(1)} collective-permute-done((bf16[576,128]{1,0:T(8,128)(2,1)S(1)}, bf16[576,128]{1,0:T(8,128)(2,1)S(1)}, u32[]{:S(2)}, u32[]{:S(2)}) %collective-permute-start.3) | collective-permute-done | bytes 147488 | tf_op jit(solution)/shard_map/ppermute | solution.py:502
  23.0 3.1 %collective-permute-start.4 = (bf16[1664,128]{1,0:T(8,128)(2,1)S(1)}, bf16[1664,128]{1,0:T(8,128)(2,1)S(1)}, u32[]{:S(2)}, u32[]{:S(2)}) collective-permute-start(bf16[1664,128]{1,0:T(8,128)(2,1)S(1)} %pad_maximum_fusion.refs_4_), channel_id=1, source_target_pairs={{0,8},{4,12},{8,0},{12,4},{1,9},{5,13},{9,1},{13,5},{2,10},{6,14},... | collective-permute-start | bytes 1277960 | tf_op jit(solution)/shard_map/ppermute | solution.py:502
  26.1 1.1 collective-permute-start.12
  28.1 1.5 collective-permute-start.6
  29.6 1.5 collective-permute-start.7
  31.2 5.5 %collective-permute-done.6.refs_2_ = bf16[1280,128]{1,0:T(8,128)(2,1)S(1)} collective-permute-done((bf16[1280,128]{1,0:T(8,128)(2,1)S(1)}, bf16[1280,128]{1,0:T(8,128)(2,1)S(1)}, u32[]{:S(2)}, u32[]{:S(2)}) %collective-permute-start.6) | collective-permute-done | bytes 327712 | tf_op jit(solution)/shard_map/ppermute | solution.py:502
  36.7 5.6 %collective-permute-done.7.refs_3_ = bf16[1280,128]{1,0:T(8,128)(2,1)S(1)} collective-permute-done((bf16[1280,128]{1,0:T(8,128)(2,1)S(1)}, bf16[1280,128]{1,0:T(8,128)(2,1)S(1)}, u32[]{:S(2)}, u32[]{:S(2)}) %collective-permute-start.7) | collective-permute-done | bytes 327712 | tf_op jit(solution)/shard_map/ppermute | solution.py:502
  43.4 1.2 collective-permute-done.13.refs_11_
  45.9 51.7 %shard_map.250 = (bf16[1280,128]{1,0:T(8,128)(2,1)S(1)}, bf16[1280,128]{1,0:T(8,128)(2,1)S(1)}, bf16[1280,128]{1,0:T(8,128)(2,1)S(1)}, bf16[1280,128]{1,0:T(8,12...) custom-call(s32[5]{0:T(128)S(1)} %copy-done.6, bf16[1280,128]{1,0:T(8,128)(2,1)S(1)} %copy-done.4, ...), custom_call_target="tpu_custom_call" | custom-call | flops 60000000 | bytes 180000000 | tf_op jit(solution)/shard_map/pallas_call | solution.py:527
  97.8 2.2 %collective-permute-start.14 = (bf16[1280,128]{1,0:T(8,128)(2,1)S(1)}, bf16[1280,128]{1,0:T(8,128)(2,1)S(1)}, u32[]{:S(2)}, u32[]{:S(2)}) collective-permute-start(bf16[1280,128]{1,0:T(8,128)(2,1)S(1)} %get-tuple-element.78), channel_id=1, source_target_pairs={{0,48},{16,0},{32,16},{48,32},{1,49},{17,1},{33,17},{49,33},{2,50}... | collective-permute-start | bytes 983048 | tf_op jit(solution)/shard_map/ppermute | solution.py:502
  101.4 1.4 collective-permute-start.18
  102.9 7.7 %collective-permute-start.19 = (bf16[1536,128]{1,0:T(8,128)(2,1)S(1)}, bf16[1536,128]{1,0:T(8,128)(2,1)S(1)}, u32[]{:S(2)}, u32[]{:S(2)}) collective-permute-start(bf16[1536,128]{1,0:T(8,128)(2,1)S(1)} %get-tuple-element.88), channel_id=1, source_target_pairs={{0,8},{4,12},{8,0},{12,4},{1,9},{5,13},{9,1},{13,5},{2,10},{6,14},... | collective-permute-start | bytes 1179656 | tf_op jit(solution)/shard_map/ppermute | solution.py:502
  111.3 1.6 %collective-permute-start.21 = (f32[8,128]{1,0:T(8,128)S(1)}, f32[8,128]{1,0:T(8,128)S(1)}, u32[]{:S(2)}, u32[]{:S(2)}) collective-permute-start(f32[8,128]{1,0:T(8,128)S(1)} %get-tuple-element.90), channel_id=1, source_target_pairs={{0,64},{64,0},{1,65},{65,1},{2,66},{66,2},{3,67},{67,3},{4,68},{68... | collective-permute-start | bytes 12296 | tf_op jit(solution)/shard_map/ppermute | solution.py:502
  112.9 1.4 collective-permute-start.15
  114.9 1.1 collective-permute-start.16
  116.0 9.1 %collective-permute-done.15.refs_2_ = bf16[1280,128]{1,0:T(8,128)(2,1)S(1)} collective-permute-done((bf16[1280,128]{1,0:T(8,128)(2,1)S(1)}, bf16[1280,128]{1,0:T(8,128)(2,1)S(1)}, u32[]{:S(2)}, u32[]{:S(2)}) %collective-permute-start.15) | collective-permute-done | bytes 327712 | tf_op jit(solution)/shard_map/ppermute | solution.py:502
  125.1 2.4 %collective-permute-start.24 = (f32[8,128]{1,0:T(8,128)S(1)}, f32[8,128]{1,0:T(8,128)S(1)}, u32[]{:S(2)}, u32[]{:S(2)}) collective-permute-start(f32[8,128]{1,0:T(8,128)S(1)} %add.3.b0), channel_id=1, source_target_pairs={{0,12},{4,0},{8,4},{12,8},{1,13},{5,1},{9,5},{13,9},{2,14},{6,2},{... | collective-permute-start | bytes 12296 | tf_op jit(solution)/shard_map/ppermute | solution.py:502
  127.5 2.5 %collective-permute-done.16.refs_3_ = bf16[1280,128]{1,0:T(8,128)(2,1)S(1)} collective-permute-done((bf16[1280,128]{1,0:T(8,128)(2,1)S(1)}, bf16[1280,128]{1,0:T(8,128)(2,1)S(1)}, u32[]{:S(2)}, u32[]{:S(2)}) %collective-permute-start.16) | collective-permute-done | bytes 327712 | tf_op jit(solution)/shard_map/ppermute | solution.py:502
  130.1 2.6 %collective-permute-start.23 = (f32[8,128]{1,0:T(8,128)S(1)}, f32[8,128]{1,0:T(8,128)S(1)}, u32[]{:S(2)}, u32[]{:S(2)}) collective-permute-start(f32[8,128]{1,0:T(8,128)S(1)} %add.3.b0), channel_id=1, source_target_pairs={{0,8},{4,12},{8,0},{12,4},{1,9},{5,13},{9,1},{13,5},{2,10},{6,14},... | collective-permute-start | bytes 12296 | tf_op jit(solution)/shard_map/ppermute | solution.py:502
  132.7 1.2 collective-permute-start.22
  133.9 1.9 %shard_map.251 = (bf16[64,2560]{1,0:T(8,128)(2,1)}, bf16[64,2560]{1,0:T(8,128)(2,1)}, bf16[64,2560]{1,0:T(8,128)(2,1)}, bf16[64,2560]{1,0:T(8,128)(2,1)}) custom-call(s32[5]{0:T(128)S(1)} %copy-done.6, bf16[1280,128]{1,0:T(8,128)(2,1)S(1)} %get-tuple-element.77.refs_0_, bf16[1280,128]{1,0:T(8,128)(2,1)S(1)} %collective-permute-done.14.refs_1_, ...), custom_call_target="tpu_custom_call" | custom-call | flops 2000000 | bytes 6000000 | tf_op jit(solution)/shard_map/pallas_call | solution.py:558
  135.8 1.7 %collective-permute-done.22.b1 = f32[8,128]{1,0:T(8,128)S(1)} collective-permute-done((f32[8,128]{1,0:T(8,128)S(1)}, f32[8,128]{1,0:T(8,128)S(1)}, u32[]{:S(2)}, u32[]{:S(2)}) %collective-permute-start.22) | collective-permute-done | bytes 4128 | tf_op jit(solution)/shard_map/ppermute | solution.py:502
  138.7 3.3 %collective-permute-start.25 = (bf16[528,128]{1,0:T(8,128)(2,1)S(1)}, bf16[528,128]{1,0:T(8,128)(2,1)S(1)}, u32[]{:S(2)}, u32[]{:S(2)}) collective-permute-start(bf16[528,128]{1,0:T(8,128)(2,1)S(1)} %get-tuple-element.93), channel_id=1, source_target_pairs={{0,1},{1,0},{2,3},{3,2},{4,5},{5,4},{6,7},{7,6},{8,9},{9,8},{10,11... | collective-permute-start | bytes 405512 | tf_op jit(solution)/shard_map/ppermute | solution.py:502
  142.0 3.3 %collective-permute-done.25.p_far = bf16[528,128]{1,0:T(8,128)(2,1)S(1)} collective-permute-done((bf16[528,128]{1,0:T(8,128)(2,1)S(1)}, bf16[528,128]{1,0:T(8,128)(2,1)S(1)}, u32[]{:S(2)}, u32[]{:S(2)}) %collective-permute-start.25) | collective-permute-done | bytes 135200 | tf_op jit(solution)/shard_map/ppermute | solution.py:502
  146.8 1.6 %collective-permute-start.27 = (bf16[272,128]{1,0:T(8,128)(2,1)S(1)}, bf16[272,128]{1,0:T(8,128)(2,1)S(1)}, u32[]{:S(2)}, u32[]{:S(2)}) collective-permute-start(bf16[272,128]{1,0:T(8,128)(2,1)S(1)} %get-tuple-element.97), channel_id=1, source_target_pairs={{0,32},{16,48},{32,0},{48,16},{1,33},{17,49},{33,1},{49,17},{2,34}... | collective-permute-start | bytes 208904 | tf_op jit(solution)/shard_map/ppermute | solution.py:502
  148.3 2.5 %collective-permute-start.28 = (bf16[272,128]{1,0:T(8,128)(2,1)S(1)}, bf16[272,128]{1,0:T(8,128)(2,1)S(1)}, u32[]{:S(2)}, u32[]{:S(2)}) collective-permute-start(bf16[272,128]{1,0:T(8,128)(2,1)S(1)} %get-tuple-element.98), channel_id=1, source_target_pairs={{0,48},{16,0},{32,16},{48,32},{1,49},{17,1},{33,17},{49,33},{2,50}... | collective-permute-start | bytes 208904 | tf_op jit(solution)/shard_map/ppermute | solution.py:502
  153.2 1.3 shard_map.255
  (60 shorter events, 16.8 us)
Async XLA Ops:
  5.2 9.4 %collective-permute-start = (bf16[272,128]{1,0:T(8,128)(2,1)}, bf16[272,128]{1,0:T(8,128)(2,1)S(1)}, u32[]{:S(2)}, u32[]{:S(2)}) collective-permute-start(bf16[272,128]{1,0:T(8,128)(2,1)} %get-tuple-element.60), channel_id=1, source_target_pairs={{0,16},{16,32},{32,48},{48,0},{1,17},{17,33},{33,49},{49,1},{2,18}... | collective-permute-start | bytes 208904 | tf_op jit(solution)/shard_map/ppermute | solution.py:502
  7.2 7.4 %collective-permute-start.1 = (bf16[272,128]{1,0:T(8,128)(2,1)}, bf16[272,128]{1,0:T(8,128)(2,1)S(1)}, u32[]{:S(2)}, u32[]{:S(2)}) collective-permute-start(bf16[272,128]{1,0:T(8,128)(2,1)} %get-tuple-element.61), channel_id=1, source_target_pairs={{0,32},{16,48},{32,0},{48,16},{1,33},{17,49},{33,1},{49,17},{2,34}... | collective-permute-start | bytes 208904 | tf_op jit(solution)/shard_map/ppermute | solution.py:502
  10.7 4.5 %collective-permute-start.2 = (bf16[272,128]{1,0:T(8,128)(2,1)}, bf16[272,128]{1,0:T(8,128)(2,1)S(1)}, u32[]{:S(2)}, u32[]{:S(2)}) collective-permute-start(bf16[272,128]{1,0:T(8,128)(2,1)} %get-tuple-element.62), channel_id=1, source_target_pairs={{0,48},{16,0},{32,16},{48,32},{1,49},{17,1},{33,17},{49,33},{2,50}... | collective-permute-start | bytes 208904 | tf_op jit(solution)/shard_map/ppermute | solution.py:502
  11.7 34.1 %copy-start.2 = (f32[64,128]{1,0:T(8,128)S(1)}, f32[64,128]{1,0:T(8,128)}, u32[]{:S(2)}) copy-start(f32[64,128]{1,0:T(8,128)} %constant.26.clone.t3.refs_15_) | copy-start | bytes 98308
  11.8 34.1 %copy-start.3 = (f32[64,128]{1,0:T(8,128)S(1)}, f32[64,128]{1,0:T(8,128)}, u32[]{:S(2)}) copy-start(f32[64,128]{1,0:T(8,128)} %constant.25.clone.t2.refs_14_) | copy-start | bytes 98308
  11.8 34.1 %copy-start.6 = (s32[5]{0:T(128)S(1)}, s32[5]{0:T(128)}, u32[]{:S(2)}) copy-start(s32[5]{0:T(128)} %stack.34.sc) | copy-start | bytes 64
  16.2 6.7 %collective-permute-start.3 = (bf16[576,128]{1,0:T(8,128)(2,1)S(1)}, bf16[576,128]{1,0:T(8,128)(2,1)S(1)}, u32[]{:S(2)}, u32[]{:S(2)}) collective-permute-start(bf16[576,128]{1,0:T(8,128)(2,1)S(1)} %bitcast.36), channel_id=1, source_target_pairs={{0,1},{1,0},{2,3},{3,2},{4,5},{5,4},{6,7},{7,6},{8,9},{9,8},{10,11... | collective-permute-start | bytes 442376 | tf_op jit(solution)/shard_map/ppermute | solution.py:502
  19.5 10.1 %collective-permute-start.5 = (bf16[1280,128]{1,0:T(8,128)(2,1)}, bf16[1280,128]{1,0:T(8,128)(2,1)S(1)}, u32[]{:S(2)}, u32[]{:S(2)}) collective-permute-start(bf16[1280,128]{1,0:T(8,128)(2,1)} %get-tuple-element.69), channel_id=1, source_target_pairs={{0,16},{16,32},{32,48},{48,0},{1,17},{17,33},{33,49},{49,1},{2,18}... | collective-permute-start | bytes 983048 | tf_op jit(solution)/shard_map/ppermute | solution.py:502
  23.0 19.3 %collective-permute-start.4 = (bf16[1664,128]{1,0:T(8,128)(2,1)S(1)}, bf16[1664,128]{1,0:T(8,128)(2,1)S(1)}, u32[]{:S(2)}, u32[]{:S(2)}) collective-permute-start(bf16[1664,128]{1,0:T(8,128)(2,1)S(1)} %pad_maximum_fusion.refs_4_), channel_id=1, source_target_pairs={{0,8},{4,12},{8,0},{12,4},{1,9},{5,13},{9,1},{13,5},{2,10},{6,14},... | collective-permute-start | bytes 1277960 | tf_op jit(solution)/shard_map/ppermute | solution.py:502
  26.1 16.8 %collective-permute-start.12 = (bf16[1664,128]{1,0:T(8,128)(2,1)S(1)}, bf16[1664,128]{1,0:T(8,128)(2,1)S(1)}, u32[]{:S(2)}, u32[]{:S(2)}) collective-permute-start(bf16[1664,128]{1,0:T(8,128)(2,1)S(1)} %pad_maximum_fusion.refs_4_), channel_id=1, source_target_pairs={{0,12},{4,0},{8,4},{12,8},{1,13},{5,1},{9,5},{13,9},{2,14},{6,2},{... | collective-permute-start | bytes 1277960 | tf_op jit(solution)/shard_map/ppermute | solution.py:502
  27.2 15.6 %collective-permute-start.9 = (bf16[1664,128]{1,0:T(8,128)(2,1)S(1)}, bf16[1664,128]{1,0:T(8,128)(2,1)S(1)}, u32[]{:S(2)}, u32[]{:S(2)}) collective-permute-start(bf16[1664,128]{1,0:T(8,128)(2,1)S(1)} %pad_maximum_fusion.refs_4_), channel_id=1, source_target_pairs={{0,4},{4,8},{8,12},{12,0},{1,5},{5,9},{9,13},{13,1},{2,6},{6,10},{... | collective-permute-start | bytes 1277960 | tf_op jit(solution)/shard_map/ppermute | solution.py:502
  28.1 8.6 %collective-permute-start.6 = (bf16[1280,128]{1,0:T(8,128)(2,1)S(1)}, bf16[1280,128]{1,0:T(8,128)(2,1)S(1)}, u32[]{:S(2)}, u32[]{:S(2)}) collective-permute-start(bf16[1280,128]{1,0:T(8,128)(2,1)S(1)} %copy-done.8), channel_id=1, source_target_pairs={{0,32},{16,48},{32,0},{48,16},{1,33},{17,49},{33,1},{49,17},{2,34}... | collective-permute-start | bytes 983048 | tf_op jit(solution)/shard_map/ppermute | solution.py:502
  29.6 12.7 %collective-permute-start.7 = (bf16[1280,128]{1,0:T(8,128)(2,1)S(1)}, bf16[1280,128]{1,0:T(8,128)(2,1)S(1)}, u32[]{:S(2)}, u32[]{:S(2)}) collective-permute-start(bf16[1280,128]{1,0:T(8,128)(2,1)S(1)} %copy-done.7), channel_id=1, source_target_pairs={{0,48},{16,0},{32,16},{48,32},{1,49},{17,1},{33,17},{49,33},{2,50}... | collective-permute-start | bytes 983048 | tf_op jit(solution)/shard_map/ppermute | solution.py:502
  36.7 6.7 %collective-permute-start.8 = (bf16[1664,128]{1,0:T(8,128)(2,1)S(1)}, bf16[1664,128]{1,0:T(8,128)(2,1)S(1)}, u32[]{:S(2)}, u32[]{:S(2)}) collective-permute-start(bf16[1664,128]{1,0:T(8,128)(2,1)S(1)} %pad_maximum_fusion.refs_4_), channel_id=1, source_target_pairs={{0,2},{2,0},{1,3},{3,1},{4,6},{6,4},{5,7},{7,5},{8,10},{10,8},{9,1... | collective-permute-start | bytes 1277960 | tf_op jit(solution)/shard_map/ppermute | solution.py:502
  42.8 1.8 %collective-permute-start.13 = (bf16[1664,128]{1,0:T(8,128)(2,1)S(1)}, bf16[1664,128]{1,0:T(8,128)(2,1)S(1)}, u32[]{:S(2)}, u32[]{:S(2)}) collective-permute-start(bf16[1664,128]{1,0:T(8,128)(2,1)S(1)} %collective-permute-done.12.refs_10_), channel_id=1, source_target_pairs={{0,2},{2,0},{1,3},{3,1},{4,6},{6,4},{5,7},{7,5},{8,10},{10,8},{9,1... | collective-permute-start | bytes 1277960 | tf_op jit(solution)/shard_map/ppermute | solution.py:502
  42.8 2.4 %collective-permute-start.10 = (bf16[1664,128]{1,0:T(8,128)(2,1)S(1)}, bf16[1664,128]{1,0:T(8,128)(2,1)S(1)}, u32[]{:S(2)}, u32[]{:S(2)}) collective-permute-start(bf16[1664,128]{1,0:T(8,128)(2,1)S(1)} %collective-permute-done.9.refs_6_), channel_id=1, source_target_pairs={{0,2},{2,0},{1,3},{3,1},{4,6},{6,4},{5,7},{7,5},{8,10},{10,8},{9,1... | collective-permute-start | bytes 1277960 | tf_op jit(solution)/shard_map/ppermute | solution.py:502
  43.4 2.5 %collective-permute-start.11 = (bf16[1664,128]{1,0:T(8,128)(2,1)S(1)}, bf16[1664,128]{1,0:T(8,128)(2,1)S(1)}, u32[]{:S(2)}, u32[]{:S(2)}) collective-permute-start(bf16[1664,128]{1,0:T(8,128)(2,1)S(1)} %collective-permute-done.4.refs_8_), channel_id=1, source_target_pairs={{0,2},{2,0},{1,3},{3,1},{4,6},{6,4},{5,7},{7,5},{8,10},{10,8},{9,1... | collective-permute-start | bytes 1277960 | tf_op jit(solution)/shard_map/ppermute | solution.py:502
  97.6 3.5 %collective-permute-start.17 = (bf16[6160,128]{1,0:T(8,128)(2,1)S(1)}, bf16[6160,128]{1,0:T(8,128)(2,1)S(1)}, u32[]{:S(2)}, u32[]{:S(2)}) collective-permute-start(bf16[6160,128]{1,0:T(8,128)(2,1)S(1)} %get-tuple-element.85), channel_id=1, source_target_pairs={{0,2},{2,0},{1,3},{3,1},{4,6},{6,4},{5,7},{7,5},{8,10},{10,8},{9,1... | collective-permute-start | bytes 4730888 | tf_op jit(solution)/shard_map/ppermute | solution.py:502
  97.8 15.1 %collective-permute-start.14 = (bf16[1280,128]{1,0:T(8,128)(2,1)S(1)}, bf16[1280,128]{1,0:T(8,128)(2,1)S(1)}, u32[]{:S(2)}, u32[]{:S(2)}) collective-permute-start(bf16[1280,128]{1,0:T(8,128)(2,1)S(1)} %get-tuple-element.78), channel_id=1, source_target_pairs={{0,48},{16,0},{32,16},{48,32},{1,49},{17,1},{33,17},{49,33},{2,50}... | collective-permute-start | bytes 983048 | tf_op jit(solution)/shard_map/ppermute | solution.py:502
  101.4 36.1 %collective-permute-start.18 = (bf16[1536,128]{1,0:T(8,128)(2,1)S(1)}, bf16[1536,128]{1,0:T(8,128)(2,1)S(1)}, u32[]{:S(2)}, u32[]{:S(2)}) collective-permute-start(bf16[1536,128]{1,0:T(8,128)(2,1)S(1)} %get-tuple-element.87), channel_id=1, source_target_pairs={{0,4},{4,8},{8,12},{12,0},{1,5},{5,9},{9,13},{13,1},{2,6},{6,10},{... | collective-permute-start | bytes 1179656 | tf_op jit(solution)/shard_map/ppermute | solution.py:502
  102.9 34.7 %collective-permute-start.19 = (bf16[1536,128]{1,0:T(8,128)(2,1)S(1)}, bf16[1536,128]{1,0:T(8,128)(2,1)S(1)}, u32[]{:S(2)}, u32[]{:S(2)}) collective-permute-start(bf16[1536,128]{1,0:T(8,128)(2,1)S(1)} %get-tuple-element.88), channel_id=1, source_target_pairs={{0,8},{4,12},{8,0},{12,4},{1,9},{5,13},{9,1},{13,5},{2,10},{6,14},... | collective-permute-start | bytes 1179656 | tf_op jit(solution)/shard_map/ppermute | solution.py:502
  110.5 27.0 %collective-permute-start.20 = (bf16[1536,128]{1,0:T(8,128)(2,1)S(1)}, bf16[1536,128]{1,0:T(8,128)(2,1)S(1)}, u32[]{:S(2)}, u32[]{:S(2)}) collective-permute-start(bf16[1536,128]{1,0:T(8,128)(2,1)S(1)} %get-tuple-element.89), channel_id=1, source_target_pairs={{0,12},{4,0},{8,4},{12,8},{1,13},{5,1},{9,5},{13,9},{2,14},{6,2},{... | collective-permute-start | bytes 1179656 | tf_op jit(solution)/shard_map/ppermute | solution.py:502
  111.3 3.6 %collective-permute-start.21 = (f32[8,128]{1,0:T(8,128)S(1)}, f32[8,128]{1,0:T(8,128)S(1)}, u32[]{:S(2)}, u32[]{:S(2)}) collective-permute-start(f32[8,128]{1,0:T(8,128)S(1)} %get-tuple-element.90), channel_id=1, source_target_pairs={{0,64},{64,0},{1,65},{65,1},{2,66},{66,2},{3,67},{67,3},{4,68},{68... | collective-permute-start | bytes 12296 | tf_op jit(solution)/shard_map/ppermute | solution.py:502
  112.9 12.2 %collective-permute-start.15 = (bf16[1280,128]{1,0:T(8,128)(2,1)S(1)}, bf16[1280,128]{1,0:T(8,128)(2,1)S(1)}, u32[]{:S(2)}, u32[]{:S(2)}) collective-permute-start(bf16[1280,128]{1,0:T(8,128)(2,1)S(1)} %get-tuple-element.79), channel_id=1, source_target_pairs={{0,32},{16,48},{32,0},{48,16},{1,33},{17,49},{33,1},{49,17},{2,34}... | collective-permute-start | bytes 983048 | tf_op jit(solution)/shard_map/ppermute | solution.py:502
  114.9 15.1 %collective-permute-start.16 = (bf16[1280,128]{1,0:T(8,128)(2,1)S(1)}, bf16[1280,128]{1,0:T(8,128)(2,1)S(1)}, u32[]{:S(2)}, u32[]{:S(2)}) collective-permute-start(bf16[1280,128]{1,0:T(8,128)(2,1)S(1)} %get-tuple-element.80), channel_id=1, source_target_pairs={{0,16},{16,32},{32,48},{48,0},{1,17},{17,33},{33,49},{49,1},{2,18}... | collective-permute-start | bytes 983048 | tf_op jit(solution)/shard_map/ppermute | solution.py:502
  125.1 7.6 %collective-permute-start.24 = (f32[8,128]{1,0:T(8,128)S(1)}, f32[8,128]{1,0:T(8,128)S(1)}, u32[]{:S(2)}, u32[]{:S(2)}) collective-permute-start(f32[8,128]{1,0:T(8,128)S(1)} %add.3.b0), channel_id=1, source_target_pairs={{0,12},{4,0},{8,4},{12,8},{1,13},{5,1},{9,5},{13,9},{2,14},{6,2},{... | collective-permute-start | bytes 12296 | tf_op jit(solution)/shard_map/ppermute | solution.py:502
  130.1 5.7 %collective-permute-start.23 = (f32[8,128]{1,0:T(8,128)S(1)}, f32[8,128]{1,0:T(8,128)S(1)}, u32[]{:S(2)}, u32[]{:S(2)}) collective-permute-start(f32[8,128]{1,0:T(8,128)S(1)} %add.3.b0), channel_id=1, source_target_pairs={{0,8},{4,12},{8,0},{12,4},{1,9},{5,13},{9,1},{13,5},{2,10},{6,14},... | collective-permute-start | bytes 12296 | tf_op jit(solution)/shard_map/ppermute | solution.py:502
  132.7 4.8 %collective-permute-start.22 = (f32[8,128]{1,0:T(8,128)S(1)}, f32[8,128]{1,0:T(8,128)S(1)}, u32[]{:S(2)}, u32[]{:S(2)}) collective-permute-start(f32[8,128]{1,0:T(8,128)S(1)} %add.3.b0), channel_id=1, source_target_pairs={{0,4},{4,8},{8,12},{12,0},{1,5},{5,9},{9,13},{13,1},{2,6},{6,10},{... | collective-permute-start | bytes 12296 | tf_op jit(solution)/shard_map/ppermute | solution.py:502
  138.7 6.6 %collective-permute-start.25 = (bf16[528,128]{1,0:T(8,128)(2,1)S(1)}, bf16[528,128]{1,0:T(8,128)(2,1)S(1)}, u32[]{:S(2)}, u32[]{:S(2)}) collective-permute-start(bf16[528,128]{1,0:T(8,128)(2,1)S(1)} %get-tuple-element.93), channel_id=1, source_target_pairs={{0,1},{1,0},{2,3},{3,2},{4,5},{5,4},{6,7},{7,6},{8,9},{9,8},{10,11... | collective-permute-start | bytes 405512 | tf_op jit(solution)/shard_map/ppermute | solution.py:502
  146.0 5.6 %collective-permute-start.26 = (bf16[272,128]{1,0:T(8,128)(2,1)S(1)}, bf16[272,128]{1,0:T(8,128)(2,1)S(1)}, u32[]{:S(2)}, u32[]{:S(2)}) collective-permute-start(bf16[272,128]{1,0:T(8,128)(2,1)S(1)} %get-tuple-element.96), channel_id=1, source_target_pairs={{0,16},{16,32},{32,48},{48,0},{1,17},{17,33},{33,49},{49,1},{2,18}... | collective-permute-start | bytes 208904 | tf_op jit(solution)/shard_map/ppermute | solution.py:502
  146.8 5.8 %collective-permute-start.27 = (bf16[272,128]{1,0:T(8,128)(2,1)S(1)}, bf16[272,128]{1,0:T(8,128)(2,1)S(1)}, u32[]{:S(2)}, u32[]{:S(2)}) collective-permute-start(bf16[272,128]{1,0:T(8,128)(2,1)S(1)} %get-tuple-element.97), channel_id=1, source_target_pairs={{0,32},{16,48},{32,0},{48,16},{1,33},{17,49},{33,1},{49,17},{2,34}... | collective-permute-start | bytes 208904 | tf_op jit(solution)/shard_map/ppermute | solution.py:502
  148.3 4.9 %collective-permute-start.28 = (bf16[272,128]{1,0:T(8,128)(2,1)S(1)}, bf16[272,128]{1,0:T(8,128)(2,1)S(1)}, u32[]{:S(2)}, u32[]{:S(2)}) collective-permute-start(bf16[272,128]{1,0:T(8,128)(2,1)S(1)} %get-tuple-element.98), channel_id=1, source_target_pairs={{0,48},{16,0},{32,16},{48,32},{1,49},{17,1},{33,17},{49,33},{2,50}... | collective-permute-start | bytes 208904 | tf_op jit(solution)/shard_map/ppermute | solution.py:502
  (6 other events, 129.2 us)

commit v3 on v2

--- a/solution.py
+++ b/solution.py
@@ -97,7 +97,7 @@
     for s, out in enumerate(outs):
         h = lax.rem(z + s, HEADS)
         at = lanes(h)
-        kb, vb = bias[:, lanes(20 + h)].astype(f32), bias[:, lanes(24 + h)].astype(f32)
+        kb, vb = bias[pl.ds(20 + h, 1), :], bias[pl.ds(24 + h, 1), :]
         out[0:64, :] = rotate(pk[:, at].astype(f32) + kb, *prompt_turn).astype(bf16)
         out[64:128, :] = (pv[:, at].astype(f32) + vb).astype(bf16)
         out[128:144, :] = note
@@ -116,7 +116,7 @@
         h = lax.rem(z + s, HEADS) * GROUP
         for m in range(GROUP):
             at = lanes(h + m)
-            qb = bias[:, at].astype(f32)
+            qb = bias[pl.ds(h + m, 1), :]
             o = m * ROWS
             out[o : o + 64, :] = rotate(pq[:, at].astype(f32) + qb, *prompt_turn).astype(bf16)
             o += STRIPE
@@ -140,11 +140,12 @@
     return [pl.ds(pl.multiple_of(row, 256), 256) for row in pair]
 
 
-def prompt_block_of(sc, i, count, pk, pv, start, place):
-    rows = prompt_rows(sc, jnp.minimum(i, PROMPT // BLOCK - 1))
-    key = i * BLOCK + lax.broadcasted_iota(jnp.int32, (BLOCK, STRIPE), 0)
+def prompt_block_of(sc, i, there, pk, pv, start, place):
+    rows = prompt_rows(sc, i)
+    key = lax.broadcasted_iota(jnp.int32, (BLOCK, STRIPE), 0)
+    start, place = start - i * BLOCK, jnp.where(there, place - i * BLOCK, -1)
     k, v = [jnp.concatenate([ref[at, :] for at in rows], axis=0) for ref in (pk, pv)]
-    return k, v, (key >= start) & (key <= jnp.where(i < count, place, -1))
+    return k, v, (key >= start) & (key <= place)
 
 
 def prompt_limits(sc, j, start):
@@ -160,8 +161,8 @@
 
 
 def reply_seen(sc, key_at, place):
-    key = key_at + lax.broadcasted_iota(jnp.int32, (BLOCK, place.shape[1]), 0)
-    return (key < sc[4]) & (key <= place)
+    key = lax.broadcasted_iota(jnp.int32, (BLOCK, place.shape[1]), 0)
+    return key <= jnp.minimum(place, sc[4] - 1) - key_at
 
 
 def prompt_places(sc, j):
@@ -197,7 +198,8 @@
     q_in, kv_in, tables = refs[0:4], refs[4:12], refs[12:16]
     back, keep, send = refs[16:20], refs[20], refs[21]
     (pq, pg, rq, rg, pk, pv, rk, rv, r_stat, p_stat, pdq, rdq, pdk, pdv, rdk, rdv,
-     stat_m, stat_l, acc_r, p_out, r_out, note, bias) = refs[22:]
+     stat_m, stat_l, acc_r, p_out, r_out, note, bias, seen_from) = refs[22:46]
+    p_top, p_total, p_acc = refs[46:48], refs[48:50], refs[50:52]
     z, x, core, b, length = sc[0], sc[1], sc[2], sc[3], sc[4]
 
     for s in range(4):
@@ -236,10 +238,10 @@
     q_all = rq[...]
 
     def forward_reply(i, state):
-        at = pl.ds(pl.multiple_of(i * BLOCK, BLOCK), BLOCK)
+        at = pl.ds(pl.multiple_of(i * 2 * BLOCK, 2 * BLOCK), 2 * BLOCK)
         return online(state, q_all, pk[at, :], pv[at, :], None)
 
-    top, total, acc = lax.fori_loop(0, PROMPT // BLOCK, forward_reply, empty(4 * STRIPE))
+    top, total, acc = lax.fori_loop(0, PROMPT // BLOCK // 2, forward_reply, empty(4 * STRIPE), unroll=2)
     half = 2 * STRIPE
     for i in range(4):
         at = slice(i * BLOCK, (i + 1) * BLOCK)
@@ -264,37 +266,66 @@
     acc_r[...] = out
     r_out[...] = acc_r[...].T
 
-    limits, seen_from, places = [], [], []
+    lows, ends, total_blocks = [], [], 0
     for j in range(4):
         ids = note[j, 1:2, :].astype(jnp.int32)
         start = jnp.zeros((1, HD), jnp.int32)
         for s in range(1, HEADS):
             start = jnp.where(ids == s, starts[s], start)
-        limits.append(prompt_limits(sc, j, start))
-        seen_from.append(jnp.concatenate([start, start, start[:, :64]], axis=1))
-        places.append(prompt_places(sc, j))
-    stripes = [slice(j * STRIPE, (j + 1) * STRIPE) for j in range(4)]
-    for pair in ((0, 1), (2, 3)):
-
-        def forward_prompt(i, states, pair=pair):
-            out = []
-            for j, state in zip(pair, states):
-                low, high = limits[j]
-                k, v, seen = prompt_block_of(
-                    sc, low + i, high, pk, pv, seen_from[j], places[j]
-                )
-                out.append(online(state, pq[stripes[j], :], k, v, seen))
-            return tuple(out)
-
-        steps = jnp.maximum(*[limits[j][1] - limits[j][0] for j in pair])
-        states = lax.fori_loop(0, steps, forward_prompt, (empty(STRIPE),) * 2)
-        for j, (top, total, acc) in zip(pair, states):
-            out = (acc / total).astype(bf16).astype(f32)
-            p_stat[j, 0:1, :] = top + jnp.log2(total)
-            p_stat[j, 1:2, :] = jnp.sum(
-                out * pg[stripes[j], :].astype(f32).T, axis=0, keepdims=True
-            )
-            p_out[stripes[j], :] = out.T
+        low, high = prompt_limits(sc, j, start)
+        lows.append(low)
+        total_blocks = total_blocks + high - low
+        ends.append(total_blocks)
+        seen_from[j, 0:1, :] = jnp.concatenate([start, start, start[:, :64]], axis=1)
+    half_list = (total_blocks + 1) // 2
+
+    def listed(i, side):
+        n = i + side * half_list
+        j, low, before = 0, lows[0], 0
+        for k in range(3):
+            later = n >= ends[k]
+            j = jnp.where(later, k + 1, j)
+            low = jnp.where(later, lows[k + 1], low)
+            before = jnp.where(later, ends[k], before)
+        there = n < total_blocks
+        return j, jnp.where(there, low + n - before, 0), there
+
+    def stripe_rows(j):
+        return pl.ds(pl.multiple_of(j * STRIPE, STRIPE), STRIPE)
+
+    def seen_block(j, block, there):
+        return prompt_block_of(
+            sc, block, there, pk, pv, seen_from[j, 0:1, :], prompt_places(sc, j)
+        )
+
+    for side in range(2):
+        p_top[side][...] = jnp.full_like(p_top[side], LOW)
+        p_total[side][...] = jnp.zeros_like(p_total[side])
+        p_acc[side][...] = jnp.zeros_like(p_acc[side])
+
+    def forward_prompt(i, carry):
+        for side in range(2):
+            j, block, there = listed(i, side)
+            k, v, seen = seen_block(j, block, there)
+            state = p_top[side][j, 0:1, :], p_total[side][j, 0:1, :], p_acc[side][j]
+            top, total, acc = online(state, pq[stripe_rows(j), :], k, v, seen)
+            p_top[side][j, 0:1, :] = top
+            p_total[side][j, 0:1, :] = total
+            p_acc[side][j] = acc
+        return carry
+
+    lax.fori_loop(0, half_list, forward_prompt, 0)
+    for j in range(4):
+        rows = slice(j * STRIPE, (j + 1) * STRIPE)
+        tops = [p_top[side][j, 0:1, :] for side in range(2)]
+        top = jnp.maximum(*tops)
+        shrinks = [jnp.exp2(t - top) for t in tops]
+        total = sum(p_total[side][j, 0:1, :] * shrinks[side] for side in range(2))
+        acc = sum(p_acc[side][j] * shrinks[side] for side in range(2))
+        out = (acc / total).astype(bf16).astype(f32)
+        p_stat[j, 0:1, :] = top + jnp.log2(total)
+        p_stat[j, 1:2, :] = jnp.sum(out * pg[rows, :].astype(f32).T, axis=0, keepdims=True)
+        p_out[rows, :] = out.T
     for s in range(4):
         at = pl.ds(pl.multiple_of(lax.rem(z + 4 - s, 4) * STRIPE, STRIPE), STRIPE)
         back[s][0:STRIPE, :] = p_out[at, :].astype(bf16)
@@ -314,28 +345,26 @@
         rdq[...] += dq
         return carry
 
-    lax.fori_loop(0, PROMPT // BLOCK, backward_reply, 0)
-    for pair in ((0, 1), (2, 3)):
-
-        def backward_prompt(i, carry, pair=pair):
-            done = []
-            for j in pair:
-                low, high = limits[j]
-                k, v, seen = prompt_block_of(sc, low + i, high, pk, pv, seen_from[j], places[j])
-                done.append(
-                    grads(pq[stripes[j], :], pg[stripes[j], :], p_stat[j, 0:1, :],
-                          p_stat[j, 1:2, :], k, v, seen)
-                )
-            for j, (dk, dv, dq) in zip(pair, done):
-                at = jnp.minimum(limits[j][0] + i, PROMPT // BLOCK - 1)
-                for n, rows in enumerate(prompt_rows(sc, at)):
-                    pdk[rows, :] += dk[n * 256 : (n + 1) * 256, :]
-                    pdv[rows, :] += dv[n * 256 : (n + 1) * 256, :]
-                pdq[stripes[j], :] += dq
-            return carry
-
-        steps = jnp.maximum(*[limits[j][1] - limits[j][0] for j in pair])
-        lax.fori_loop(0, steps, backward_prompt, 0)
+    lax.fori_loop(0, PROMPT // BLOCK, backward_reply, 0, unroll=2)
+
+    def backward_prompt(i, carry):
+        done = []
+        for side in range(2):
+            j, block, there = listed(i, side)
+            k, v, seen = seen_block(j, block, there)
+            rows = stripe_rows(j)
+            terms = grads(
+                pq[rows, :], pg[rows, :], p_stat[j, 0:1, :], p_stat[j, 1:2, :], k, v, seen
+            )
+            done.append((rows, prompt_rows(sc, block), terms))
+        for rows, keys, (dk, dv, dq) in done:
+            for n, at in enumerate(keys):
+                pdk[at, :] += dk[n * 256 : (n + 1) * 256, :]
+                pdv[at, :] += dv[n * 256 : (n + 1) * 256, :]
+            pdq[rows, :] += dq
+        return carry
+
+    lax.fori_loop(0, half_list, backward_prompt, 0)
     for i in range(4):
         at = slice(i * BLOCK, (i + 1) * BLOCK)
         cols = slice(0 if i < 2 else half, 4 * STRIPE)
@@ -507,7 +536,7 @@
         [lax.axis_index(a) for a in ("z", "x", "core", "branch")] + [lengths[0, 0]]
     ).astype(jnp.int32)
     tables = angle_tables()
-    bias = jnp.concatenate([qbias, kbias, vbias])[None]
+    bias = jnp.concatenate([qbias, kbias, vbias]).astype(f32).reshape(-1, HD)
     kv = call(prepare_kv_body, 10, [((OWN, HD), bf16)] * 4, mib=56)(
         sc, pk[0], pv[0], rk[0, 0], rv[0, 0], bias, segments, *tables
     )
@@ -538,7 +567,10 @@
         + [pltpu.VMEM((8, rows), f32)] * 2
         + [pltpu.VMEM((HD, rows), f32)]
         + [pltpu.VMEM((rows, HD), f32)] * 2
-        + [pltpu.VMEM((4, 16, HD), f32), pltpu.VMEM((8, HD), f32)],
+        + [pltpu.VMEM((4, 16, HD), f32), pltpu.VMEM((8, HD), f32)]
+        + [pltpu.VMEM((4, 8, STRIPE), jnp.int32)]
+        + [pltpu.VMEM((4, 8, STRIPE), f32)] * 4
+        + [pltpu.VMEM((4, HD, STRIPE), f32)] * 2,
         us=60,
         mib=40,
     )(sc, *q, *pieces, *tables)

time: 155 us -> 152 us (0.981)
  Pallas kernels: 60.7 us -> 55.7 us
  waiting for transfers between devices: 38.7 us -> 41.5 us
  starting transfers between devices: 49.8 us -> 47.6 us
    pallas_call x1, Pallas kernels: 51.7 us -> 46.7 us  [on_device(): call(attend_body, 16, [((rows, HD), bf16)] * 4 + [((4 * TERMS + 16, HD),...]
    ppermute x29, waiting for transfers between devices: 38.7 us -> 41.5 us  [shift(): return lax.ppermute(v, axis, [(i, (i + s) % n) for i in range(n)])]
    ppermute x29, starting transfers between devices: 49.8 us -> 47.6 us  [shift(): return lax.ppermute(v, axis, [(i, (i + s) % n) for i in range(n)])]
where the time goes in v3:
time: 152 us; the launch traced here: 151 us
  Pallas kernels  55.7 us (37%)
  starting transfers between devices  47.6 us (31%)
  waiting for transfers between devices  41.5 us (27%)
  other arithmetic  2.91 us (2%)
  local copies, waits for them, and re-layouts  1.61 us (1%)
    ppermute x29, starting transfers between devices, shift(): return lax.ppermute(v, axis, [(i, (i + s) % n) for i in range(n)])  47.6 us
    pallas_call x1, Pallas kernels, on_device(): call(attend_body, 16, [((rows, HD), bf16)] * 4 + [((4 * TERMS + 16, HD),...  46.7 us
    ppermute x29, waiting for transfers between devices, shift(): return lax.ppermute(v, axis, [(i, (i + s) % n) for i in range(n)])  41.5 us
  transfers between devices with their start and end apart: 29, of which 17 were waited for; matrix products, arithmetic and copies ran while one was open for 0% of the time, Pallas kernels for 3%

profile of v3, /device:TPU:0, one launch (start us, length us, event | category | flops | bytes accessed | tf_op | source)
XLA Modules:
  0.0 150.8 jit_solution(925824760766031664)
XLA Ops:
  1.3 1.3 fusion.bias
  3.2 1.9 %shard_map.248 = (bf16[272,128]{1,0:T(8,128)(2,1)}, bf16[272,128]{1,0:T(8,128)(2,1)}, bf16[272,128]{1,0:T(8,128)(2,1)}, bf16[272,128]{1,0:T(8,128)(2,1)}) custom-call(s32[5]{0:T(128)} %stack.34.sc, bf16[64,512]{1,0:T(8,128)(2,1)} %bitcast.46, bf16[64,512]{1,0:T(8,128)(2,1)} %bitcast.47, bf16[64,512]{1,0:T(8,128)(2,1)} %bitcast.48, bf16[64,512]{1,0:T(8,128)(2,1)} %bitcast.49, ...), custom_call_target="tpu_custom_call" | custom-call | flops 1000000 | bytes 3000000 | tf_op jit(solution)/shard_map/pallas_call | solution.py:540
  5.1 2.0 %collective-permute-start = (bf16[272,128]{1,0:T(8,128)(2,1)}, bf16[272,128]{1,0:T(8,128)(2,1)S(1)}, u32[]{:S(2)}, u32[]{:S(2)}) collective-permute-start(bf16[272,128]{1,0:T(8,128)(2,1)} %get-tuple-element.60), channel_id=1, source_target_pairs={{0,16},{16,32},{32,48},{48,0},{1,17},{17,33},{33,49},{49,1},{2,18}... | collective-permute-start | bytes 208904 | tf_op jit(solution)/shard_map/ppermute | solution.py:531
  7.1 3.6 %collective-permute-start.1 = (bf16[272,128]{1,0:T(8,128)(2,1)}, bf16[272,128]{1,0:T(8,128)(2,1)S(1)}, u32[]{:S(2)}, u32[]{:S(2)}) collective-permute-start(bf16[272,128]{1,0:T(8,128)(2,1)} %get-tuple-element.61), channel_id=1, source_target_pairs={{0,32},{16,48},{32,0},{48,16},{1,33},{17,49},{33,1},{49,17},{2,34}... | collective-permute-start | bytes 208904 | tf_op jit(solution)/shard_map/ppermute | solution.py:531
  11.8 2.7 %shard_map.249 = (bf16[1280,128]{1,0:T(8,128)(2,1)}, bf16[1280,128]{1,0:T(8,128)(2,1)}, bf16[1280,128]{1,0:T(8,128)(2,1)}, bf16[1280,128]{1,0:T(8,128)(2,1)}) custom-call(s32[5]{0:T(128)} %stack.34.sc, bf16[64,2560]{1,0:T(8,128)(2,1)} %bitcast.37, bf16[64,2560]{1,0:T(8,128)(2,1)} %bitcast.38, bf16[64,2560]{1,0:T(8,128)(2,1)} %bitcast.39, ...), custom_call_target="tpu_custom_call" | custom-call | flops 1000000 | bytes 3000000 | tf_op jit(solution)/shard_map/pallas_call | solution.py:543
  16.2 3.3 %collective-permute-start.3 = (bf16[576,128]{1,0:T(8,128)(2,1)S(1)}, bf16[576,128]{1,0:T(8,128)(2,1)S(1)}, u32[]{:S(2)}, u32[]{:S(2)}) collective-permute-start(bf16[576,128]{1,0:T(8,128)(2,1)S(1)} %bitcast.41), channel_id=1, source_target_pairs={{0,1},{1,0},{2,3},{3,2},{4,5},{5,4},{6,7},{7,6},{8,9},{9,8},{10,11... | collective-permute-start | bytes 442376 | tf_op jit(solution)/shard_map/ppermute | solution.py:531
  19.8 3.1 %collective-permute-done.3 = bf16[576,128]{1,0:T(8,128)(2,1)S(1)} collective-permute-done((bf16[576,128]{1,0:T(8,128)(2,1)S(1)}, bf16[576,128]{1,0:T(8,128)(2,1)S(1)}, u32[]{:S(2)}, u32[]{:S(2)}) %collective-permute-start.3) | collective-permute-done | bytes 147488 | tf_op jit(solution)/shard_map/ppermute | solution.py:531
  22.9 3.1 %collective-permute-start.4 = (bf16[1664,128]{1,0:T(8,128)(2,1)S(1)}, bf16[1664,128]{1,0:T(8,128)(2,1)S(1)}, u32[]{:S(2)}, u32[]{:S(2)}) collective-permute-start(bf16[1664,128]{1,0:T(8,128)(2,1)S(1)} %pad_maximum_fusion.refs_4_), channel_id=1, source_target_pairs={{0,8},{4,12},{8,0},{12,4},{1,9},{5,13},{9,1},{13,5},{2,10},{6,14},... | collective-permute-start | bytes 1277960 | tf_op jit(solution)/shard_map/ppermute | solution.py:531
  26.1 1.1 collective-permute-start.12
  28.1 1.5 %collective-permute-start.6 = (bf16[1280,128]{1,0:T(8,128)(2,1)S(1)}, bf16[1280,128]{1,0:T(8,128)(2,1)S(1)}, u32[]{:S(2)}, u32[]{:S(2)}) collective-permute-start(bf16[1280,128]{1,0:T(8,128)(2,1)S(1)} %copy-done.8), channel_id=1, source_target_pairs={{0,32},{16,48},{32,0},{48,16},{1,33},{17,49},{33,1},{49,17},{2,34}... | collective-permute-start | bytes 983048 | tf_op jit(solution)/shard_map/ppermute | solution.py:531
  29.6 1.5 %collective-permute-start.7 = (bf16[1280,128]{1,0:T(8,128)(2,1)S(1)}, bf16[1280,128]{1,0:T(8,128)(2,1)S(1)}, u32[]{:S(2)}, u32[]{:S(2)}) collective-permute-start(bf16[1280,128]{1,0:T(8,128)(2,1)S(1)} %copy-done.7), channel_id=1, source_target_pairs={{0,48},{16,0},{32,16},{48,32},{1,49},{17,1},{33,17},{49,33},{2,50}... | collective-permute-start | bytes 983048 | tf_op jit(solution)/shard_map/ppermute | solution.py:531
  31.1 5.5 %collective-permute-done.6.refs_2_ = bf16[1280,128]{1,0:T(8,128)(2,1)S(1)} collective-permute-done((bf16[1280,128]{1,0:T(8,128)(2,1)S(1)}, bf16[1280,128]{1,0:T(8,128)(2,1)S(1)}, u32[]{:S(2)}, u32[]{:S(2)}) %collective-permute-start.6) | collective-permute-done | bytes 327712 | tf_op jit(solution)/shard_map/ppermute | solution.py:531
  36.7 5.6 %collective-permute-done.7.refs_3_ = bf16[1280,128]{1,0:T(8,128)(2,1)S(1)} collective-permute-done((bf16[1280,128]{1,0:T(8,128)(2,1)S(1)}, bf16[1280,128]{1,0:T(8,128)(2,1)S(1)}, u32[]{:S(2)}, u32[]{:S(2)}) %collective-permute-start.7) | collective-permute-done | bytes 327712 | tf_op jit(solution)/shard_map/ppermute | solution.py:531
  43.4 1.2 collective-permute-done.13.refs_11_
  45.9 46.7 %shard_map.250 = (bf16[1280,128]{1,0:T(8,128)(2,1)S(1)}, bf16[1280,128]{1,0:T(8,128)(2,1)S(1)}, bf16[1280,128]{1,0:T(8,128)(2,1)S(1)}, bf16[1280,128]{1,0:T(8,12...) custom-call(s32[5]{0:T(128)S(1)} %copy-done.6, bf16[1280,128]{1,0:T(8,128)(2,1)S(1)} %copy-done.4, ...), custom_call_target="tpu_custom_call" | custom-call | flops 60000000 | bytes 180000000 | tf_op jit(solution)/shard_map/pallas_call | solution.py:556
  92.8 2.3 %collective-permute-start.14 = (bf16[1280,128]{1,0:T(8,128)(2,1)S(1)}, bf16[1280,128]{1,0:T(8,128)(2,1)S(1)}, u32[]{:S(2)}, u32[]{:S(2)}) collective-permute-start(bf16[1280,128]{1,0:T(8,128)(2,1)S(1)} %get-tuple-element.78), channel_id=1, source_target_pairs={{0,48},{16,0},{32,16},{48,32},{1,49},{17,1},{33,17},{49,33},{2,50}... | collective-permute-start | bytes 983048 | tf_op jit(solution)/shard_map/ppermute | solution.py:531
  96.4 1.4 collective-permute-start.18
  97.9 6.5 %collective-permute-start.19 = (bf16[1536,128]{1,0:T(8,128)(2,1)S(1)}, bf16[1536,128]{1,0:T(8,128)(2,1)S(1)}, u32[]{:S(2)}, u32[]{:S(2)}) collective-permute-start(bf16[1536,128]{1,0:T(8,128)(2,1)S(1)} %get-tuple-element.88), channel_id=1, source_target_pairs={{0,8},{4,12},{8,0},{12,4},{1,9},{5,13},{9,1},{13,5},{2,10},{6,14},... | collective-permute-start | bytes 1179656 | tf_op jit(solution)/shard_map/ppermute | solution.py:531
  104.4 2.5 %collective-permute-start.20 = (bf16[1536,128]{1,0:T(8,128)(2,1)S(1)}, bf16[1536,128]{1,0:T(8,128)(2,1)S(1)}, u32[]{:S(2)}, u32[]{:S(2)}) collective-permute-start(bf16[1536,128]{1,0:T(8,128)(2,1)S(1)} %get-tuple-element.89), channel_id=1, source_target_pairs={{0,12},{4,0},{8,4},{12,8},{1,13},{5,1},{9,5},{13,9},{2,14},{6,2},{... | collective-permute-start | bytes 1179656 | tf_op jit(solution)/shard_map/ppermute | solution.py:531
  106.9 1.5 collective-permute-start.15
  108.4 2.1 %collective-permute-done.21 = f32[8,128]{1,0:T(8,128)S(1)} collective-permute-done((f32[8,128]{1,0:T(8,128)S(1)}, f32[8,128]{1,0:T(8,128)S(1)}, u32[]{:S(2)}, u32[]{:S(2)}) %collective-permute-start.21) | collective-permute-done | bytes 4128 | tf_op jit(solution)/shard_map/ppermute | solution.py:531
  111.4 7.7 %collective-permute-done.15.refs_2_ = bf16[1280,128]{1,0:T(8,128)(2,1)S(1)} collective-permute-done((bf16[1280,128]{1,0:T(8,128)(2,1)S(1)}, bf16[1280,128]{1,0:T(8,128)(2,1)S(1)}, u32[]{:S(2)}, u32[]{:S(2)}) %collective-permute-start.15) | collective-permute-done | bytes 327712 | tf_op jit(solution)/shard_map/ppermute | solution.py:531
  119.1 1.2 collective-permute-start.24
  120.4 4.0 %collective-permute-done.16.refs_3_ = bf16[1280,128]{1,0:T(8,128)(2,1)S(1)} collective-permute-done((bf16[1280,128]{1,0:T(8,128)(2,1)S(1)}, bf16[1280,128]{1,0:T(8,128)(2,1)S(1)}, u32[]{:S(2)}, u32[]{:S(2)}) %collective-permute-start.16) | collective-permute-done | bytes 327712 | tf_op jit(solution)/shard_map/ppermute | solution.py:531
  124.4 4.0 %collective-permute-start.23 = (f32[8,128]{1,0:T(8,128)S(1)}, f32[8,128]{1,0:T(8,128)S(1)}, u32[]{:S(2)}, u32[]{:S(2)}) collective-permute-start(f32[8,128]{1,0:T(8,128)S(1)} %add.3.b0), channel_id=1, source_target_pairs={{0,8},{4,12},{8,0},{12,4},{1,9},{5,13},{9,1},{13,5},{2,10},{6,14},... | collective-permute-start | bytes 12296 | tf_op jit(solution)/shard_map/ppermute | solution.py:531
  128.4 1.9 %shard_map.251 = (bf16[64,2560]{1,0:T(8,128)(2,1)}, bf16[64,2560]{1,0:T(8,128)(2,1)}, bf16[64,2560]{1,0:T(8,128)(2,1)}, bf16[64,2560]{1,0:T(8,128)(2,1)}) custom-call(s32[5]{0:T(128)S(1)} %copy-done.6, bf16[1280,128]{1,0:T(8,128)(2,1)S(1)} %get-tuple-element.77.refs_0_, bf16[1280,128]{1,0:T(8,128)(2,1)S(1)} %collective-permute-done.14.refs_1_, ...), custom_call_target="tpu_custom_call" | custom-call | flops 2000000 | bytes 6000000 | tf_op jit(solution)/shard_map/pallas_call | solution.py:590
  130.3 2.9 %collective-permute-done.22.b1 = f32[8,128]{1,0:T(8,128)S(1)} collective-permute-done((f32[8,128]{1,0:T(8,128)S(1)}, f32[8,128]{1,0:T(8,128)S(1)}, u32[]{:S(2)}, u32[]{:S(2)}) %collective-permute-start.22) | collective-permute-done | bytes 4128 | tf_op jit(solution)/shard_map/ppermute | solution.py:531
  134.4 3.3 %collective-permute-start.25 = (bf16[528,128]{1,0:T(8,128)(2,1)S(1)}, bf16[528,128]{1,0:T(8,128)(2,1)S(1)}, u32[]{:S(2)}, u32[]{:S(2)}) collective-permute-start(bf16[528,128]{1,0:T(8,128)(2,1)S(1)} %get-tuple-element.93), channel_id=1, source_target_pairs={{0,1},{1,0},{2,3},{3,2},{4,5},{5,4},{6,7},{7,6},{8,9},{9,8},{10,11... | collective-permute-start | bytes 405512 | tf_op jit(solution)/shard_map/ppermute | solution.py:531
  137.6 3.3 %collective-permute-done.25.p_far = bf16[528,128]{1,0:T(8,128)(2,1)S(1)} collective-permute-done((bf16[528,128]{1,0:T(8,128)(2,1)S(1)}, bf16[528,128]{1,0:T(8,128)(2,1)S(1)}, u32[]{:S(2)}, u32[]{:S(2)}) %collective-permute-start.25) | collective-permute-done | bytes 135200 | tf_op jit(solution)/shard_map/ppermute | solution.py:531
  142.4 1.6 %collective-permute-start.27 = (bf16[272,128]{1,0:T(8,128)(2,1)S(1)}, bf16[272,128]{1,0:T(8,128)(2,1)S(1)}, u32[]{:S(2)}, u32[]{:S(2)}) collective-permute-start(bf16[272,128]{1,0:T(8,128)(2,1)S(1)} %get-tuple-element.97), channel_id=1, source_target_pairs={{0,32},{16,48},{32,0},{48,16},{1,33},{17,49},{33,1},{49,17},{2,34}... | collective-permute-start | bytes 208904 | tf_op jit(solution)/shard_map/ppermute | solution.py:531
  143.9 2.5 %collective-permute-start.28 = (bf16[272,128]{1,0:T(8,128)(2,1)S(1)}, bf16[272,128]{1,0:T(8,128)(2,1)S(1)}, u32[]{:S(2)}, u32[]{:S(2)}) collective-permute-start(bf16[272,128]{1,0:T(8,128)(2,1)S(1)} %get-tuple-element.98), channel_id=1, source_target_pairs={{0,48},{16,0},{32,16},{48,32},{1,49},{17,1},{33,17},{49,33},{2,50}... | collective-permute-start | bytes 208904 | tf_op jit(solution)/shard_map/ppermute | solution.py:531
  148.8 1.3 shard_map.255
  (59 shorter events, 14.9 us)
Async XLA Ops:
  5.1 9.3 %collective-permute-start = (bf16[272,128]{1,0:T(8,128)(2,1)}, bf16[272,128]{1,0:T(8,128)(2,1)S(1)}, u32[]{:S(2)}, u32[]{:S(2)}) collective-permute-start(bf16[272,128]{1,0:T(8,128)(2,1)} %get-tuple-element.60), channel_id=1, source_target_pairs={{0,16},{16,32},{32,48},{48,0},{1,17},{17,33},{33,49},{49,1},{2,18}... | collective-permute-start | bytes 208904 | tf_op jit(solution)/shard_map/ppermute | solution.py:531
  7.1 7.4 %collective-permute-start.1 = (bf16[272,128]{1,0:T(8,128)(2,1)}, bf16[272,128]{1,0:T(8,128)(2,1)S(1)}, u32[]{:S(2)}, u32[]{:S(2)}) collective-permute-start(bf16[272,128]{1,0:T(8,128)(2,1)} %get-tuple-element.61), channel_id=1, source_target_pairs={{0,32},{16,48},{32,0},{48,16},{1,33},{17,49},{33,1},{49,17},{2,34}... | collective-permute-start | bytes 208904 | tf_op jit(solution)/shard_map/ppermute | solution.py:531
  10.7 4.5 %collective-permute-start.2 = (bf16[272,128]{1,0:T(8,128)(2,1)}, bf16[272,128]{1,0:T(8,128)(2,1)S(1)}, u32[]{:S(2)}, u32[]{:S(2)}) collective-permute-start(bf16[272,128]{1,0:T(8,128)(2,1)} %get-tuple-element.62), channel_id=1, source_target_pairs={{0,48},{16,0},{32,16},{48,32},{1,49},{17,1},{33,17},{49,33},{2,50}... | collective-permute-start | bytes 208904 | tf_op jit(solution)/shard_map/ppermute | solution.py:531
  11.7 34.1 %copy-start.2 = (f32[64,128]{1,0:T(8,128)S(1)}, f32[64,128]{1,0:T(8,128)}, u32[]{:S(2)}) copy-start(f32[64,128]{1,0:T(8,128)} %constant.26.clone.t3.refs_15_) | copy-start | bytes 98308
  11.7 34.1 %copy-start.3 = (f32[64,128]{1,0:T(8,128)S(1)}, f32[64,128]{1,0:T(8,128)}, u32[]{:S(2)}) copy-start(f32[64,128]{1,0:T(8,128)} %constant.25.clone.t2.refs_14_) | copy-start | bytes 98308
  11.7 34.1 %copy-start.6 = (s32[5]{0:T(128)S(1)}, s32[5]{0:T(128)}, u32[]{:S(2)}) copy-start(s32[5]{0:T(128)} %stack.34.sc) | copy-start | bytes 64
  16.2 6.7 %collective-permute-start.3 = (bf16[576,128]{1,0:T(8,128)(2,1)S(1)}, bf16[576,128]{1,0:T(8,128)(2,1)S(1)}, u32[]{:S(2)}, u32[]{:S(2)}) collective-permute-start(bf16[576,128]{1,0:T(8,128)(2,1)S(1)} %bitcast.41), channel_id=1, source_target_pairs={{0,1},{1,0},{2,3},{3,2},{4,5},{5,4},{6,7},{7,6},{8,9},{9,8},{10,11... | collective-permute-start | bytes 442376 | tf_op jit(solution)/shard_map/ppermute | solution.py:531
  19.5 10.1 %collective-permute-start.5 = (bf16[1280,128]{1,0:T(8,128)(2,1)}, bf16[1280,128]{1,0:T(8,128)(2,1)S(1)}, u32[]{:S(2)}, u32[]{:S(2)}) collective-permute-start(bf16[1280,128]{1,0:T(8,128)(2,1)} %get-tuple-element.69), channel_id=1, source_target_pairs={{0,16},{16,32},{32,48},{48,0},{1,17},{17,33},{33,49},{49,1},{2,18}... | collective-permute-start | bytes 983048 | tf_op jit(solution)/shard_map/ppermute | solution.py:531
  22.9 19.3 %collective-permute-start.4 = (bf16[1664,128]{1,0:T(8,128)(2,1)S(1)}, bf16[1664,128]{1,0:T(8,128)(2,1)S(1)}, u32[]{:S(2)}, u32[]{:S(2)}) collective-permute-start(bf16[1664,128]{1,0:T(8,128)(2,1)S(1)} %pad_maximum_fusion.refs_4_), channel_id=1, source_target_pairs={{0,8},{4,12},{8,0},{12,4},{1,9},{5,13},{9,1},{13,5},{2,10},{6,14},... | collective-permute-start | bytes 1277960 | tf_op jit(solution)/shard_map/ppermute | solution.py:531
  26.1 16.8 %collective-permute-start.12 = (bf16[1664,128]{1,0:T(8,128)(2,1)S(1)}, bf16[1664,128]{1,0:T(8,128)(2,1)S(1)}, u32[]{:S(2)}, u32[]{:S(2)}) collective-permute-start(bf16[1664,128]{1,0:T(8,128)(2,1)S(1)} %pad_maximum_fusion.refs_4_), channel_id=1, source_target_pairs={{0,12},{4,0},{8,4},{12,8},{1,13},{5,1},{9,5},{13,9},{2,14},{6,2},{... | collective-permute-start | bytes 1277960 | tf_op jit(solution)/shard_map/ppermute | solution.py:531
  27.2 15.6 %collective-permute-start.9 = (bf16[1664,128]{1,0:T(8,128)(2,1)S(1)}, bf16[1664,128]{1,0:T(8,128)(2,1)S(1)}, u32[]{:S(2)}, u32[]{:S(2)}) collective-permute-start(bf16[1664,128]{1,0:T(8,128)(2,1)S(1)} %pad_maximum_fusion.refs_4_), channel_id=1, source_target_pairs={{0,4},{4,8},{8,12},{12,0},{1,5},{5,9},{9,13},{13,1},{2,6},{6,10},{... | collective-permute-start | bytes 1277960 | tf_op jit(solution)/shard_map/ppermute | solution.py:531
  28.1 8.6 %collective-permute-start.6 = (bf16[1280,128]{1,0:T(8,128)(2,1)S(1)}, bf16[1280,128]{1,0:T(8,128)(2,1)S(1)}, u32[]{:S(2)}, u32[]{:S(2)}) collective-permute-start(bf16[1280,128]{1,0:T(8,128)(2,1)S(1)} %copy-done.8), channel_id=1, source_target_pairs={{0,32},{16,48},{32,0},{48,16},{1,33},{17,49},{33,1},{49,17},{2,34}... | collective-permute-start | bytes 983048 | tf_op jit(solution)/shard_map/ppermute | solution.py:531
  29.6 12.7 %collective-permute-start.7 = (bf16[1280,128]{1,0:T(8,128)(2,1)S(1)}, bf16[1280,128]{1,0:T(8,128)(2,1)S(1)}, u32[]{:S(2)}, u32[]{:S(2)}) collective-permute-start(bf16[1280,128]{1,0:T(8,128)(2,1)S(1)} %copy-done.7), channel_id=1, source_target_pairs={{0,48},{16,0},{32,16},{48,32},{1,49},{17,1},{33,17},{49,33},{2,50}... | collective-permute-start | bytes 983048 | tf_op jit(solution)/shard_map/ppermute | solution.py:531
  36.7 6.7 %collective-permute-start.8 = (bf16[1664,128]{1,0:T(8,128)(2,1)S(1)}, bf16[1664,128]{1,0:T(8,128)(2,1)S(1)}, u32[]{:S(2)}, u32[]{:S(2)}) collective-permute-start(bf16[1664,128]{1,0:T(8,128)(2,1)S(1)} %pad_maximum_fusion.refs_4_), channel_id=1, source_target_pairs={{0,2},{2,0},{1,3},{3,1},{4,6},{6,4},{5,7},{7,5},{8,10},{10,8},{9,1... | collective-permute-start | bytes 1277960 | tf_op jit(solution)/shard_map/ppermute | solution.py:531
  42.8 1.8 %collective-permute-start.13 = (bf16[1664,128]{1,0:T(8,128)(2,1)S(1)}, bf16[1664,128]{1,0:T(8,128)(2,1)S(1)}, u32[]{:S(2)}, u32[]{:S(2)}) collective-permute-start(bf16[1664,128]{1,0:T(8,128)(2,1)S(1)} %collective-permute-done.12.refs_10_), channel_id=1, source_target_pairs={{0,2},{2,0},{1,3},{3,1},{4,6},{6,4},{5,7},{7,5},{8,10},{10,8},{9,1... | collective-permute-start | bytes 1277960 | tf_op jit(solution)/shard_map/ppermute | solution.py:531
  42.8 2.4 %collective-permute-start.10 = (bf16[1664,128]{1,0:T(8,128)(2,1)S(1)}, bf16[1664,128]{1,0:T(8,128)(2,1)S(1)}, u32[]{:S(2)}, u32[]{:S(2)}) collective-permute-start(bf16[1664,128]{1,0:T(8,128)(2,1)S(1)} %collective-permute-done.9.refs_6_), channel_id=1, source_target_pairs={{0,2},{2,0},{1,3},{3,1},{4,6},{6,4},{5,7},{7,5},{8,10},{10,8},{9,1... | collective-permute-start | bytes 1277960 | tf_op jit(solution)/shard_map/ppermute | solution.py:531
  43.3 2.5 %collective-permute-start.11 = (bf16[1664,128]{1,0:T(8,128)(2,1)S(1)}, bf16[1664,128]{1,0:T(8,128)(2,1)S(1)}, u32[]{:S(2)}, u32[]{:S(2)}) collective-permute-start(bf16[1664,128]{1,0:T(8,128)(2,1)S(1)} %collective-permute-done.4.refs_8_), channel_id=1, source_target_pairs={{0,2},{2,0},{1,3},{3,1},{4,6},{6,4},{5,7},{7,5},{8,10},{10,8},{9,1... | collective-permute-start | bytes 1277960 | tf_op jit(solution)/shard_map/ppermute | solution.py:531
  92.6 3.5 %collective-permute-start.17 = (bf16[6160,128]{1,0:T(8,128)(2,1)S(1)}, bf16[6160,128]{1,0:T(8,128)(2,1)S(1)}, u32[]{:S(2)}, u32[]{:S(2)}) collective-permute-start(bf16[6160,128]{1,0:T(8,128)(2,1)S(1)} %get-tuple-element.85), channel_id=1, source_target_pairs={{0,2},{2,0},{1,3},{3,1},{4,6},{6,4},{5,7},{7,5},{8,10},{10,8},{9,1... | collective-permute-start | bytes 4730888 | tf_op jit(solution)/shard_map/ppermute | solution.py:531
  92.8 14.1 %collective-permute-start.14 = (bf16[1280,128]{1,0:T(8,128)(2,1)S(1)}, bf16[1280,128]{1,0:T(8,128)(2,1)S(1)}, u32[]{:S(2)}, u32[]{:S(2)}) collective-permute-start(bf16[1280,128]{1,0:T(8,128)(2,1)S(1)} %get-tuple-element.78), channel_id=1, source_target_pairs={{0,48},{16,0},{32,16},{48,32},{1,49},{17,1},{33,17},{49,33},{2,50}... | collective-permute-start | bytes 983048 | tf_op jit(solution)/shard_map/ppermute | solution.py:531
  96.4 36.8 %collective-permute-start.18 = (bf16[1536,128]{1,0:T(8,128)(2,1)S(1)}, bf16[1536,128]{1,0:T(8,128)(2,1)S(1)}, u32[]{:S(2)}, u32[]{:S(2)}) collective-permute-start(bf16[1536,128]{1,0:T(8,128)(2,1)S(1)} %get-tuple-element.87), channel_id=1, source_target_pairs={{0,4},{4,8},{8,12},{12,0},{1,5},{5,9},{9,13},{13,1},{2,6},{6,10},{... | collective-permute-start | bytes 1179656 | tf_op jit(solution)/shard_map/ppermute | solution.py:531
  97.9 35.3 %collective-permute-start.19 = (bf16[1536,128]{1,0:T(8,128)(2,1)S(1)}, bf16[1536,128]{1,0:T(8,128)(2,1)S(1)}, u32[]{:S(2)}, u32[]{:S(2)}) collective-permute-start(bf16[1536,128]{1,0:T(8,128)(2,1)S(1)} %get-tuple-element.88), channel_id=1, source_target_pairs={{0,8},{4,12},{8,0},{12,4},{1,9},{5,13},{9,1},{13,5},{2,10},{6,14},... | collective-permute-start | bytes 1179656 | tf_op jit(solution)/shard_map/ppermute | solution.py:531
  104.4 28.8 %collective-permute-start.20 = (bf16[1536,128]{1,0:T(8,128)(2,1)S(1)}, bf16[1536,128]{1,0:T(8,128)(2,1)S(1)}, u32[]{:S(2)}, u32[]{:S(2)}) collective-permute-start(bf16[1536,128]{1,0:T(8,128)(2,1)S(1)} %get-tuple-element.89), channel_id=1, source_target_pairs={{0,12},{4,0},{8,4},{12,8},{1,13},{5,1},{9,5},{13,9},{2,14},{6,2},{... | collective-permute-start | bytes 1179656 | tf_op jit(solution)/shard_map/ppermute | solution.py:531
  106.9 3.6 %collective-permute-start.21 = (f32[8,128]{1,0:T(8,128)S(1)}, f32[8,128]{1,0:T(8,128)S(1)}, u32[]{:S(2)}, u32[]{:S(2)}) collective-permute-start(f32[8,128]{1,0:T(8,128)S(1)} %get-tuple-element.90), channel_id=1, source_target_pairs={{0,64},{64,0},{1,65},{65,1},{2,66},{66,2},{3,67},{67,3},{4,68},{68... | collective-permute-start | bytes 12296 | tf_op jit(solution)/shard_map/ppermute | solution.py:531
  106.9 12.2 %collective-permute-start.15 = (bf16[1280,128]{1,0:T(8,128)(2,1)S(1)}, bf16[1280,128]{1,0:T(8,128)(2,1)S(1)}, u32[]{:S(2)}, u32[]{:S(2)}) collective-permute-start(bf16[1280,128]{1,0:T(8,128)(2,1)S(1)} %get-tuple-element.79), channel_id=1, source_target_pairs={{0,32},{16,48},{32,0},{48,16},{1,33},{17,49},{33,1},{49,17},{2,34}... | collective-permute-start | bytes 983048 | tf_op jit(solution)/shard_map/ppermute | solution.py:531
  110.5 13.8 %collective-permute-start.16 = (bf16[1280,128]{1,0:T(8,128)(2,1)S(1)}, bf16[1280,128]{1,0:T(8,128)(2,1)S(1)}, u32[]{:S(2)}, u32[]{:S(2)}) collective-permute-start(bf16[1280,128]{1,0:T(8,128)(2,1)S(1)} %get-tuple-element.80), channel_id=1, source_target_pairs={{0,16},{16,32},{32,48},{48,0},{1,17},{17,33},{33,49},{49,1},{2,18}... | collective-permute-start | bytes 983048 | tf_op jit(solution)/shard_map/ppermute | solution.py:531
  119.1 9.3 %collective-permute-start.24 = (f32[8,128]{1,0:T(8,128)S(1)}, f32[8,128]{1,0:T(8,128)S(1)}, u32[]{:S(2)}, u32[]{:S(2)}) collective-permute-start(f32[8,128]{1,0:T(8,128)S(1)} %add.3.b0), channel_id=1, source_target_pairs={{0,12},{4,0},{8,4},{12,8},{1,13},{5,1},{9,5},{13,9},{2,14},{6,2},{... | collective-permute-start | bytes 12296 | tf_op jit(solution)/shard_map/ppermute | solution.py:531
  124.4 5.9 %collective-permute-start.23 = (f32[8,128]{1,0:T(8,128)S(1)}, f32[8,128]{1,0:T(8,128)S(1)}, u32[]{:S(2)}, u32[]{:S(2)}) collective-permute-start(f32[8,128]{1,0:T(8,128)S(1)} %add.3.b0), channel_id=1, source_target_pairs={{0,8},{4,12},{8,0},{12,4},{1,9},{5,13},{9,1},{13,5},{2,10},{6,14},... | collective-permute-start | bytes 12296 | tf_op jit(solution)/shard_map/ppermute | solution.py:531
  128.4 4.8 %collective-permute-start.22 = (f32[8,128]{1,0:T(8,128)S(1)}, f32[8,128]{1,0:T(8,128)S(1)}, u32[]{:S(2)}, u32[]{:S(2)}) collective-permute-start(f32[8,128]{1,0:T(8,128)S(1)} %add.3.b0), channel_id=1, source_target_pairs={{0,4},{4,8},{8,12},{12,0},{1,5},{5,9},{9,13},{13,1},{2,6},{6,10},{... | collective-permute-start | bytes 12296 | tf_op jit(solution)/shard_map/ppermute | solution.py:531
  134.4 6.6 %collective-permute-start.25 = (bf16[528,128]{1,0:T(8,128)(2,1)S(1)}, bf16[528,128]{1,0:T(8,128)(2,1)S(1)}, u32[]{:S(2)}, u32[]{:S(2)}) collective-permute-start(bf16[528,128]{1,0:T(8,128)(2,1)S(1)} %get-tuple-element.93), channel_id=1, source_target_pairs={{0,1},{1,0},{2,3},{3,2},{4,5},{5,4},{6,7},{7,6},{8,9},{9,8},{10,11... | collective-permute-start | bytes 405512 | tf_op jit(solution)/shard_map/ppermute | solution.py:531
  141.7 5.6 %collective-permute-start.26 = (bf16[272,128]{1,0:T(8,128)(2,1)S(1)}, bf16[272,128]{1,0:T(8,128)(2,1)S(1)}, u32[]{:S(2)}, u32[]{:S(2)}) collective-permute-start(bf16[272,128]{1,0:T(8,128)(2,1)S(1)} %get-tuple-element.96), channel_id=1, source_target_pairs={{0,16},{16,32},{32,48},{48,0},{1,17},{17,33},{33,49},{49,1},{2,18}... | collective-permute-start | bytes 208904 | tf_op jit(solution)/shard_map/ppermute | solution.py:531
  142.4 5.8 %collective-permute-start.27 = (bf16[272,128]{1,0:T(8,128)(2,1)S(1)}, bf16[272,128]{1,0:T(8,128)(2,1)S(1)}, u32[]{:S(2)}, u32[]{:S(2)}) collective-permute-start(bf16[272,128]{1,0:T(8,128)(2,1)S(1)} %get-tuple-element.97), channel_id=1, source_target_pairs={{0,32},{16,48},{32,0},{48,16},{1,33},{17,49},{33,1},{49,17},{2,34}... | collective-permute-start | bytes 208904 | tf_op jit(solution)/shard_map/ppermute | solution.py:531
  143.9 4.9 %collective-permute-start.28 = (bf16[272,128]{1,0:T(8,128)(2,1)S(1)}, bf16[272,128]{1,0:T(8,128)(2,1)S(1)}, u32[]{:S(2)}, u32[]{:S(2)}) collective-permute-start(bf16[272,128]{1,0:T(8,128)(2,1)S(1)} %get-tuple-element.98), channel_id=1, source_target_pairs={{0,48},{16,0},{32,16},{48,32},{1,49},{17,1},{33,17},{49,33},{2,50}... | collective-permute-start | bytes 208904 | tf_op jit(solution)/shard_map/ppermute | solution.py:531
  (6 other events, 129.3 us)

commit v4 on v3

--- a/solution.py
+++ b/solution.py
@@ -448,17 +448,21 @@
     return x[0:8] + x[8:16]
 
 
-def along_core_body(keep, got, near, p1, p2, p3, bias):
+def along_core_body(keep, got, near, *parts):
     at = slice(4 * TERMS, 4 * TERMS + 16)
-    bias[...] = one_word(keep[at, :]) + one_word(got[at, :])
-    for i, out in enumerate((near, p1, p2, p3)):
+    words = two_words(one_word(keep[at, :]) + one_word(got[at, :]))
+    for i, out in enumerate((near, *parts)):
         at = slice(i * TERMS, (i + 1) * TERMS)
-        out[...] = (keep[at, :].astype(f32) + got[at, :].astype(f32)).astype(out.dtype)
-
-
-def along_x_body(after, own, r1, r2, r3, b0, b1, b2, b3, p_own, r_own, p_far, bias):
-    total = own[...] + (r1[...].astype(f32) + r2[...].astype(f32) + r3[...].astype(f32))
-    words = two_words((b0[...] + b2[...]) + (b1[...] + b3[...]))
+        out[0:TERMS, :] = (keep[at, :].astype(f32) + got[at, :].astype(f32)).astype(out.dtype)
+        out[TERMS : TERMS + 16, :] = words.astype(out.dtype)
+
+
+def along_x_body(after, own, r1, r2, r3, p_own, r_own, p_far, bias):
+    total = own[0:TERMS, :] + (
+        r1[0:TERMS, :].astype(f32) + r2[0:TERMS, :].astype(f32) + r3[0:TERMS, :].astype(f32)
+    )
+    b0, b1, b2, b3 = [one_word(r[TERMS : TERMS + 16, :]) for r in (own, r1, r2, r3)]
+    words = two_words((b0 + b2) + (b1 + b3))
     p_own[...] = total[0:512]
     r_own[...] = total[1024:1536]
     p_far[0:512, :] = total[512:1024].astype(bf16)
@@ -466,10 +470,10 @@
     bias[...] = one_word(words)
 
 
-def settle_body(sc, p_own, r_own, p_far, b0, t0, t1, t2, t3, *outs):
+def settle_body(sc, p_own, r_own, p_far, b0, b2, b3, t0, t1, t2, t3, *outs):
     tables = (t0, t1, t2, t3)
     z = sc[0]
-    words = two_words(b0[...] + one_word(p_far[512:528, :]))
+    words = two_words((b0[...] + one_word(p_far[512:528, :])) + (b2[...] + b3[...]))
     for t, out in enumerate(outs):
         zz = lax.rem(z + t, 4)
         o = t * ROWS
@@ -575,32 +579,31 @@
         mib=40,
     )(sc, *q, *pieces, *tables)
     back, (keep, send) = outs[:4], outs[4:]
-    own, *parts, bias = call(
+    own, *parts = call(
         along_core_body,
         2,
-        [((TERMS, HD), f32)] + [((TERMS, HD), bf16)] * 3 + [((8, HD), f32)],
+        [((TERMS + 16, HD), f32)] + [((TERMS + 16, HD), bf16)] * 3,
         scalars=False,
         us=2,
     )(keep, shift(send, "core", 1))
     back = [back[0]] + [shift(back[s], "z", -s) for s in (1, 2, 3)]
     parts = [shift(parts[s - 1], "x", s) for s in (1, 2, 3)]
-    bias = bias + shift(bias, "dp", 1)
-    biases = [bias] + [shift(bias, "x", s) for s in (1, 2, 3)]
     wide = ((ROWS, HEADS * GROUP * HD), bf16)
     p_out, r_out, p_dq, r_dq = call(functools.partial(gather_heads_body, 1), 4, [wide] * 4, us=2)(
         sc, *back
     )
     p_own, r_own, p_far, bias = call(
         along_x_body,
-        9,
+        5,
         [((512, HD), f32)] * 2 + [((528, HD), bf16), ((8, HD), f32)],
         scalars=False,
         anywhere=(0,),
         us=2,
-    )(p_out, own, *parts, *biases)
+    )(p_out, own, *parts)
     p_far = shift(p_far, "branch", 1)
-    dkv = call(settle_body, 8, [((4 * ROWS + 16, HD), bf16)] * 4)(
-        sc, p_own, r_own, p_far, bias, *tables
+    across = lax.ppermute(bias, ("dp", "branch"), [(0, 3), (1, 2), (2, 1), (3, 0)])
+    dkv = call(settle_body, 10, [((4 * ROWS + 16, HD), bf16)] * 4)(
+        sc, p_own, r_own, p_far, bias, shift(bias, "dp", 1), across, *tables
     )
     dkv = [dkv[0]] + [shift(dkv[t], "z", t) for t in (1, 2, 3)]
     narrow = ((ROWS, HEADS * HD), bf16)

time: 152 us -> 149 us (0.980)
  starting transfers between devices: 47.6 us -> 42.6 us
  Pallas kernels: 55.7 us -> 58.5 us
    ppermute x29 -> x26, waiting for transfers between devices: 41.5 us -> 36.5 us  [shift(): return lax.ppermute(v, axis, [(i, (i + s) % n) for i in range(n)])]
    ppermute x29 -> x26, starting transfers between devices: 47.6 us -> 42.6 us  [shift(): return lax.ppermute(v, axis, [(i, (i + s) % n) for i in range(n)])]
    ppermute x0 -> x1, waiting for transfers between devices: none -> 4.53 us  [on_device(): lax.ppermute(bias, ('dp', 'branch'), [(0, 3), (1, 2), (2, 1), (3, 0)])]
    pallas_call x1, Pallas kernels: 46.7 us -> 49.5 us  [on_device(): call(attend_body, 16, [((rows, HD), bf16)] * 4 + [((4 * TERMS + 16, HD),...]
  transfers between devices with their start and end apart: 29 -> 27, of which waited for: 17 -> 14; matrix products, arithmetic and copies ran while one was open for 0% -> 0% of each run, Pallas kernels for 3% -> 3%
where the time goes in v4:
time: 149 us; the launch traced here: 148 us
  Pallas kernels  58.5 us (39%)
  starting transfers between devices  42.6 us (29%)
  waiting for transfers between devices  41 us (28%)
  other arithmetic  2.91 us (2%)
  local copies, waits for them, and re-layouts  1.61 us (1%)
    pallas_call x1, Pallas kernels, on_device(): call(attend_body, 16, [((rows, HD), bf16)] * 4 + [((4 * TERMS + 16, HD),...  49.5 us
    ppermute x26, starting transfers between devices, shift(): return lax.ppermute(v, axis, [(i, (i + s) % n) for i in range(n)])  42.6 us
    ppermute x26, waiting for transfers between devices, shift(): return lax.ppermute(v, axis, [(i, (i + s) % n) for i in range(n)])  36.5 us
    ppermute x1, waiting for transfers between devices, on_device(): lax.ppermute(bias, ('dp', 'branch'), [(0, 3), (1, 2), (2, 1), (3, 0)])  4.53 us
  transfers between devices with their start and end apart: 27, of which 14 were waited for; matrix products, arithmetic and copies ran while one was open for 0% of the time, Pallas kernels for 3%

profile of v4, /device:TPU:0, one launch (start us, length us, event | category | flops | bytes accessed | tf_op | source)
XLA Modules:
  0.0 148.0 jit_solution(10643599446581387388)
XLA Ops:
  1.3 1.3 fusion.bias
  3.2 1.9 %shard_map.248 = (bf16[272,128]{1,0:T(8,128)(2,1)}, bf16[272,128]{1,0:T(8,128)(2,1)}, bf16[272,128]{1,0:T(8,128)(2,1)}, bf16[272,128]{1,0:T(8,128)(2,1)}) custom-call(s32[5]{0:T(128)} %stack.34.sc, bf16[64,512]{1,0:T(8,128)(2,1)} %bitcast.46, bf16[64,512]{1,0:T(8,128)(2,1)} %bitcast.47, bf16[64,512]{1,0:T(8,128)(2,1)} %bitcast.48, bf16[64,512]{1,0:T(8,128)(2,1)} %bitcast.49, ...), custom_call_target="tpu_custom_call" | custom-call | flops 1000000 | bytes 3000000 | tf_op jit(solution)/shard_map/pallas_call | solution.py:544
  5.1 2.0 %collective-permute-start = (bf16[272,128]{1,0:T(8,128)(2,1)}, bf16[272,128]{1,0:T(8,128)(2,1)S(1)}, u32[]{:S(2)}, u32[]{:S(2)}) collective-permute-start(bf16[272,128]{1,0:T(8,128)(2,1)} %get-tuple-element.59), channel_id=1, source_target_pairs={{0,16},{16,32},{32,48},{48,0},{1,17},{17,33},{33,49},{49,1},{2,18}... | collective-permute-start | bytes 208904 | tf_op jit(solution)/shard_map/ppermute | solution.py:535
  7.1 3.6 %collective-permute-start.1 = (bf16[272,128]{1,0:T(8,128)(2,1)}, bf16[272,128]{1,0:T(8,128)(2,1)S(1)}, u32[]{:S(2)}, u32[]{:S(2)}) collective-permute-start(bf16[272,128]{1,0:T(8,128)(2,1)} %get-tuple-element.60), channel_id=1, source_target_pairs={{0,32},{16,48},{32,0},{48,16},{1,33},{17,49},{33,1},{49,17},{2,34}... | collective-permute-start | bytes 208904 | tf_op jit(solution)/shard_map/ppermute | solution.py:535
  10.7 1.0 collective-permute-start.2
  11.7 2.7 %shard_map.249 = (bf16[1280,128]{1,0:T(8,128)(2,1)}, bf16[1280,128]{1,0:T(8,128)(2,1)}, bf16[1280,128]{1,0:T(8,128)(2,1)}, bf16[1280,128]{1,0:T(8,128)(2,1)}) custom-call(s32[5]{0:T(128)} %stack.34.sc, bf16[64,2560]{1,0:T(8,128)(2,1)} %bitcast.37, bf16[64,2560]{1,0:T(8,128)(2,1)} %bitcast.38, bf16[64,2560]{1,0:T(8,128)(2,1)} %bitcast.39, ...), custom_call_target="tpu_custom_call" | custom-call | flops 1000000 | bytes 3000000 | tf_op jit(solution)/shard_map/pallas_call | solution.py:547
  16.1 3.3 %collective-permute-start.3 = (bf16[576,128]{1,0:T(8,128)(2,1)S(1)}, bf16[576,128]{1,0:T(8,128)(2,1)S(1)}, u32[]{:S(2)}, u32[]{:S(2)}) collective-permute-start(bf16[576,128]{1,0:T(8,128)(2,1)S(1)} %bitcast.41), channel_id=1, source_target_pairs={{0,1},{1,0},{2,3},{3,2},{4,5},{5,4},{6,7},{7,6},{8,9},{9,8},{10,11... | collective-permute-start | bytes 442376 | tf_op jit(solution)/shard_map/ppermute | solution.py:535
  19.8 3.1 %collective-permute-done.3 = bf16[576,128]{1,0:T(8,128)(2,1)S(1)} collective-permute-done((bf16[576,128]{1,0:T(8,128)(2,1)S(1)}, bf16[576,128]{1,0:T(8,128)(2,1)S(1)}, u32[]{:S(2)}, u32[]{:S(2)}) %collective-permute-start.3) | collective-permute-done | bytes 147488 | tf_op jit(solution)/shard_map/ppermute | solution.py:535
  22.9 3.1 %collective-permute-start.4 = (bf16[1664,128]{1,0:T(8,128)(2,1)S(1)}, bf16[1664,128]{1,0:T(8,128)(2,1)S(1)}, u32[]{:S(2)}, u32[]{:S(2)}) collective-permute-start(bf16[1664,128]{1,0:T(8,128)(2,1)S(1)} %pad_maximum_fusion.refs_4_), channel_id=1, source_target_pairs={{0,8},{4,12},{8,0},{12,4},{1,9},{5,13},{9,1},{13,5},{2,10},{6,14},... | collective-permute-start | bytes 1277960 | tf_op jit(solution)/shard_map/ppermute | solution.py:535
  26.0 1.1 collective-permute-start.12
  28.0 1.5 %collective-permute-start.6 = (bf16[1280,128]{1,0:T(8,128)(2,1)S(1)}, bf16[1280,128]{1,0:T(8,128)(2,1)S(1)}, u32[]{:S(2)}, u32[]{:S(2)}) collective-permute-start(bf16[1280,128]{1,0:T(8,128)(2,1)S(1)} %copy-done.8), channel_id=1, source_target_pairs={{0,32},{16,48},{32,0},{48,16},{1,33},{17,49},{33,1},{49,17},{2,34}... | collective-permute-start | bytes 983048 | tf_op jit(solution)/shard_map/ppermute | solution.py:535
  29.6 1.5 %collective-permute-start.7 = (bf16[1280,128]{1,0:T(8,128)(2,1)S(1)}, bf16[1280,128]{1,0:T(8,128)(2,1)S(1)}, u32[]{:S(2)}, u32[]{:S(2)}) collective-permute-start(bf16[1280,128]{1,0:T(8,128)(2,1)S(1)} %copy-done.7), channel_id=1, source_target_pairs={{0,48},{16,0},{32,16},{48,32},{1,49},{17,1},{33,17},{49,33},{2,50}... | collective-permute-start | bytes 983048 | tf_op jit(solution)/shard_map/ppermute | solution.py:535
  31.1 5.5 %collective-permute-done.6.refs_2_ = bf16[1280,128]{1,0:T(8,128)(2,1)S(1)} collective-permute-done((bf16[1280,128]{1,0:T(8,128)(2,1)S(1)}, bf16[1280,128]{1,0:T(8,128)(2,1)S(1)}, u32[]{:S(2)}, u32[]{:S(2)}) %collective-permute-start.6) | collective-permute-done | bytes 327712 | tf_op jit(solution)/shard_map/ppermute | solution.py:535
  36.6 5.6 %collective-permute-done.7.refs_3_ = bf16[1280,128]{1,0:T(8,128)(2,1)S(1)} collective-permute-done((bf16[1280,128]{1,0:T(8,128)(2,1)S(1)}, bf16[1280,128]{1,0:T(8,128)(2,1)S(1)}, u32[]{:S(2)}, u32[]{:S(2)}) %collective-permute-start.7) | collective-permute-done | bytes 327712 | tf_op jit(solution)/shard_map/ppermute | solution.py:535
  43.3 1.2 collective-permute-done.13.refs_11_
  45.8 49.5 %shard_map.250 = (bf16[1280,128]{1,0:T(8,128)(2,1)S(1)}, bf16[1280,128]{1,0:T(8,128)(2,1)S(1)}, bf16[1280,128]{1,0:T(8,128)(2,1)S(1)}, bf16[1280,128]{1,0:T(8,12...) custom-call(s32[5]{0:T(128)S(1)} %copy-done.6, bf16[1280,128]{1,0:T(8,128)(2,1)S(1)} %copy-done.4, ...), custom_call_target="tpu_custom_call" | custom-call | flops 60000000 | bytes 180000000 | tf_op jit(solution)/shard_map/pallas_call | solution.py:560
  95.5 2.2 %collective-permute-start.14 = (bf16[1280,128]{1,0:T(8,128)(2,1)S(1)}, bf16[1280,128]{1,0:T(8,128)(2,1)S(1)}, u32[]{:S(2)}, u32[]{:S(2)}) collective-permute-start(bf16[1280,128]{1,0:T(8,128)(2,1)S(1)} %get-tuple-element.77), channel_id=1, source_target_pairs={{0,48},{16,0},{32,16},{48,32},{1,49},{17,1},{33,17},{49,33},{2,50}... | collective-permute-start | bytes 983048 | tf_op jit(solution)/shard_map/ppermute | solution.py:535
  97.7 1.1 collective-permute-done.17.got
  99.1 1.4 collective-permute-start.18
  100.6 6.5 %collective-permute-start.19 = (bf16[1552,128]{1,0:T(8,128)(2,1)S(1)}, bf16[1552,128]{1,0:T(8,128)(2,1)S(1)}, u32[]{:S(2)}, u32[]{:S(2)}) collective-permute-start(bf16[1552,128]{1,0:T(8,128)(2,1)S(1)} %get-tuple-element.87), channel_id=1, source_target_pairs={{0,8},{4,12},{8,0},{12,4},{1,9},{5,13},{9,1},{13,5},{2,10},{6,14},... | collective-permute-start | bytes 1191944 | tf_op jit(solution)/shard_map/ppermute | solution.py:535
  107.1 2.5 %collective-permute-start.20 = (bf16[1552,128]{1,0:T(8,128)(2,1)S(1)}, bf16[1552,128]{1,0:T(8,128)(2,1)S(1)}, u32[]{:S(2)}, u32[]{:S(2)}) collective-permute-start(bf16[1552,128]{1,0:T(8,128)(2,1)S(1)} %get-tuple-element.88), channel_id=1, source_target_pairs={{0,12},{4,0},{8,4},{12,8},{1,13},{5,1},{9,5},{13,9},{2,14},{6,2},{... | collective-permute-start | bytes 1191944 | tf_op jit(solution)/shard_map/ppermute | solution.py:535
  109.6 1.5 collective-permute-start.15
  111.1 1.6 %collective-permute-start.16 = (bf16[1280,128]{1,0:T(8,128)(2,1)S(1)}, bf16[1280,128]{1,0:T(8,128)(2,1)S(1)}, u32[]{:S(2)}, u32[]{:S(2)}) collective-permute-start(bf16[1280,128]{1,0:T(8,128)(2,1)S(1)} %get-tuple-element.79), channel_id=1, source_target_pairs={{0,16},{16,32},{32,48},{48,0},{1,17},{17,33},{33,49},{49,1},{2,18}... | collective-permute-start | bytes 983048 | tf_op jit(solution)/shard_map/ppermute | solution.py:535
  112.7 9.1 %collective-permute-done.15.refs_2_ = bf16[1280,128]{1,0:T(8,128)(2,1)S(1)} collective-permute-done((bf16[1280,128]{1,0:T(8,128)(2,1)S(1)}, bf16[1280,128]{1,0:T(8,128)(2,1)S(1)}, u32[]{:S(2)}, u32[]{:S(2)}) %collective-permute-start.15) | collective-permute-done | bytes 327712 | tf_op jit(solution)/shard_map/ppermute | solution.py:535
  121.8 5.2 %collective-permute-done.16.refs_3_ = bf16[1280,128]{1,0:T(8,128)(2,1)S(1)} collective-permute-done((bf16[1280,128]{1,0:T(8,128)(2,1)S(1)}, bf16[1280,128]{1,0:T(8,128)(2,1)S(1)}, u32[]{:S(2)}, u32[]{:S(2)}) %collective-permute-start.16) | collective-permute-done | bytes 327712 | tf_op jit(solution)/shard_map/ppermute | solution.py:535
  127.0 1.9 %shard_map.251 = (bf16[64,2560]{1,0:T(8,128)(2,1)}, bf16[64,2560]{1,0:T(8,128)(2,1)}, bf16[64,2560]{1,0:T(8,128)(2,1)}, bf16[64,2560]{1,0:T(8,128)(2,1)}) custom-call(s32[5]{0:T(128)S(1)} %copy-done.6, bf16[1280,128]{1,0:T(8,128)(2,1)S(1)} %get-tuple-element.76.refs_0_, bf16[1280,128]{1,0:T(8,128)(2,1)S(1)} %collective-permute-done.14.refs_1_, ...), custom_call_target="tpu_custom_call" | custom-call | flops 2000000 | bytes 6000000 | tf_op jit(solution)/shard_map/pallas_call | solution.py:592
  130.1 3.3 %collective-permute-start.21 = (bf16[528,128]{1,0:T(8,128)(2,1)S(1)}, bf16[528,128]{1,0:T(8,128)(2,1)S(1)}, u32[]{:S(2)}, u32[]{:S(2)}) collective-permute-start(bf16[528,128]{1,0:T(8,128)(2,1)S(1)} %get-tuple-element.91), channel_id=1, source_target_pairs={{0,1},{1,0},{2,3},{3,2},{4,5},{5,4},{6,7},{7,6},{8,9},{9,8},{10,11... | collective-permute-start | bytes 405512 | tf_op jit(solution)/shard_map/ppermute | solution.py:535
  133.7 4.5 %collective-permute-done.23.b3 = f32[8,128]{1,0:T(8,128)S(1)} collective-permute-done((f32[8,128]{1,0:T(8,128)S(1)}, f32[8,128]{1,0:T(8,128)S(1)}, u32[]{:S(2)}, u32[]{:S(2)}) %collective-permute-start.23) | collective-permute-done | bytes 4128 | tf_op jit(solution)/shard_map/ppermute | solution.py:604
  139.0 2.1 %collective-permute-start.25 = (bf16[272,128]{1,0:T(8,128)(2,1)S(1)}, bf16[272,128]{1,0:T(8,128)(2,1)S(1)}, u32[]{:S(2)}, u32[]{:S(2)}) collective-permute-start(bf16[272,128]{1,0:T(8,128)(2,1)S(1)} %get-tuple-element.95), channel_id=1, source_target_pairs={{0,32},{16,48},{32,0},{48,16},{1,33},{17,49},{33,1},{49,17},{2,34}... | collective-permute-start | bytes 208904 | tf_op jit(solution)/shard_map/ppermute | solution.py:535
  141.1 2.0 %collective-permute-start.26 = (bf16[272,128]{1,0:T(8,128)(2,1)S(1)}, bf16[272,128]{1,0:T(8,128)(2,1)S(1)}, u32[]{:S(2)}, u32[]{:S(2)}) collective-permute-start(bf16[272,128]{1,0:T(8,128)(2,1)S(1)} %get-tuple-element.96), channel_id=1, source_target_pairs={{0,48},{16,0},{32,16},{48,32},{1,49},{17,1},{33,17},{49,33},{2,50}... | collective-permute-start | bytes 208904 | tf_op jit(solution)/shard_map/ppermute | solution.py:535
  143.1 2.2 %collective-permute-done.24.refs_1_ = bf16[272,128]{1,0:T(8,128)(2,1)S(1)} collective-permute-done((bf16[272,128]{1,0:T(8,128)(2,1)S(1)}, bf16[272,128]{1,0:T(8,128)(2,1)S(1)}, u32[]{:S(2)}, u32[]{:S(2)}) %collective-permute-start.24) | collective-permute-done | bytes 69664 | tf_op jit(solution)/shard_map/ppermute | solution.py:535
  146.1 1.3 shard_map.255
  (54 shorter events, 10.2 us)
Async XLA Ops:
  5.1 9.3 %collective-permute-start = (bf16[272,128]{1,0:T(8,128)(2,1)}, bf16[272,128]{1,0:T(8,128)(2,1)S(1)}, u32[]{:S(2)}, u32[]{:S(2)}) collective-permute-start(bf16[272,128]{1,0:T(8,128)(2,1)} %get-tuple-element.59), channel_id=1, source_target_pairs={{0,16},{16,32},{32,48},{48,0},{1,17},{17,33},{33,49},{49,1},{2,18}... | collective-permute-start | bytes 208904 | tf_op jit(solution)/shard_map/ppermute | solution.py:535
  7.1 7.4 %collective-permute-start.1 = (bf16[272,128]{1,0:T(8,128)(2,1)}, bf16[272,128]{1,0:T(8,128)(2,1)S(1)}, u32[]{:S(2)}, u32[]{:S(2)}) collective-permute-start(bf16[272,128]{1,0:T(8,128)(2,1)} %get-tuple-element.60), channel_id=1, source_target_pairs={{0,32},{16,48},{32,0},{48,16},{1,33},{17,49},{33,1},{49,17},{2,34}... | collective-permute-start | bytes 208904 | tf_op jit(solution)/shard_map/ppermute | solution.py:535
  10.7 4.5 %collective-permute-start.2 = (bf16[272,128]{1,0:T(8,128)(2,1)}, bf16[272,128]{1,0:T(8,128)(2,1)S(1)}, u32[]{:S(2)}, u32[]{:S(2)}) collective-permute-start(bf16[272,128]{1,0:T(8,128)(2,1)} %get-tuple-element.61), channel_id=1, source_target_pairs={{0,48},{16,0},{32,16},{48,32},{1,49},{17,1},{33,17},{49,33},{2,50}... | collective-permute-start | bytes 208904 | tf_op jit(solution)/shard_map/ppermute | solution.py:535
  11.7 34.1 %copy-start = (f32[96,128]{1,0:T(8,128)S(1)}, f32[96,128]{1,0:T(8,128)}, u32[]{:S(2)}) copy-start(f32[96,128]{1,0:T(8,128)} %constant.24.clone.t1.refs_13_) | copy-start | bytes 147460
  11.7 34.1 %copy-start.1 = (f32[96,128]{1,0:T(8,128)S(1)}, f32[96,128]{1,0:T(8,128)}, u32[]{:S(2)}) copy-start(f32[96,128]{1,0:T(8,128)} %constant.23.clone.t0.refs_12_) | copy-start | bytes 147460
  11.7 34.1 %copy-start.2 = (f32[64,128]{1,0:T(8,128)S(1)}, f32[64,128]{1,0:T(8,128)}, u32[]{:S(2)}) copy-start(f32[64,128]{1,0:T(8,128)} %constant.26.clone.t3.refs_15_) | copy-start | bytes 98308
  11.7 34.1 %copy-start.3 = (f32[64,128]{1,0:T(8,128)S(1)}, f32[64,128]{1,0:T(8,128)}, u32[]{:S(2)}) copy-start(f32[64,128]{1,0:T(8,128)} %constant.25.clone.t2.refs_14_) | copy-start | bytes 98308
  11.7 34.1 %copy-start.6 = (s32[5]{0:T(128)S(1)}, s32[5]{0:T(128)}, u32[]{:S(2)}) copy-start(s32[5]{0:T(128)} %stack.34.sc) | copy-start | bytes 64
  16.1 6.7 %collective-permute-start.3 = (bf16[576,128]{1,0:T(8,128)(2,1)S(1)}, bf16[576,128]{1,0:T(8,128)(2,1)S(1)}, u32[]{:S(2)}, u32[]{:S(2)}) collective-permute-start(bf16[576,128]{1,0:T(8,128)(2,1)S(1)} %bitcast.41), channel_id=1, source_target_pairs={{0,1},{1,0},{2,3},{3,2},{4,5},{5,4},{6,7},{7,6},{8,9},{9,8},{10,11... | collective-permute-start | bytes 442376 | tf_op jit(solution)/shard_map/ppermute | solution.py:535
  19.4 10.1 %collective-permute-start.5 = (bf16[1280,128]{1,0:T(8,128)(2,1)}, bf16[1280,128]{1,0:T(8,128)(2,1)S(1)}, u32[]{:S(2)}, u32[]{:S(2)}) collective-permute-start(bf16[1280,128]{1,0:T(8,128)(2,1)} %get-tuple-element.68), channel_id=1, source_target_pairs={{0,16},{16,32},{32,48},{48,0},{1,17},{17,33},{33,49},{49,1},{2,18}... | collective-permute-start | bytes 983048 | tf_op jit(solution)/shard_map/ppermute | solution.py:535
  22.9 19.3 %collective-permute-start.4 = (bf16[1664,128]{1,0:T(8,128)(2,1)S(1)}, bf16[1664,128]{1,0:T(8,128)(2,1)S(1)}, u32[]{:S(2)}, u32[]{:S(2)}) collective-permute-start(bf16[1664,128]{1,0:T(8,128)(2,1)S(1)} %pad_maximum_fusion.refs_4_), channel_id=1, source_target_pairs={{0,8},{4,12},{8,0},{12,4},{1,9},{5,13},{9,1},{13,5},{2,10},{6,14},... | collective-permute-start | bytes 1277960 | tf_op jit(solution)/shard_map/ppermute | solution.py:535
  26.0 16.8 %collective-permute-start.12 = (bf16[1664,128]{1,0:T(8,128)(2,1)S(1)}, bf16[1664,128]{1,0:T(8,128)(2,1)S(1)}, u32[]{:S(2)}, u32[]{:S(2)}) collective-permute-start(bf16[1664,128]{1,0:T(8,128)(2,1)S(1)} %pad_maximum_fusion.refs_4_), channel_id=1, source_target_pairs={{0,12},{4,0},{8,4},{12,8},{1,13},{5,1},{9,5},{13,9},{2,14},{6,2},{... | collective-permute-start | bytes 1277960 | tf_op jit(solution)/shard_map/ppermute | solution.py:535
  27.1 15.6 %collective-permute-start.9 = (bf16[1664,128]{1,0:T(8,128)(2,1)S(1)}, bf16[1664,128]{1,0:T(8,128)(2,1)S(1)}, u32[]{:S(2)}, u32[]{:S(2)}) collective-permute-start(bf16[1664,128]{1,0:T(8,128)(2,1)S(1)} %pad_maximum_fusion.refs_4_), channel_id=1, source_target_pairs={{0,4},{4,8},{8,12},{12,0},{1,5},{5,9},{9,13},{13,1},{2,6},{6,10},{... | collective-permute-start | bytes 1277960 | tf_op jit(solution)/shard_map/ppermute | solution.py:535
  28.0 8.6 %collective-permute-start.6 = (bf16[1280,128]{1,0:T(8,128)(2,1)S(1)}, bf16[1280,128]{1,0:T(8,128)(2,1)S(1)}, u32[]{:S(2)}, u32[]{:S(2)}) collective-permute-start(bf16[1280,128]{1,0:T(8,128)(2,1)S(1)} %copy-done.8), channel_id=1, source_target_pairs={{0,32},{16,48},{32,0},{48,16},{1,33},{17,49},{33,1},{49,17},{2,34}... | collective-permute-start | bytes 983048 | tf_op jit(solution)/shard_map/ppermute | solution.py:535
  29.6 12.7 %collective-permute-start.7 = (bf16[1280,128]{1,0:T(8,128)(2,1)S(1)}, bf16[1280,128]{1,0:T(8,128)(2,1)S(1)}, u32[]{:S(2)}, u32[]{:S(2)}) collective-permute-start(bf16[1280,128]{1,0:T(8,128)(2,1)S(1)} %copy-done.7), channel_id=1, source_target_pairs={{0,48},{16,0},{32,16},{48,32},{1,49},{17,1},{33,17},{49,33},{2,50}... | collective-permute-start | bytes 983048 | tf_op jit(solution)/shard_map/ppermute | solution.py:535
  36.6 6.7 %collective-permute-start.8 = (bf16[1664,128]{1,0:T(8,128)(2,1)S(1)}, bf16[1664,128]{1,0:T(8,128)(2,1)S(1)}, u32[]{:S(2)}, u32[]{:S(2)}) collective-permute-start(bf16[1664,128]{1,0:T(8,128)(2,1)S(1)} %pad_maximum_fusion.refs_4_), channel_id=1, source_target_pairs={{0,2},{2,0},{1,3},{3,1},{4,6},{6,4},{5,7},{7,5},{8,10},{10,8},{9,1... | collective-permute-start | bytes 1277960 | tf_op jit(solution)/shard_map/ppermute | solution.py:535
  42.8 1.8 %collective-permute-start.13 = (bf16[1664,128]{1,0:T(8,128)(2,1)S(1)}, bf16[1664,128]{1,0:T(8,128)(2,1)S(1)}, u32[]{:S(2)}, u32[]{:S(2)}) collective-permute-start(bf16[1664,128]{1,0:T(8,128)(2,1)S(1)} %collective-permute-done.12.refs_10_), channel_id=1, source_target_pairs={{0,2},{2,0},{1,3},{3,1},{4,6},{6,4},{5,7},{7,5},{8,10},{10,8},{9,1... | collective-permute-start | bytes 1277960 | tf_op jit(solution)/shard_map/ppermute | solution.py:535
  42.8 2.4 %collective-permute-start.10 = (bf16[1664,128]{1,0:T(8,128)(2,1)S(1)}, bf16[1664,128]{1,0:T(8,128)(2,1)S(1)}, u32[]{:S(2)}, u32[]{:S(2)}) collective-permute-start(bf16[1664,128]{1,0:T(8,128)(2,1)S(1)} %collective-permute-done.9.refs_6_), channel_id=1, source_target_pairs={{0,2},{2,0},{1,3},{3,1},{4,6},{6,4},{5,7},{7,5},{8,10},{10,8},{9,1... | collective-permute-start | bytes 1277960 | tf_op jit(solution)/shard_map/ppermute | solution.py:535
  43.3 2.5 %collective-permute-start.11 = (bf16[1664,128]{1,0:T(8,128)(2,1)S(1)}, bf16[1664,128]{1,0:T(8,128)(2,1)S(1)}, u32[]{:S(2)}, u32[]{:S(2)}) collective-permute-start(bf16[1664,128]{1,0:T(8,128)(2,1)S(1)} %collective-permute-done.4.refs_8_), channel_id=1, source_target_pairs={{0,2},{2,0},{1,3},{3,1},{4,6},{6,4},{5,7},{7,5},{8,10},{10,8},{9,1... | collective-permute-start | bytes 1277960 | tf_op jit(solution)/shard_map/ppermute | solution.py:535
  95.3 3.5 %collective-permute-start.17 = (bf16[6160,128]{1,0:T(8,128)(2,1)S(1)}, bf16[6160,128]{1,0:T(8,128)(2,1)S(1)}, u32[]{:S(2)}, u32[]{:S(2)}) collective-permute-start(bf16[6160,128]{1,0:T(8,128)(2,1)S(1)} %get-tuple-element.84), channel_id=1, source_target_pairs={{0,2},{2,0},{1,3},{3,1},{4,6},{6,4},{5,7},{7,5},{8,10},{10,8},{9,1... | collective-permute-start | bytes 4730888 | tf_op jit(solution)/shard_map/ppermute | solution.py:535
  95.5 15.6 %collective-permute-start.14 = (bf16[1280,128]{1,0:T(8,128)(2,1)S(1)}, bf16[1280,128]{1,0:T(8,128)(2,1)S(1)}, u32[]{:S(2)}, u32[]{:S(2)}) collective-permute-start(bf16[1280,128]{1,0:T(8,128)(2,1)S(1)} %get-tuple-element.77), channel_id=1, source_target_pairs={{0,48},{16,0},{32,16},{48,32},{1,49},{17,1},{33,17},{49,33},{2,50}... | collective-permute-start | bytes 983048 | tf_op jit(solution)/shard_map/ppermute | solution.py:535
  99.1 29.8 %collective-permute-start.18 = (bf16[1552,128]{1,0:T(8,128)(2,1)S(1)}, bf16[1552,128]{1,0:T(8,128)(2,1)S(1)}, u32[]{:S(2)}, u32[]{:S(2)}) collective-permute-start(bf16[1552,128]{1,0:T(8,128)(2,1)S(1)} %get-tuple-element.86), channel_id=1, source_target_pairs={{0,4},{4,8},{8,12},{12,0},{1,5},{5,9},{9,13},{13,1},{2,6},{6,10},{... | collective-permute-start | bytes 1191944 | tf_op jit(solution)/shard_map/ppermute | solution.py:535
  100.6 28.3 %collective-permute-start.19 = (bf16[1552,128]{1,0:T(8,128)(2,1)S(1)}, bf16[1552,128]{1,0:T(8,128)(2,1)S(1)}, u32[]{:S(2)}, u32[]{:S(2)}) collective-permute-start(bf16[1552,128]{1,0:T(8,128)(2,1)S(1)} %get-tuple-element.87), channel_id=1, source_target_pairs={{0,8},{4,12},{8,0},{12,4},{1,9},{5,13},{9,1},{13,5},{2,10},{6,14},... | collective-permute-start | bytes 1191944 | tf_op jit(solution)/shard_map/ppermute | solution.py:535
  107.1 21.9 %collective-permute-start.20 = (bf16[1552,128]{1,0:T(8,128)(2,1)S(1)}, bf16[1552,128]{1,0:T(8,128)(2,1)S(1)}, u32[]{:S(2)}, u32[]{:S(2)}) collective-permute-start(bf16[1552,128]{1,0:T(8,128)(2,1)S(1)} %get-tuple-element.88), channel_id=1, source_target_pairs={{0,12},{4,0},{8,4},{12,8},{1,13},{5,1},{9,5},{13,9},{2,14},{6,2},{... | collective-permute-start | bytes 1191944 | tf_op jit(solution)/shard_map/ppermute | solution.py:535
  109.6 12.2 %collective-permute-start.15 = (bf16[1280,128]{1,0:T(8,128)(2,1)S(1)}, bf16[1280,128]{1,0:T(8,128)(2,1)S(1)}, u32[]{:S(2)}, u32[]{:S(2)}) collective-permute-start(bf16[1280,128]{1,0:T(8,128)(2,1)S(1)} %get-tuple-element.78), channel_id=1, source_target_pairs={{0,32},{16,48},{32,0},{48,16},{1,33},{17,49},{33,1},{49,17},{2,34}... | collective-permute-start | bytes 983048 | tf_op jit(solution)/shard_map/ppermute | solution.py:535
  111.1 16.0 %collective-permute-start.16 = (bf16[1280,128]{1,0:T(8,128)(2,1)S(1)}, bf16[1280,128]{1,0:T(8,128)(2,1)S(1)}, u32[]{:S(2)}, u32[]{:S(2)}) collective-permute-start(bf16[1280,128]{1,0:T(8,128)(2,1)S(1)} %get-tuple-element.79), channel_id=1, source_target_pairs={{0,16},{16,32},{32,48},{48,0},{1,17},{17,33},{33,49},{49,1},{2,18}... | collective-permute-start | bytes 983048 | tf_op jit(solution)/shard_map/ppermute | solution.py:535
  130.1 8.1 %collective-permute-start.21 = (bf16[528,128]{1,0:T(8,128)(2,1)S(1)}, bf16[528,128]{1,0:T(8,128)(2,1)S(1)}, u32[]{:S(2)}, u32[]{:S(2)}) collective-permute-start(bf16[528,128]{1,0:T(8,128)(2,1)S(1)} %get-tuple-element.91), channel_id=1, source_target_pairs={{0,1},{1,0},{2,3},{3,2},{4,5},{5,4},{6,7},{7,6},{8,9},{9,8},{10,11... | collective-permute-start | bytes 405512 | tf_op jit(solution)/shard_map/ppermute | solution.py:535
  133.4 4.8 %collective-permute-start.23 = (f32[8,128]{1,0:T(8,128)S(1)}, f32[8,128]{1,0:T(8,128)S(1)}, u32[]{:S(2)}, u32[]{:S(2)}) collective-permute-start(f32[8,128]{1,0:T(8,128)S(1)} %get-tuple-element.92.b0), channel_id=1, source_target_pairs={{0,65},{1,64},{64,1},{65,0},{2,67},{3,66},{66,3},{67,2},{4,69},{5,... | collective-permute-start | bytes 12296 | tf_op jit(solution)/shard_map/ppermute | solution.py:604
  133.4 4.8 %collective-permute-start.22 = (f32[8,128]{1,0:T(8,128)S(1)}, f32[8,128]{1,0:T(8,128)S(1)}, u32[]{:S(2)}, u32[]{:S(2)}) collective-permute-start(f32[8,128]{1,0:T(8,128)S(1)} %get-tuple-element.92.b0), channel_id=1, source_target_pairs={{0,64},{64,0},{1,65},{65,1},{2,66},{66,2},{3,67},{67,3},{4,68},{68... | collective-permute-start | bytes 12296 | tf_op jit(solution)/shard_map/ppermute | solution.py:535
  138.9 6.3 %collective-permute-start.24 = (bf16[272,128]{1,0:T(8,128)(2,1)S(1)}, bf16[272,128]{1,0:T(8,128)(2,1)S(1)}, u32[]{:S(2)}, u32[]{:S(2)}) collective-permute-start(bf16[272,128]{1,0:T(8,128)(2,1)S(1)} %get-tuple-element.94), channel_id=1, source_target_pairs={{0,16},{16,32},{32,48},{48,0},{1,17},{17,33},{33,49},{49,1},{2,18}... | collective-permute-start | bytes 208904 | tf_op jit(solution)/shard_map/ppermute | solution.py:535
  139.0 6.3 %collective-permute-start.25 = (bf16[272,128]{1,0:T(8,128)(2,1)S(1)}, bf16[272,128]{1,0:T(8,128)(2,1)S(1)}, u32[]{:S(2)}, u32[]{:S(2)}) collective-permute-start(bf16[272,128]{1,0:T(8,128)(2,1)S(1)} %get-tuple-element.95), channel_id=1, source_target_pairs={{0,32},{16,48},{32,0},{48,16},{1,33},{17,49},{33,1},{49,17},{2,34}... | collective-permute-start | bytes 208904 | tf_op jit(solution)/shard_map/ppermute | solution.py:535
  141.1 5.1 %collective-permute-start.26 = (bf16[272,128]{1,0:T(8,128)(2,1)S(1)}, bf16[272,128]{1,0:T(8,128)(2,1)S(1)}, u32[]{:S(2)}, u32[]{:S(2)}) collective-permute-start(bf16[272,128]{1,0:T(8,128)(2,1)S(1)} %get-tuple-element.96), channel_id=1, source_target_pairs={{0,48},{16,0},{32,16},{48,32},{1,49},{17,1},{33,17},{49,33},{2,50}... | collective-permute-start | bytes 208904 | tf_op jit(solution)/shard_map/ppermute | solution.py:535
  (4 other events, 61.1 us)
